TPU v7x, 512 devices: a whole 4x4x16 slice. The times are simulated.
512 devices in a mesh: seq: 128 (over z_lo, y, x), ch: 4 (over z_hi, core).
Axes of the slice: x: 4, y: 4, z: 16 (z_hi: 2, z_lo: 8; z = z_hi * 8 + z_lo), core: 2. Of those that a mesh axis runs over, the one named last changes fastest.
Arguments:
- queries: bfloat16 [512, 16384], P('ch', 'seq'), may hold values from -6 to 6
- key_inputs: bfloat16 [512, 16384], P('ch', 'seq'), may hold values from -6 to 6
- value_inputs: bfloat16 [512, 16384], P('ch', 'seq'), may hold values from -6 to 6
- skip_gain: float32 [512], P('ch'), may hold values from -4 to 4
- residue: float32 [32, 16], P('ch'), may hold values from -4 to 4
- timescale: float32 [32, 16], P('ch'), may hold values from 20 to 32768
- cotangent: bfloat16 [512, 16384], P('ch', 'seq'), may hold values from -6 to 6
Outputs:
- output: bfloat16 [512, 16384], P('ch', 'seq')
- grad_queries: bfloat16 [512, 16384], P('ch', 'seq')
- grad_keys: bfloat16 [512, 16384], P('ch', 'seq')
- grad_values: bfloat16 [512, 16384], P('ch', 'seq')
- grad_skip: float32 [512], P('ch')
- grad_residue: float32 [32, 16], replicated
- grad_timescale: float32 [32, 16], replicated
All inputs are finite; a program needn't handle non-finite values.
Results may differ from a plain program's by a relative error of at most 0.0023.
Values sent between devices are 32-bit elements; how exact they have to be, the bound alone decides.
No kernel may reach another device: no remote copies, remote signals or barrier semaphores. Data moves between devices by JAX's collectives and lax.ppermute only.
A program may use at most 64 MiB of HBM per device.

v0:
```python
from functools import partial
import math

import jax
import jax.numpy as jnp
from jax import lax
from jax.sharding import PartitionSpec as P

HIGHEST = lax.Precision.HIGHEST


def partner_2(x, axis, bit):
    return lax.ppermute(x, axis, [(i, i ^ 1 << bit) for i in range(lax.axis_size(axis))])


def complex_mul(left, right):
    return jnp.stack(
        [left[0] * right[0] - left[1] * right[1], left[0] * right[1] + left[1] * right[0]]
    )


def conjugate(value):
    return jnp.stack([value[0], -value[1]])


def rotation(phase_angle):
    return jnp.stack([jnp.cos(phase_angle), jnp.sin(phase_angle)])


def filter_rows(residue, timescale, positions):
    decay_rate = 1.0 / timescale
    amplitude = residue * jnp.sqrt(2.0 * decay_rate) / math.sqrt(residue.shape[-1])
    return jnp.sum(
        amplitude[:, :, None] * jnp.exp(-positions[None, None, :] * decay_rate[:, :, None]), axis=1
    )


def local_dft(signal, direction):
    length = signal.shape[-1]
    position = jnp.arange(length, dtype=jnp.int32)
    phase_index = position[:, None] * position[None, :] % length
    turn_table = rotation(phase_index.astype(jnp.float32) * (direction * 2.0 * math.pi / length))
    matmul_hi = partial(jnp.dot, precision=HIGHEST, preferred_element_type=jnp.float32)
    real_part = matmul_hi(signal[0], turn_table[0]) - matmul_hi(signal[1], turn_table[1])
    imag_part = matmul_hi(signal[0], turn_table[1]) + matmul_hi(signal[1], turn_table[0])
    return jnp.stack([real_part, imag_part])


def section_count():
    return lax.axis_size("seq").bit_length() - 1


def butterfly_section(signal, section_bit, backward_step):
    length = signal.shape[-1]
    device = lax.axis_index("seq")
    partner = partner_2(signal, "seq", section_bit)
    upper_half = jnp.right_shift(device, section_bit) % 2
    within = device % 2**section_bit
    pair_span = length * 2**section_bit
    position = (within * length + jnp.arange(length, dtype=jnp.int32)).astype(jnp.float32)
    twiddle = rotation(position * (-math.pi / pair_span))[:, None, :]
    if backward_step:
        back_turn = conjugate(twiddle)
        lower_out = 0.5 * (signal + complex_mul(partner, back_turn))
        upper_out = 0.5 * (partner - complex_mul(signal, back_turn))
    else:
        lower_out = signal + partner
        upper_out = complex_mul(partner - signal, twiddle)
    return jnp.where(upper_half == 1, upper_out, lower_out)


def butterfly_forward(signal):
    for section_bit in reversed(range(section_count())):
        signal = butterfly_section(signal, section_bit, False)
    return local_dft(signal, -1.0)


def butterfly_inverse(spectrum):
    signal = local_dft(spectrum, 1.0) / spectrum.shape[-1]
    for section_bit in range(section_count()):
        signal = butterfly_section(signal, section_bit, True)
    return signal


def spectral_path(
    product, grad_mixed, residue, timescale, positions, full_length, to_freq, to_time
):
    channel_count, length = product.shape
    group_count = residue.shape[0]
    members = channel_count // group_count
    half_turn = rotation(positions * (-math.pi / full_length))[:, None, :]

    def split_halves(signal_rows):
        real_rows = jnp.stack([signal_rows, jnp.zeros_like(signal_rows)])
        return jnp.concatenate([real_rows, complex_mul(real_rows, half_turn)], axis=1)

    def combine(time_rows, count):
        even_part = time_rows[:, :count]
        odd_part = time_rows[:, count:]
        return 0.5 * (even_part[0] + complex_mul(odd_part, conjugate(half_turn))[0])

    def group_mul(signal, kernel_spec):
        grouped = signal.reshape(2, group_count, members, length)
        return complex_mul(grouped, kernel_spec[:, :, None, :]).reshape(2, channel_count, length)

    def group_sum(signal):
        return jnp.sum(signal.reshape(2, group_count, members, length), axis=2)

    kernel = filter_rows(residue, timescale, positions)
    row_width = channel_count + group_count
    spectra = to_freq(split_halves(jnp.concatenate([product, kernel], axis=0)))
    even_prod = spectra[:, :channel_count]
    even_kern = spectra[:, channel_count:row_width]
    odd_prod = spectra[:, row_width : row_width + channel_count]
    odd_kern = spectra[:, row_width + channel_count :]
    conv_spec = jnp.concatenate(
        [group_mul(even_prod, even_kern), group_mul(odd_prod, odd_kern)], axis=1
    )
    convolved = combine(to_time(conv_spec), channel_count)
    grad_spec = to_freq(split_halves(grad_mixed))
    even_grad = grad_spec[:, :channel_count]
    odd_grad = grad_spec[:, channel_count:]
    back_spec = jnp.concatenate(
        [
            group_mul(even_grad, conjugate(even_kern)),
            group_sum(complex_mul(conjugate(even_prod), even_grad)),
            group_mul(odd_grad, conjugate(odd_kern)),
            group_sum(complex_mul(conjugate(odd_prod), odd_grad)),
        ],
        axis=1,
    )
    back_time = combine(to_time(back_spec), row_width)
    grad_kernel = back_time[channel_count:]
    _, pullback = jax.vjp(
        lambda res_arg, time_arg: filter_rows(res_arg, time_arg, positions), residue, timescale
    )
    part_residue, part_time = pullback(grad_kernel)
    return (convolved, back_time[:channel_count], part_residue, part_time * timescale)


def per_device(queries, key_inputs, value_inputs, skip_gain, residue, timescale, cotangent):
    channel_count, length = queries.shape
    group_count, order = residue.shape
    members = channel_count // group_count
    device = lax.axis_index("seq")
    full_length = length * lax.axis_size("seq")
    positions = (device * length + jnp.arange(length, dtype=jnp.int32)).astype(jnp.float32)
    query_float = queries.astype(jnp.float32)
    key_float = key_inputs.astype(jnp.float32)
    value_float = value_inputs.astype(jnp.float32)
    cot_float = cotangent.astype(jnp.float32)
    product = query_float * key_float
    grad_mixed = cot_float * value_float
    convolved, back_conv, residue_terms, time_terms = spectral_path(
        product,
        grad_mixed,
        residue,
        timescale,
        positions,
        full_length,
        butterfly_forward,
        butterfly_inverse,
    )
    mixed_rows = convolved + skip_gain[:, None] * product
    output = (value_float * mixed_rows).astype(jnp.bfloat16)
    grad_values = (cot_float * mixed_rows).astype(jnp.bfloat16)
    grad_product = back_conv + skip_gain[:, None] * grad_mixed
    grad_queries = (grad_product * key_float).astype(jnp.bfloat16)
    grad_keys = (grad_product * query_float).astype(jnp.bfloat16)
    skip_terms = jnp.sum(grad_mixed * product, axis=1)
    sum_residue, sum_time, sum_skip = lax.psum((residue_terms, time_terms, skip_terms), "seq")
    sum_residue, sum_time = (
        lax.all_gather(sum_residue, "ch", axis=0, tiled=True),
        lax.all_gather(sum_time, "ch", axis=0, tiled=True),
    )
    grad_scale = 1.0 / math.sqrt(full_length * members)
    grad_skip = sum_skip / math.sqrt(full_length)
    return (
        output,
        grad_queries,
        grad_keys,
        grad_values,
        grad_skip,
        sum_residue * grad_scale,
        sum_time * grad_scale,
    )


def solution(mesh):
    placed = (
        P("ch", "seq"),
        P("ch", "seq"),
        P("ch", "seq"),
        P("ch"),
        P("ch", None),
        P("ch", None),
        P("ch", "seq"),
    )
    return jax.shard_map(
        per_device,
        mesh=mesh,
        in_specs=placed,
        out_specs=(
            P("ch", "seq"),
            P("ch", "seq"),
            P("ch", "seq"),
            P("ch", "seq"),
            P("ch"),
            P(),
            P(),
        ),
        check_vma=False,
    )
```

profile of v0, /device:TPU:1, one launch (start us, length us, event | category | flops | bytes accessed | tf_op | source)
XLA Modules:
  0.0 824.4 jit_solution(3835874085248140666)
XLA Ops:
  1.7 9.6 %collective-permute-start.14 = (f32[2,256,128]{2,1,0:T(8,128)S(1)}, f32[2,256,128]{2,1,0:T(8,128)S(1)}, u32[]{:S(2)}, u32[]{:S(2)}) collective-permute-start(f32[2,256,128]{2,1,0:T(8,128)S(1)} %select_maximum_fusion.1), channel_id=1, source_target_pairs={{0,256},{4,260},{8,264},{12,268},{16,272},{20,276},{24,280},{28,28... | collective-permute-start | bytes 786440 | tf_op jit(solution)/shard_map/ppermute | solution.py:13
  14.0 37.4 %collective-permute-done.14 = f32[2,256,128]{2,1,0:T(8,128)S(1)} collective-permute-done((f32[2,256,128]{2,1,0:T(8,128)S(1)}, f32[2,256,128]{2,1,0:T(8,128)S(1)}, u32[]{:S(2)}, u32[]{:S(2)}) %collective-permute-start.14) | collective-permute-done | bytes 262176 | tf_op jit(solution)/shard_map/ppermute | solution.py:13
  53.5 3.9 collective-permute-done
  59.4 16.6 %collective-permute-done.15 = f32[2,256,128]{2,1,0:T(8,128)S(1)} collective-permute-done((f32[2,256,128]{2,1,0:T(8,128)S(1)}, f32[2,256,128]{2,1,0:T(8,128)S(1)}, u32[]{:S(2)}, u32[]{:S(2)}) %collective-permute-start.15) | collective-permute-done | bytes 262176 | tf_op jit(solution)/shard_map/ppermute | solution.py:13
  78.1 3.8 collective-permute-done.1
  87.7 4.8 collective-permute-start.17
  93.6 4.8 collective-permute-start.3
  110.6 4.7 collective-permute-start.19
  116.6 4.7 collective-permute-start.5
  121.5 5.0 collective-permute-done.5
  138.4 3.7 collective-permute-start.7
  142.3 3.5 collective-permute-done.7
  150.4 3.5 collective-permute-start.21
  154.0 4.4 collective-permute-start.8
  158.6 4.3 collective-permute-start.22
  180.0 4.5 collective-permute-done.10
  186.5 3.7 collective-permute-done.24
  194.3 3.6 collective-permute-done.25
  202.2 9.5 %collective-permute-start.13 = (f32[2,256,128]{2,1,0:T(8,128)S(1)}, f32[2,256,128]{2,1,0:T(8,128)S(1)}, u32[]{:S(2)}, u32[]{:S(2)}) collective-permute-start(f32[2,256,128]{2,1,0:T(8,128)S(1)} %fusion.45), channel_id=1, source_target_pairs={{0,256},{4,260},{8,264},{12,268},{16,272},{20,276},{24,280},{28,28... | collective-permute-start | bytes 786440 | tf_op jit(solution)/shard_map/ppermute | solution.py:13
  211.8 6.8 collective-permute-start.27
  218.8 14.8 %collective-permute-done.27 = f32[2,272,128]{2,1,0:T(8,128)S(1)} collective-permute-done((f32[2,272,128]{2,1,0:T(8,128)S(1)}, f32[2,272,128]{2,1,0:T(8,128)S(1)}, u32[]{:S(2)}, u32[]{:S(2)}) %collective-permute-start.27) | collective-permute-done | bytes 278560 | tf_op jit(solution)/shard_map/ppermute | solution.py:13
  235.2 476.9 %all-reduce.2 = (f32[128]{0:T(128)S(1)}, f32[8,16]{1,0:T(8,128)S(1)}, f32[8,16]{1,0:T(8,128)S(1)}) all-reduce(f32[128]{0:T(128)S(1)} %get-tuple-element.136, f32[8,16]{1,0:T(8,128)S(1)} %get-tuple-element.147, f32[8,16]{1,0:T(8,128)S(1)} %get-tuple-element.146), channel_id=1, replica_groups=mesh['seq'=128,'ch'=4] {'seq'}, use_global_device_ids=true, to_apply=%region_4.5 | all-reduce | flops 384 | bytes 3072 | tf_op jit(solution)/shard_map/psum | solution.py:171
  712.6 95.9 %all_gather.6 = f32[32,16]{1,0:T(8,128)S(1)} all-gather(f32[8,16]{1,0:T(8,128)S(1)} %get-tuple-element.24), channel_id=1, replica_groups=mesh['seq'=128,'ch'=4] {'ch'}, dimensions={0}, use_global_device_ids=true | all-gather | bytes 2560 | tf_op jit(solution)/shard_map/all_gather | solution.py:173
  809.2 13.9 %all_gather.7 = f32[32,16]{1,0:T(8,128)S(1)} all-gather(f32[8,16]{1,0:T(8,128)S(1)} %get-tuple-element.25), channel_id=1, replica_groups=mesh['seq'=128,'ch'=4] {'ch'}, dimensions={0}, use_global_device_ids=true | all-gather | bytes 2560 | tf_op jit(solution)/shard_map/all_gather | solution.py:174
  (188 shorter events, 78.4 us)
Async XLA Ops:
  1.7 49.7 %collective-permute-start.14 = (f32[2,256,128]{2,1,0:T(8,128)S(1)}, f32[2,256,128]{2,1,0:T(8,128)S(1)}, u32[]{:S(2)}, u32[]{:S(2)}) collective-permute-start(f32[2,256,128]{2,1,0:T(8,128)S(1)} %select_maximum_fusion.1), channel_id=1, source_target_pairs={{0,256},{4,260},{8,264},{12,268},{16,272},{20,276},{24,280},{28,28... | collective-permute-start | bytes 786440 | tf_op jit(solution)/shard_map/ppermute | solution.py:13
  11.6 45.8 %collective-permute-start = (f32[2,272,128]{2,1,0:T(8,128)S(1)}, f32[2,272,128]{2,1,0:T(8,128)S(1)}, u32[]{:S(2)}, u32[]{:S(2)}) collective-permute-start(f32[2,272,128]{2,1,0:T(8,128)S(1)} %select_maximum_fusion), channel_id=1, source_target_pairs={{0,256},{4,260},{8,264},{12,268},{16,272},{20,276},{24,280},{28,28... | collective-permute-start | bytes 835592 | tf_op jit(solution)/shard_map/ppermute | solution.py:13
  51.5 24.5 %collective-permute-start.15 = (f32[2,256,128]{2,1,0:T(8,128)S(1)}, f32[2,256,128]{2,1,0:T(8,128)S(1)}, u32[]{:S(2)}, u32[]{:S(2)}) collective-permute-start(f32[2,256,128]{2,1,0:T(8,128)S(1)} %maximum_select_fusion.7), channel_id=1, source_target_pairs={{0,128},{4,132},{8,136},{12,140},{16,144},{20,148},{24,152},{28,15... | collective-permute-start | bytes 786440 | tf_op jit(solution)/shard_map/ppermute | solution.py:13
  57.5 24.5 %collective-permute-start.1 = (f32[2,272,128]{2,1,0:T(8,128)S(1)}, f32[2,272,128]{2,1,0:T(8,128)S(1)}, u32[]{:S(2)}, u32[]{:S(2)}) collective-permute-start(f32[2,272,128]{2,1,0:T(8,128)S(1)} %maximum_select_fusion), channel_id=1, source_target_pairs={{0,128},{4,132},{8,136},{12,140},{16,144},{20,148},{24,152},{28,15... | collective-permute-start | bytes 835592 | tf_op jit(solution)/shard_map/ppermute | solution.py:13
  76.2 11.4 %collective-permute-start.16 = (f32[2,256,128]{2,1,0:T(8,128)S(1)}, f32[2,256,128]{2,1,0:T(8,128)S(1)}, u32[]{:S(2)}, u32[]{:S(2)}) collective-permute-start(f32[2,256,128]{2,1,0:T(8,128)S(1)} %maximum_select_fusion.8), channel_id=1, source_target_pairs={{0,64},{4,68},{8,72},{12,76},{16,80},{20,84},{24,88},{28,92},{32,9... | collective-permute-start | bytes 786440 | tf_op jit(solution)/shard_map/ppermute | solution.py:13
  82.2 11.3 %collective-permute-start.2 = (f32[2,272,128]{2,1,0:T(8,128)S(1)}, f32[2,272,128]{2,1,0:T(8,128)S(1)}, u32[]{:S(2)}, u32[]{:S(2)}) collective-permute-start(f32[2,272,128]{2,1,0:T(8,128)S(1)} %maximum_select_fusion.1), channel_id=1, source_target_pairs={{0,64},{4,68},{8,72},{12,76},{16,80},{20,84},{24,88},{28,92},{32,9... | collective-permute-start | bytes 835592 | tf_op jit(solution)/shard_map/ppermute | solution.py:13
  87.7 10.7 %collective-permute-start.17 = (f32[2,256,128]{2,1,0:T(8,128)S(1)}, f32[2,256,128]{2,1,0:T(8,128)S(1)}, u32[]{:S(2)}, u32[]{:S(2)}) collective-permute-start(f32[2,256,128]{2,1,0:T(8,128)S(1)} %maximum_select_fusion.9), channel_id=1, source_target_pairs={{0,32},{4,36},{8,40},{12,44},{16,48},{20,52},{24,56},{28,60},{32,0... | collective-permute-start | bytes 786440 | tf_op jit(solution)/shard_map/ppermute | solution.py:13
  93.6 11.0 %collective-permute-start.3 = (f32[2,272,128]{2,1,0:T(8,128)S(1)}, f32[2,272,128]{2,1,0:T(8,128)S(1)}, u32[]{:S(2)}, u32[]{:S(2)}) collective-permute-start(f32[2,272,128]{2,1,0:T(8,128)S(1)} %maximum_select_fusion.2), channel_id=1, source_target_pairs={{0,32},{4,36},{8,40},{12,44},{16,48},{20,52},{24,56},{28,60},{32,0... | collective-permute-start | bytes 835592 | tf_op jit(solution)/shard_map/ppermute | solution.py:13
  98.5 12.0 %collective-permute-start.18 = (f32[2,256,128]{2,1,0:T(8,128)S(1)}, f32[2,256,128]{2,1,0:T(8,128)S(1)}, u32[]{:S(2)}, u32[]{:S(2)}) collective-permute-start(f32[2,256,128]{2,1,0:T(8,128)S(1)} %maximum_select_fusion.10), channel_id=1, source_target_pairs={{0,16},{4,20},{8,24},{12,28},{16,0},{20,4},{24,8},{28,12},{32,48},... | collective-permute-start | bytes 786440 | tf_op jit(solution)/shard_map/ppermute | solution.py:13
  104.7 11.8 %collective-permute-start.4 = (f32[2,272,128]{2,1,0:T(8,128)S(1)}, f32[2,272,128]{2,1,0:T(8,128)S(1)}, u32[]{:S(2)}, u32[]{:S(2)}) collective-permute-start(f32[2,272,128]{2,1,0:T(8,128)S(1)} %maximum_select_fusion.3), channel_id=1, source_target_pairs={{0,16},{4,20},{8,24},{12,28},{16,0},{20,4},{24,8},{28,12},{32,48},... | collective-permute-start | bytes 835592 | tf_op jit(solution)/shard_map/ppermute | solution.py:13
  110.6 10.8 %collective-permute-start.19 = (f32[2,256,128]{2,1,0:T(8,128)S(1)}, f32[2,256,128]{2,1,0:T(8,128)S(1)}, u32[]{:S(2)}, u32[]{:S(2)}) collective-permute-start(f32[2,256,128]{2,1,0:T(8,128)S(1)} %maximum_select_fusion.11), channel_id=1, source_target_pairs={{0,8},{4,12},{8,0},{12,4},{16,24},{20,28},{24,16},{28,20},{32,40},... | collective-permute-start | bytes 786440 | tf_op jit(solution)/shard_map/ppermute | solution.py:13
  116.6 9.9 %collective-permute-start.5 = (f32[2,272,128]{2,1,0:T(8,128)S(1)}, f32[2,272,128]{2,1,0:T(8,128)S(1)}, u32[]{:S(2)}, u32[]{:S(2)}) collective-permute-start(f32[2,272,128]{2,1,0:T(8,128)S(1)} %maximum_select_fusion.4), channel_id=1, source_target_pairs={{0,8},{4,12},{8,0},{12,4},{16,24},{20,28},{24,16},{28,20},{32,40},... | collective-permute-start | bytes 835592 | tf_op jit(solution)/shard_map/ppermute | solution.py:13
  130.1 12.2 %collective-permute-start.20 = (f32[2,256,128]{2,1,0:T(8,128)S(1)}, f32[2,256,128]{2,1,0:T(8,128)S(1)}, u32[]{:S(2)}, u32[]{:S(2)}) collective-permute-start(f32[2,256,128]{2,1,0:T(8,128)S(1)} %maximum_select_fusion.12), channel_id=1, source_target_pairs={{0,4},{4,0},{8,12},{12,8},{16,20},{20,16},{24,28},{28,24},{32,36},... | collective-permute-start | bytes 786440 | tf_op jit(solution)/shard_map/ppermute | solution.py:13
  150.4 8.0 collective-permute-start.21
  154.0 9.1 %collective-permute-start.8 = (f32[2,256,128]{2,1,0:T(8,128)S(1)}, f32[2,256,128]{2,1,0:T(8,128)S(1)}, u32[]{:S(2)}, u32[]{:S(2)}) collective-permute-start(f32[2,256,128]{2,1,0:T(8,128)S(1)} %fusion.30), channel_id=1, source_target_pairs={{0,8},{4,12},{8,0},{12,4},{16,24},{20,28},{24,16},{28,20},{32,40},... | collective-permute-start | bytes 786440 | tf_op jit(solution)/shard_map/ppermute | solution.py:13
  158.6 11.2 %collective-permute-start.22 = (f32[2,272,128]{2,1,0:T(8,128)S(1)}, f32[2,272,128]{2,1,0:T(8,128)S(1)}, u32[]{:S(2)}, u32[]{:S(2)}) collective-permute-start(f32[2,272,128]{2,1,0:T(8,128)S(1)} %fusion.9), channel_id=1, source_target_pairs={{0,8},{4,12},{8,0},{12,4},{16,24},{20,28},{24,16},{28,20},{32,40},... | collective-permute-start | bytes 835592 | tf_op jit(solution)/shard_map/ppermute | solution.py:13
  163.3 9.6 %collective-permute-start.9 = (f32[2,256,128]{2,1,0:T(8,128)S(1)}, f32[2,256,128]{2,1,0:T(8,128)S(1)}, u32[]{:S(2)}, u32[]{:S(2)}) collective-permute-start(f32[2,256,128]{2,1,0:T(8,128)S(1)} %fusion.33), channel_id=1, source_target_pairs={{0,16},{4,20},{8,24},{12,28},{16,0},{20,4},{24,8},{28,12},{32,48},... | collective-permute-start | bytes 786440 | tf_op jit(solution)/shard_map/ppermute | solution.py:13
  173.1 11.4 %collective-permute-start.10 = (f32[2,256,128]{2,1,0:T(8,128)S(1)}, f32[2,256,128]{2,1,0:T(8,128)S(1)}, u32[]{:S(2)}, u32[]{:S(2)}) collective-permute-start(f32[2,256,128]{2,1,0:T(8,128)S(1)} %fusion.36), channel_id=1, source_target_pairs={{0,32},{4,36},{8,40},{12,44},{16,48},{20,52},{24,56},{28,60},{32,0... | collective-permute-start | bytes 786440 | tf_op jit(solution)/shard_map/ppermute | solution.py:13
  177.7 12.5 %collective-permute-start.24 = (f32[2,272,128]{2,1,0:T(8,128)S(1)}, f32[2,272,128]{2,1,0:T(8,128)S(1)}, u32[]{:S(2)}, u32[]{:S(2)}) collective-permute-start(f32[2,272,128]{2,1,0:T(8,128)S(1)} %fusion.15), channel_id=1, source_target_pairs={{0,32},{4,36},{8,40},{12,44},{16,48},{20,52},{24,56},{28,60},{32,0... | collective-permute-start | bytes 835592 | tf_op jit(solution)/shard_map/ppermute | solution.py:13
  184.6 7.7 collective-permute-start.11
  192.4 9.6 %collective-permute-start.12 = (f32[2,256,128]{2,1,0:T(8,128)S(1)}, f32[2,256,128]{2,1,0:T(8,128)S(1)}, u32[]{:S(2)}, u32[]{:S(2)}) collective-permute-start(f32[2,256,128]{2,1,0:T(8,128)S(1)} %fusion.42), channel_id=1, source_target_pairs={{0,128},{4,132},{8,136},{12,140},{16,144},{20,148},{24,152},{28,15... | collective-permute-start | bytes 786440 | tf_op jit(solution)/shard_map/ppermute | solution.py:13
  198.1 13.6 %collective-permute-start.26 = (f32[2,272,128]{2,1,0:T(8,128)S(1)}, f32[2,272,128]{2,1,0:T(8,128)S(1)}, u32[]{:S(2)}, u32[]{:S(2)}) collective-permute-start(f32[2,272,128]{2,1,0:T(8,128)S(1)} %fusion.21), channel_id=1, source_target_pairs={{0,128},{4,132},{8,136},{12,140},{16,144},{20,148},{24,152},{28,15... | collective-permute-start | bytes 835592 | tf_op jit(solution)/shard_map/ppermute | solution.py:13
  202.2 16.4 %collective-permute-start.13 = (f32[2,256,128]{2,1,0:T(8,128)S(1)}, f32[2,256,128]{2,1,0:T(8,128)S(1)}, u32[]{:S(2)}, u32[]{:S(2)}) collective-permute-start(f32[2,256,128]{2,1,0:T(8,128)S(1)} %fusion.45), channel_id=1, source_target_pairs={{0,256},{4,260},{8,264},{12,268},{16,272},{20,276},{24,280},{28,28... | collective-permute-start | bytes 786440 | tf_op jit(solution)/shard_map/ppermute | solution.py:13
  211.8 21.7 %collective-permute-start.27 = (f32[2,272,128]{2,1,0:T(8,128)S(1)}, f32[2,272,128]{2,1,0:T(8,128)S(1)}, u32[]{:S(2)}, u32[]{:S(2)}) collective-permute-start(f32[2,272,128]{2,1,0:T(8,128)S(1)} %fusion.24), channel_id=1, source_target_pairs={{0,256},{4,260},{8,264},{12,268},{16,272},{20,276},{24,280},{28,28... | collective-permute-start | bytes 835592 | tf_op jit(solution)/shard_map/ppermute | solution.py:13
  (11 other events, 71.1 us)
where the time goes:
time: 825 us; the launch traced here: 824 us
  blocking collectives  587 us (71%)
  waiting for transfers between devices  118 us (14%)
  starting transfers between devices  99.8 us (12%)
    psum x1, blocking collectives, per_device(): lax.psum((residue_terms, time_terms, skip_terms), 'seq')  477 us
    ppermute x28, waiting for transfers between devices, partner_2(): lax.ppermute(x, axis, [(i, i ^ 1 << bit) for i in range(lax.axis_size(axi...  118 us
    ppermute x28, starting transfers between devices, partner_2(): lax.ppermute(x, axis, [(i, i ^ 1 << bit) for i in range(lax.axis_size(axi...  99.8 us
    all_gather x1, blocking collectives, per_device(): lax.all_gather(sum_residue, 'ch', axis=0, tiled=True)  95.9 us
  transfers between devices with their start and end apart: 28, of which 20 were waited for; matrix products, arithmetic and copies ran while one was open for 1% of the time, Pallas kernels for 0%

commit v1 on v0

v1 whole, which is shorter than its diff:
```python
import math

import jax
import jax.numpy as jnp
from jax import lax
from jax.experimental import pallas as pl
from jax.experimental.pallas import tpu as pltpu
from jax.sharding import Mesh, PartitionSpec as P

F32 = jnp.float32
HI = lax.Precision.HIGHEST
L = 128
CH = 128
G = 8
R = 16
M = 16
SUM_ROW = 4 * R
ROWS = SUM_ROW + 8
NP = 16
NZ = 8


def dot(a, b, ca=1, cb=0):
    return lax.dot_general(a, b, (((ca,), (cb,)), ((), ())), precision=HI, preferred_element_type=F32)


def iota(shape, axis):
    return lax.broadcasted_iota(jnp.int32, shape, axis)


def ones_where(cond):
    return jnp.where(cond, jnp.float32(1), jnp.float32(0))


def by_mode_and_channel(table):
    pick = ones_where(iota((G, CH), 1) // M == iota((G, CH), 0))
    return dot(table, pick, 0, 0)


def by_group_mode(table):
    pick = ones_where(iota((G * R, G), 0) // R == iota((G * R, G), 1))
    rows = dot(pick, table)
    rows = jnp.where(iota((G * R, R), 0) % R == iota((G * R, R), 1), rows, 0.0)
    return dot(rows, jnp.ones((R, L), F32))


def same_group():
    return iota((128, 128), 0) // M == iota((128, 128), 1) // M


def fold_states(full):
    own = jnp.where(same_group(), full, 0.0)
    return jnp.sum(own.reshape(G, R, CH), axis=0)


def spread_states(state):
    return jnp.where(same_group(), jnp.concatenate([state] * G, axis=0), 0.0)


def group_sums(h0, h1, skip_terms=None):
    pick = ones_where(iota((G, CH), 1) // M == iota((G, CH), 0))
    rows = jnp.concatenate([h0, h1, jnp.zeros((CH - 2 * R, CH), F32)], axis=0)
    return dot(pick, rows, 1, 1)


def local_kernel(q_ref, k_ref, v_ref, ct_ref, tau_ref, msg_ref):
    product = q_ref[...].astype(F32) * k_ref[...].astype(F32)
    grad_mixed = ct_ref[...].astype(F32) * v_ref[...].astype(F32)
    rate = by_group_mode(1.0 / tau_ref[...])
    lane = iota((128, 128), 1)
    row = iota((128, 128), 0)
    step = lane.astype(F32)
    decay = jnp.exp(-step * rate)
    left = jnp.float32(L) - step
    decay_end = jnp.exp(-left * rate)
    fwd = dot(jnp.concatenate([decay_end, left * decay_end], axis=0), product, 1, 1)
    bwd = dot(jnp.concatenate([decay, step * decay], axis=0), grad_mixed, 1, 1)
    flipped = dot(product, ones_where(lane + row == L - 1))
    inside = lane + row >= L - 1
    lags = []
    for g in range(G):
        c = slice(g * M, (g + 1) * M)
        outer = jnp.where(inside, dot(flipped[c], grad_mixed[c], 0, 0), 0.0)
        aligned = pltpu.roll(outer, 1, 1, stride=1, stride_axis=0)
        lags.append(jnp.sum(aligned, axis=0, keepdims=True))
    lags = jnp.concatenate(lags, axis=0)
    lags = jnp.concatenate([lags, lags * iota((G, L), 1).astype(F32)], axis=0)
    modal = dot(lags, decay, 1, 1)
    modal = jnp.where(iota((2 * G, G * R), 0) % G == iota((2 * G, G * R), 1) // R, modal, 0.0)
    sums = dot(modal[:G], ones_where(row % R == lane)) + dot(modal[G:], ones_where(row % R == lane - R))
    skip_col = jnp.sum(grad_mixed * product, axis=1, keepdims=True)
    skip_at = jnp.where(row % M == lane - 2 * R, skip_col, 0.0)
    pick = ones_where(iota((G, CH), 1) // M == iota((G, CH), 0))
    sums = sums + dot(pick, skip_at)
    message = jnp.concatenate(
        [fold_states(fwd[:128]), fold_states(bwd[:128]), fold_states(fwd[128:]), fold_states(bwd[128:]), sums], axis=0
    )
    for i in range(NP):
        msg_ref[i] = message


def conv_kernel(q_ref, k_ref, v_ref, ct_ref, tau_ref, res_ref, skip_ref, fwd_ref, bwd_ref, head_ref, tail_ref):
    product = q_ref[...].astype(F32) * k_ref[...].astype(F32)
    grad_mixed = ct_ref[...].astype(F32) * v_ref[...].astype(F32)
    inv = 1.0 / tau_ref[...]
    rate = by_group_mode(inv)
    gain = by_group_mode(res_ref[...] * jnp.sqrt(2.0 * inv) * (1.0 / math.sqrt(R)))
    lane = iota((128, 128), 1)
    row = iota((128, 128), 0)
    step = lane.astype(F32)
    head = gain * jnp.exp(-step * rate)
    head_ref[...] = head
    tail_ref[...] = gain * jnp.exp(-(jnp.float32(L) - step) * rate)
    taps = jnp.sum(head.reshape(G, R, L), axis=1)
    skip = jnp.sum(jnp.where(lane == row, skip_ref[...], 0.0), axis=1, keepdims=True)
    for g in range(G):
        c = slice(g * M, (g + 1) * M)
        table = pltpu.roll(jnp.broadcast_to(taps[g : g + 1], (L, L)), 0, 1, stride=1, stride_axis=0)
        table = jnp.where(lane >= row, table, 0.0)
        fwd_ref[c] = dot(product[c], table) + skip[c] * product[c]
        bwd_ref[c] = dot(grad_mixed[c], table, 1, 1) + skip[c] * grad_mixed[c]


def scan_states(msg_ref, count, rate, span, me):
    decay = jnp.exp(-jnp.float32(span) * rate)
    zero = jnp.zeros((R, CH), F32)
    part = lambda i, k: msg_ref[i, k * R : (k + 1) * R]
    f, f1, h0, h1, own_f = zero, zero, zero, zero, zero
    sums = jnp.zeros((G, 128), F32)
    for i in range(count):
        own_f = jnp.where(me == i, f, own_f)
        h0 = h0 + f * part(i, 1)
        h1 = h1 + f * part(i, 3) + f1 * part(i, 1)
        f1 = decay * (f1 + jnp.float32(span) * f) + part(i, 2)
        f = decay * f + part(i, 0)
        sums = sums + msg_ref[i, SUM_ROW : SUM_ROW + G]
    b, b1, own_b = zero, zero, zero
    for i in reversed(range(count)):
        own_b = jnp.where(me == i, b, own_b)
        b1 = decay * (b1 + jnp.float32(span) * b) + part(i, 3)
        b = decay * b + part(i, 1)
    return own_f, own_b, f, b, f1, b1, sums + group_sums(h0, h1)


def plane_index():
    return lax.axis_index("y") * 4 + lax.axis_index("x")


def plane_kernel(msg_ref, tau_ref, out_ref, carry_ref):
    rate = by_mode_and_channel(1.0 / tau_ref[...])
    own_f, own_b, f, b, f1, b1, sums = scan_states(msg_ref, NP, rate, L, plane_index())
    carry_ref[:R] = own_f
    carry_ref[R:] = own_b
    message = jnp.concatenate([f, b, f1, b1, sums], axis=0)
    for i in range(NZ):
        out_ref[i] = message


def final_kernel(msg_ref, tau_ref, res_ref, plane_ref, carry_ref, param_ref, skip_ref):
    inv = 1.0 / tau_ref[...]
    rate = by_mode_and_channel(inv)
    me = plane_index().astype(F32)
    own_f, own_b, _, _, _, _, sums = scan_states(msg_ref, NZ, rate, L * NP, lax.axis_index("z"))
    carry_ref[:R] = plane_ref[:R] + jnp.exp(-(L * me) * rate) * own_f
    carry_ref[R:] = plane_ref[R:] + jnp.exp(-(L * (NP - 1 - me)) * rate) * own_b
    scale = 1.0 / math.sqrt(L * NP * NZ * M)
    h0, h1 = sums[:, :R], sums[:, R : 2 * R]
    root = jnp.sqrt(2.0 * inv) * (1.0 / math.sqrt(R))
    param_ref[:, :R] = h0 * root * scale
    param_ref[:, R : 2 * R] = res_ref[...] * root * (h1 * inv - 0.5 * h0) * scale
    param_ref[:, 2 * R :] = jnp.zeros((G, 128 - 2 * R), F32)
    lane = iota((128, 128), 1)
    row = iota((128, 128), 0)
    spread = dot(sums, ones_where(row - 2 * R == lane % M) * ones_where(row >= 2 * R) * ones_where(row < 3 * R))
    spread = jnp.where(iota((G, CH), 1) // M == iota((G, CH), 0), spread, 0.0)
    skip_ref[...] = jnp.sum(spread, axis=0, keepdims=True) * (1.0 / math.sqrt(L * NP * NZ))


def output_kernel(
    q_ref, k_ref, v_ref, ct_ref, fwd_ref, bwd_ref, head_ref, tail_ref, carry_ref, out_ref, gq_ref, gk_ref, gv_ref
):
    mixed = fwd_ref[...] + dot(spread_states(carry_ref[:R]), head_ref[...], 0, 0)
    grad_product = bwd_ref[...] + dot(spread_states(carry_ref[R:]), tail_ref[...], 0, 0)
    out_ref[...] = (v_ref[...].astype(F32) * mixed).astype(jnp.bfloat16)
    gv_ref[...] = (ct_ref[...].astype(F32) * mixed).astype(jnp.bfloat16)
    gq_ref[...] = (grad_product * k_ref[...].astype(F32)).astype(jnp.bfloat16)
    gk_ref[...] = (grad_product * q_ref[...].astype(F32)).astype(jnp.bfloat16)


def shape(*dims, dtype=F32):
    return jax.ShapeDtypeStruct(dims, dtype)


def call(kernel, outs, flops, name):
    return pl.pallas_call(
        kernel,
        out_shape=outs,
        name=name,
        cost_estimate=pl.CostEstimate(flops=flops, bytes_accessed=500_000, transcendentals=0),
        compiler_params=pltpu.CompilerParams(vmem_limit_bytes=32 * 1024 * 1024),
    )


def per_device(queries, key_inputs, value_inputs, skip_gain, residue, timescale, cotangent):
    arrays = (queries, key_inputs, value_inputs, cotangent)
    message = call(local_kernel, shape(NP, ROWS, 128), 10**8, "local_states")(*arrays, timescale)
    plane_states = lax.all_to_all(message, ("y", "x"), 0, 0)
    tables = call(conv_kernel, (shape(128, 128),) * 4, 10**8, "local_conv")(
        *arrays, timescale, residue, skip_gain.reshape(1, CH)
    )
    totals, plane_carry = call(plane_kernel, (shape(NZ, ROWS, 128), shape(2 * R, CH)), 10**7, "plane_scan")(
        plane_states, timescale
    )
    z_states = lax.all_to_all(totals, "z", 0, 0)
    carry, params, grad_skip = call(
        final_kernel, (shape(2 * R, CH), shape(G, 128), shape(1, CH)), 10**7, "z_scan"
    )(z_states, timescale, residue, plane_carry)
    swap = [(0, 1), (1, 0)]
    other = lax.ppermute(params, "zh", swap)
    outs = call(output_kernel, (shape(CH, L, dtype=jnp.bfloat16),) * 4, 10**8, "outputs")(
        *arrays, *tables, carry
    )
    flip = lax.axis_index("zh") == 1
    pair = jnp.stack([jnp.where(flip, other, params), jnp.where(flip, params, other)])
    other_pair = lax.ppermute(pair, "core", swap)
    odd = lax.axis_index("core") == 1
    whole = jnp.stack([jnp.where(odd, other_pair, pair), jnp.where(odd, pair, other_pair)], axis=1)
    whole = whole.reshape(4 * G, 128)
    output, grad_queries, grad_keys, grad_values = outs
    return (
        output,
        grad_queries,
        grad_keys,
        grad_values,
        grad_skip.reshape(CH),
        whole[:, :R],
        whole[:, R : 2 * R],
    )


def solution(mesh):
    grid = Mesh(mesh.devices.reshape(NZ, 4, 4, 2, 2), ("z", "y", "x", "zh", "core"))
    seq = ("z", "y", "x")
    ch = ("zh", "core")
    return jax.shard_map(
        per_device,
        mesh=grid,
        in_specs=(P(ch, seq), P(ch, seq), P(ch, seq), P(ch), P(ch, None), P(ch, None), P(ch, seq)),
        out_specs=(P(ch, seq), P(ch, seq), P(ch, seq), P(ch, seq), P(ch), P(), P()),
        check_vma=False,
    )
```

time: 825 us -> 78.2 us (0.09)
  blocking collectives: 587 us -> 47.3 us
  waiting for transfers between devices: 118 us -> 3.13 us
  starting transfers between devices: 99.8 us -> 14.7 us
    psum x1 -> x0, blocking collectives: 477 us -> none  [per_device(): lax.psum((residue_terms, time_terms, skip_terms), 'seq')]
    ppermute x28 -> x2, waiting for transfers between devices: 118 us -> 3.13 us  [the longest x1 3.13 us: per_device(): other = lax.ppermute(params, 'zh', swap)]
    all_gather x2 -> x0, blocking collectives: 110 us -> none  [the longest x1 95.9 us: per_device(): lax.all_gather(sum_residue, 'ch', axis=0, tiled=True)]
    ppermute x28 -> x2, starting transfers between devices: 99.8 us -> 14.7 us  [the longest x1 8.06 us: per_device(): other = lax.ppermute(params, 'zh', swap)]
    all_to_all x0 -> x2, blocking collectives: none -> 47.3 us  [the longest x1 29.5 us: per_device(): z_states = lax.all_to_all(totals, 'z', 0, 0)]
  transfers between devices with their start and end apart: 28 -> 2, of which waited for: 20 -> 1; matrix products, arithmetic and copies ran while one was open for 1% -> 0% of each run, Pallas kernels for 0% -> 4%
where the time goes in v1:
time: 78.2 us; the launch traced here: 77.6 us
  blocking collectives  47.3 us (60%)
  starting transfers between devices  14.7 us (19%)
  Pallas kernels  6.6 us (8%)
  local copies, waits for them, and re-layouts  5.15 us (7%)
  waiting for transfers between devices  3.13 us (4%)
    all_to_all x1, blocking collectives, per_device(): z_states = lax.all_to_all(totals, 'z', 0, 0)  29.5 us
    all_to_all x1, blocking collectives, per_device(): plane_states = lax.all_to_all(message, ('y', 'x'), 0, 0)  17.8 us
    ppermute x1, starting transfers between devices, per_device(): other = lax.ppermute(params, 'zh', swap)  8.06 us
    ppermute x1, starting transfers between devices, per_device(): other_pair = lax.ppermute(pair, 'core', swap)  6.62 us
    unnamed x26, local copies, waits for them, and re-layouts  5.08 us
    ppermute x1, waiting for transfers between devices, per_device(): other = lax.ppermute(params, 'zh', swap)  3.13 us
    pallas_call x1, Pallas kernels, per_device(): call(local_kernel, shape(NP, ROWS, 128), 10 ** 8, 'local_states')  2.16 us
    pallas_call x1, Pallas kernels, per_device(): call(conv_kernel, (shape(128, 128),) * 4, 10 ** 8, 'local_conv')  1.94 us
  transfers between devices with their start and end apart: 2, of which 1 were waited for; matrix products, arithmetic and copies ran while one was open for 0% of the time, Pallas kernels for 4%

profile of v1, /device:TPU:1, one launch (start us, length us, event | category | flops | bytes accessed | tf_op | source)
XLA Modules:
  0.0 77.6 jit_solution(18440085786633443572)
XLA Ops:
  0.6 0.0 copy-start
  0.6 0.7 copy-done
  1.4 0.8 copy-done.2
  2.2 0.8 copy-done.4
  2.9 0.8 copy-done.6
  3.7 0.7 copy-done.8
  4.4 2.2 %local_states.1 = f32[16,72,128]{2,1,0:T(8,128)S(1)} custom-call(bf16[128,128]{1,0:T(8,128)(2,1)S(1)} %copy-done, bf16[128,128]{1,0:T(8,128)(2,1)S(1)} %copy-done.2, bf16[128,128]{1,0:T(8,128)(2,1)S(1)} %copy-done.4, bf16[128,128]{1,0:T(8,128)(2,1)S(1)} %copy-done.6, f32[8,16]{1,0:T(8,128)S(1)} %copy-done.8), custom_call_target="tpu_custom_call" | custom-call | flops 100000000 | bytes 500000 | tf_op jit(solution)/shard_map/local_states/pallas_call | solution.py:206
  6.5 17.8 %all_to_all.10.msg_ref = f32[16,72,128]{2,1,0:T(8,128)S(1)} all-to-all(f32[16,72,128]{2,1,0:T(8,128)S(1)} %local_states.1), channel_id=1, replica_groups=mesh['z'=8,'y'=4,'x'=4,'zh'=2,'core'=2] {'y','x'}, dimensions={0} | all-to-all | bytes 1179648 | tf_op jit(solution)/shard_map/all_to_all | solution.py:207
  24.3 0.0 copy-done.9
  24.3 0.4 plane_scan.1
  24.7 29.5 %all_to_all.11.msg_ref = f32[8,72,128]{2,1,0:T(8,128)S(1)} all-to-all(f32[8,72,128]{2,1,0:T(8,128)S(1)} %get-tuple-element.24), channel_id=1, replica_groups=mesh['z'=8,'y'=4,'x'=4,'zh'=2,'core'=2] {'z'}, dimensions={0} | all-to-all | bytes 589824 | tf_op jit(solution)/shard_map/all_to_all | solution.py:214
  54.2 0.0 copy-done.10
  54.2 0.0 copy-start.7
  54.2 1.1 %z_scan.1 = (f32[32,128]{1,0:T(8,128)S(1)}, f32[8,128]{1,0:T(8,128)S(1)}, f32[1,128]{1,0:T(1,128)}) custom-call(f32[8,72,128]{2,1,0:T(8,128)S(1)} %all_to_all.11.msg_ref, f32[8,16]{1,0:T(8,128)S(1)} %copy-done.9, f32[8,16]{1,0:T(8,128)S(1)} %copy-done.10, f32[32,128]{1,0:T(8,128)S(1)} %get-tuple-element.25.plane_ref), custom_call_target="tpu_custom_call" | custom-call | flops 10000000 | bytes 500000 | tf_op jit(solution)/shard_map/z_scan/pallas_call | solution.py:215
  55.3 8.1 %collective-permute-start = (f32[8,128]{1,0:T(8,128)S(1)}, f32[8,128]{1,0:T(8,128)S(1)}, u32[]{:S(2)}, u32[]{:S(2)}) collective-permute-start(f32[8,128]{1,0:T(8,128)S(1)} %get-tuple-element.32), channel_id=1, source_target_pairs={{0,2},{2,0},{1,3},{3,1},{4,6},{6,4},{5,7},{7,5},{8,10},{10,8},{9,1... | collective-permute-start | bytes 12296 | tf_op jit(solution)/shard_map/ppermute | solution.py:219
  63.4 0.0 copy-done.1
  63.5 1.9 %local_conv.1 = (f32[128,128]{1,0:T(8,128)S(1)}, f32[128,128]{1,0:T(8,128)S(1)}, f32[128,128]{1,0:T(8,128)S(1)}, f32[128,128]{1,0:T(8,128)S(1)}) custom-call(bf16[128,128]{1,0:T(8,128)(2,1)S(1)} %copy-done.1, bf16[128,128]{1,0:T(8,128)(2,1)S(1)} %copy-done.3, bf16[128,128]{1,0:T(8,128)(2,1)S(1)} %copy-done.5, bf16[128,128]{1,0:T(8,128)(2,1)S(1)} %copy-done.7, ...), custom_call_target="tpu_custom_call" | custom-call | flops 100000000 | bytes 500000 | tf_op jit(solution)/shard_map/local_conv/pallas_call | solution.py:208
  65.4 3.1 %collective-permute-done = f32[8,128]{1,0:T(8,128)S(1)} collective-permute-done((f32[8,128]{1,0:T(8,128)S(1)}, f32[8,128]{1,0:T(8,128)S(1)}, u32[]{:S(2)}, u32[]{:S(2)}) %collective-permute-start) | collective-permute-done | bytes 4128 | tf_op jit(solution)/shard_map/ppermute | solution.py:219
  68.5 6.6 %collective-permute-start.1 = (f32[2,8,128]{2,1,0:T(8,128)S(1)}, f32[2,8,128]{2,1,0:T(8,128)S(1)}, u32[]{:S(2)}, u32[]{:S(2)}) collective-permute-start(f32[2,8,128]{2,1,0:T(8,128)S(1)} %pad_maximum_fusion.1), channel_id=1, source_target_pairs={{0,1},{1,0},{2,3},{3,2},{4,5},{5,4},{6,7},{7,6},{8,9},{9,8},{10,11... | collective-permute-start | bytes 24584 | tf_op jit(solution)/shard_map/ppermute | solution.py:225
  75.2 1.0 %outputs.1 = (bf16[128,128]{1,0:T(8,128)(2,1)}, bf16[128,128]{1,0:T(8,128)(2,1)}, bf16[128,128]{1,0:T(8,128)(2,1)}, bf16[128,128]{1,0:T(8,128)(2,1)}) custom-call(bf16[128,128]{1,0:T(8,128)(2,1)S(1)} %copy-done.1, bf16[128,128]{1,0:T(8,128)(2,1)S(1)} %copy-done.3, bf16[128,128]{1,0:T(8,128)(2,1)S(1)} %copy-done.5, bf16[128,128]{1,0:T(8,128)(2,1)S(1)} %copy-done.7, ...), custom_call_target="tpu_custom_call" | custom-call | flops 100000000 | bytes 500000 | tf_op jit(solution)/shard_map/outputs/pallas_call | solution.py:220
  76.1 0.0 collective-permute-done.1
  76.2 0.1 fusion
  76.3 0.7 copy.15
  76.9 0.7 copy.16
  (19 shorter events, 0.0 us)
Async XLA Ops:
  0.6 0.8 copy-start
  1.4 0.8 copy-start.2
  2.2 0.8 copy-start.4
  2.9 0.8 copy-start.6
  3.7 0.7 copy-start.8
  6.5 17.8 %copy-start.9 = (f32[8,16]{1,0:T(8,128)S(1)}, f32[8,16]{1,0:T(8,128)}, u32[]{:S(2)}) copy-start(f32[8,16]{1,0:T(8,128)} %tau_ref.7) | copy-start | bytes 1540
  24.7 29.5 %copy-start.10 = (f32[8,16]{1,0:T(8,128)S(1)}, f32[8,16]{1,0:T(8,128)}, u32[]{:S(2)}) copy-start(f32[8,16]{1,0:T(8,128)} %res_ref.3) | copy-start | bytes 1540
  54.2 9.2 %copy-start.1 = (bf16[128,128]{1,0:T(8,128)(2,1)S(1)}, bf16[128,128]{1,0:T(8,128)(2,1)}, u32[]{:S(2)}) copy-start(bf16[128,128]{1,0:T(8,128)(2,1)} %q_ref.5) | copy-start | bytes 98308
  54.2 9.2 %copy-start.3 = (bf16[128,128]{1,0:T(8,128)(2,1)S(1)}, bf16[128,128]{1,0:T(8,128)(2,1)}, u32[]{:S(2)}) copy-start(bf16[128,128]{1,0:T(8,128)(2,1)} %k_ref.5) | copy-start | bytes 98308
  54.2 9.2 %copy-start.5 = (bf16[128,128]{1,0:T(8,128)(2,1)S(1)}, bf16[128,128]{1,0:T(8,128)(2,1)}, u32[]{:S(2)}) copy-start(bf16[128,128]{1,0:T(8,128)(2,1)} %v_ref.5) | copy-start | bytes 98308
  54.2 9.2 %copy-start.7 = (bf16[128,128]{1,0:T(8,128)(2,1)S(1)}, bf16[128,128]{1,0:T(8,128)(2,1)}, u32[]{:S(2)}) copy-start(bf16[128,128]{1,0:T(8,128)(2,1)} %ct_ref.5) | copy-start | bytes 98308
  55.3 8.1 %copy-start.11 = (f32[128]{0:T(128)S(1)}, f32[128]{0:T(128)}, u32[]{:S(2)}) copy-start(f32[128]{0:T(128)} %param.10) | copy-start | bytes 1540
  55.3 13.2 %collective-permute-start = (f32[8,128]{1,0:T(8,128)S(1)}, f32[8,128]{1,0:T(8,128)S(1)}, u32[]{:S(2)}, u32[]{:S(2)}) collective-permute-start(f32[8,128]{1,0:T(8,128)S(1)} %get-tuple-element.32), channel_id=1, source_target_pairs={{0,2},{2,0},{1,3},{3,1},{4,6},{6,4},{5,7},{7,5},{8,10},{10,8},{9,1... | collective-permute-start | bytes 12296 | tf_op jit(solution)/shard_map/ppermute | solution.py:219
  68.5 7.6 %collective-permute-start.1 = (f32[2,8,128]{2,1,0:T(8,128)S(1)}, f32[2,8,128]{2,1,0:T(8,128)S(1)}, u32[]{:S(2)}, u32[]{:S(2)}) collective-permute-start(f32[2,8,128]{2,1,0:T(8,128)S(1)} %pad_maximum_fusion.1), channel_id=1, source_target_pairs={{0,1},{1,0},{2,3},{3,2},{4,5},{5,4},{6,7},{7,6},{8,9},{9,8},{10,11... | collective-permute-start | bytes 24584 | tf_op jit(solution)/shard_map/ppermute | solution.py:225

commit v2 on v1

v2 whole, which is shorter than its diff:
```python
import math

import jax
import jax.numpy as jnp
from jax import lax
from jax.experimental import pallas as pl
from jax.experimental.pallas import tpu as pltpu
from jax.sharding import Mesh, PartitionSpec as P

F32 = jnp.float32
HI = lax.Precision.HIGHEST
L = 128
CH = 128
G = 8
R = 16
M = 16
MOMENT_ROW = 2 * R
SUM_ROW = MOMENT_ROW + R // 2
ROWS = SUM_ROW + G
NP = 16
NZ = 8
SHARE = CH // 4
Z_ROWS = 2 * R + G
PEERS = 16


def dot(a, b, ca=1, cb=0):
    return lax.dot_general(a, b, (((ca,), (cb,)), ((), ())), precision=HI, preferred_element_type=F32)


def iota(shape, axis):
    return lax.broadcasted_iota(jnp.int32, shape, axis)


def ones_where(cond):
    return jnp.where(cond, jnp.float32(1), jnp.float32(0))


def by_mode_and_channel(table):
    pick = ones_where(iota((G, CH), 1) // M == iota((G, CH), 0))
    return dot(table, pick, 0, 0)


def by_group_mode(table):
    pick = ones_where(iota((G * R, G), 0) // R == iota((G * R, G), 1))
    rows = dot(pick, table)
    rows = jnp.where(iota((G * R, R), 0) % R == iota((G * R, R), 1), rows, 0.0)
    return dot(rows, jnp.ones((R, L), F32))


def same_group():
    return iota((128, 128), 0) // M == iota((128, 128), 1) // M


def fold_states(full):
    own = jnp.where(same_group(), full, 0.0)
    return jnp.sum(own.reshape(G, R, CH), axis=0)


def spread_states(state):
    return jnp.where(same_group(), jnp.concatenate([state] * G, axis=0), 0.0)


def group_sums(h0, h1):
    pick = ones_where(iota((G, CH), 1) // M == iota((G, CH), 0))
    rows = jnp.concatenate([h0, h1, jnp.zeros((CH - 2 * R, CH), F32)], axis=0)
    return dot(pick, rows, 1, 1)


def fetch(pairs, sems):
    copies = [pltpu.make_async_copy(src, dst, sems.at[i]) for i, (src, dst) in enumerate(pairs)]
    for copy in copies:
        copy.start()
    for copy in copies:
        copy.wait()


def local_kernel(
    q_hbm, k_hbm, v_hbm, ct_hbm, tau_hbm, res_hbm, msg_ref, table_ref, q_ref, k_ref, v_ref, ct_ref, tau_ref, res_ref, sems
):
    fetch(
        (
            (tau_hbm, tau_ref),
            (q_hbm, q_ref),
            (k_hbm, k_ref),
            (v_hbm, v_ref),
            (ct_hbm, ct_ref),
            (res_hbm, res_ref),
        ),
        sems,
    )
    table_ref[0] = tau_ref[...]
    table_ref[1] = res_ref[...]
    product = q_ref[...].astype(F32) * k_ref[...].astype(F32)
    grad_mixed = ct_ref[...].astype(F32) * v_ref[...].astype(F32)
    rate = by_group_mode(1.0 / tau_ref[...])
    lane = iota((128, 128), 1)
    row = iota((128, 128), 0)
    step = lane.astype(F32)
    decay = jnp.exp(-step * rate)
    left = jnp.float32(L) - step
    decay_end = jnp.exp(-left * rate)
    fwd = dot(jnp.concatenate([decay_end, left * decay_end], axis=0), product, 1, 1)
    bwd = dot(jnp.concatenate([decay, step * decay], axis=0), grad_mixed, 1, 1)
    flipped = dot(product, ones_where(lane + row == L - 1))
    inside = lane + row >= L - 1
    lags = []
    for g in range(G):
        c = slice(g * M, (g + 1) * M)
        outer = jnp.where(inside, dot(flipped[c], grad_mixed[c], 0, 0), 0.0)
        aligned = pltpu.roll(outer, 1, 1, stride=1, stride_axis=0)
        lags.append(jnp.sum(aligned, axis=0, keepdims=True))
    lags = jnp.concatenate(lags, axis=0)
    lags = jnp.concatenate([lags, lags * iota((G, L), 1).astype(F32)], axis=0)
    modal = dot(lags, decay, 1, 1)
    modal = jnp.where(iota((2 * G, G * R), 0) % G == iota((2 * G, G * R), 1) // R, modal, 0.0)
    sums = dot(modal[:G], ones_where(row % R == lane)) + dot(modal[G:], ones_where(row % R == lane - R))
    skip_col = jnp.sum(grad_mixed * product, axis=1, keepdims=True)
    skip_at = jnp.where(row % M == lane - 2 * R, skip_col, 0.0)
    pick = ones_where(iota((G, CH), 1) // M == iota((G, CH), 0))
    sums = sums + dot(pick, skip_at)
    states = jnp.concatenate([fold_states(fwd[:128]), fold_states(bwd[:128])], axis=0)
    moments = (fold_states(fwd[128:]), fold_states(bwd[128:]))
    quarters = (moments[0][:8], moments[0][8:], moments[1][:8], moments[1][8:])
    for y in range(4):
        packed = jnp.zeros((8, CH), F32)
        for k, quarter in enumerate(quarters):
            packed = jnp.where(lane[:8] // SHARE == k, pltpu.roll(quarter, (k - y) % 4 * SHARE, 1), packed)
        for x in range(4):
            msg_ref[4 * y + x, :MOMENT_ROW] = states
            msg_ref[4 * y + x, MOMENT_ROW:SUM_ROW] = packed
            msg_ref[4 * y + x, SUM_ROW:] = sums


def conv_kernel(
    q_hbm, k_hbm, v_hbm, ct_hbm, skip_hbm, table_ref, fwd_ref, bwd_ref, head_ref, tail_ref, q_ref, k_ref, v_ref, ct_ref, skip_ref, sems
):
    fetch(((q_hbm, q_ref), (k_hbm, k_ref), (v_hbm, v_ref), (ct_hbm, ct_ref), (skip_hbm, skip_ref)), sems)
    product = q_ref[...].astype(F32) * k_ref[...].astype(F32)
    grad_mixed = ct_ref[...].astype(F32) * v_ref[...].astype(F32)
    inv = 1.0 / table_ref[0]
    rate = by_group_mode(inv)
    gain = by_group_mode(table_ref[1] * jnp.sqrt(2.0 * inv) * (1.0 / math.sqrt(R)))
    lane = iota((128, 128), 1)
    row = iota((128, 128), 0)
    step = lane.astype(F32)
    head = gain * jnp.exp(-step * rate)
    head_ref[...] = head
    tail_ref[...] = gain * jnp.exp(-(jnp.float32(L) - step) * rate)
    taps = jnp.sum(head.reshape(G, R, L), axis=1)
    skip = jnp.sum(jnp.where(lane == row, skip_ref[...], 0.0), axis=1, keepdims=True)
    for g in range(G):
        c = slice(g * M, (g + 1) * M)
        table = pltpu.roll(jnp.broadcast_to(taps[g : g + 1], (L, L)), 0, 1, stride=1, stride_axis=0)
        table = jnp.where(lane >= row, table, 0.0)
        fwd_ref[c] = dot(product[c], table) + skip[c] * product[c]
        bwd_ref[c] = dot(grad_mixed[c], table, 1, 1) + skip[c] * grad_mixed[c]


def plane_index():
    return lax.axis_index("y") * 4 + lax.axis_index("x")


def plane_kernel(msg_ref, table_ref, out_ref, carry_ref):
    rate = by_mode_and_channel(1.0 / table_ref[0])
    me = plane_index()
    y = lax.axis_index("y")
    span = jnp.float32(L)
    decay = jnp.exp(-span * rate)
    zero = jnp.zeros((R, CH), F32)

    def moments(i):
        packed = msg_ref[i, MOMENT_ROW:SUM_ROW]
        moved = [pltpu.roll(packed, lax.rem(y + 4 - k, 4) * SHARE, 1) for k in range(4)]
        return jnp.concatenate(moved[:2], axis=0), jnp.concatenate(moved[2:], axis=0)

    f, f1, h0, h1, own_f = zero, zero, zero, zero, zero
    sums = jnp.zeros((G, 128), F32)
    back_moments = []
    for i in range(NP):
        own_f = jnp.where(me == i, f, own_f)
        fwd, bwd = msg_ref[i, :R], msg_ref[i, R : 2 * R]
        fwd1, bwd1 = moments(i)
        back_moments.append(bwd1)
        h0 = h0 + f * bwd
        h1 = h1 + f * bwd1 + f1 * bwd
        f1 = decay * (f1 + span * f) + fwd1
        f = decay * f + fwd
        sums = sums + msg_ref[i, SUM_ROW:]
    b, b1, own_b = zero, zero, zero
    for i in reversed(range(NP)):
        own_b = jnp.where(me == i, b, own_b)
        b1 = decay * (b1 + span * b) + back_moments[i]
        b = decay * b + msg_ref[i, R : 2 * R]
    carry_ref[:R] = own_f
    carry_ref[R:] = own_b
    mine = iota((R, CH), 1) // SHARE == y
    sums = sums + group_sums(jnp.where(mine, h0, 0.0), jnp.where(mine, h1, 0.0))
    share = share_of(f, b, f1, b1)
    z = lax.axis_index("z")
    for i in range(NZ):
        out_ref[i, :R] = jnp.where(z < i, f, b)
        out_ref[i, R : 2 * R] = share
        out_ref[i, 2 * R :] = sums


def share_of(f, b, f1, b1):
    start = lax.axis_index("y") * SHARE
    lane = iota((R, CH), 1)
    out = jnp.zeros((R, CH), F32)
    for k, state in enumerate((f, b, f1, b1)):
        moved = pltpu.roll(state, lax.rem(k * SHARE + CH - start, CH), 1)
        out = jnp.where(lane // SHARE == k, moved, out)
    return out


def final_kernel(msg_ref, table_ref, plane_ref, carry_ref, param_ref, skip_ref):
    inv = 1.0 / table_ref[0]
    rate = by_mode_and_channel(inv)
    me = plane_index().astype(F32)
    z = lax.axis_index("z")
    y = lax.axis_index("y")
    span = jnp.float32(L * NP)
    decay = jnp.exp(-span * rate)
    share_decay = pltpu.roll(decay, lax.rem(CH - y * SHARE, CH), 1)
    zero = jnp.zeros((R, CH), F32)
    own_f, own_b, f, f1, h0, h1 = zero, zero, zero, zero, zero, zero
    sums = jnp.zeros((G, 128), F32)
    for i in range(NZ):
        own_f = jnp.where(i < z, decay * own_f + msg_ref[i, :R], own_f)
        part = msg_ref[i, R : 2 * R]
        back = pltpu.roll(part, CH - SHARE, 1)
        f1_part = pltpu.roll(part, CH - 2 * SHARE, 1)
        b1_part = pltpu.roll(part, CH - 3 * SHARE, 1)
        h0 = h0 + f * back
        h1 = h1 + f * b1_part + f1 * back
        f1 = share_decay * (f1 + span * f) + f1_part
        f = share_decay * f + part
        sums = sums + msg_ref[i, 2 * R :]
    for i in reversed(range(NZ)):
        own_b = jnp.where(i > z, decay * own_b + msg_ref[i, :R], own_b)
    carry_ref[:R] = plane_ref[:R] + jnp.exp(-(L * me) * rate) * own_f
    carry_ref[R:] = plane_ref[R:] + jnp.exp(-(L * (NP - 1 - me)) * rate) * own_b
    pick = ones_where(iota((G, CH), 1) // M + y * (SHARE // M) == iota((G, CH), 0)) * ones_where(iota((G, CH), 1) < SHARE)
    mine = iota((R, CH), 1) < SHARE
    pairs = jnp.concatenate([jnp.where(mine, h0, 0.0), jnp.where(mine, h1, 0.0)], axis=0)
    whole = dot(pick, pairs, 1, 1)
    whole = whole + sums[:, : 2 * R]
    scale = 1.0 / math.sqrt(L * NP * NZ * M)
    h0, h1 = whole[:, :R], whole[:, R:]
    root = jnp.sqrt(2.0 * inv) * (1.0 / math.sqrt(R))
    params = jnp.concatenate(
        [
            h0 * root * scale,
            table_ref[1] * root * (h1 * inv - 0.5 * h0) * scale,
            jnp.zeros((G, 128 - 2 * R), F32),
        ],
        axis=1,
    )
    group = iota((G, 128), 0) - 2 * y
    params = jnp.where(group == 0, params, 0.0) + jnp.where(group == 1, pltpu.roll(params, 2 * R, 1), 0.0)
    params = jnp.sum(params, axis=0, keepdims=True)
    for i in range(PEERS):
        param_ref[i] = params
    lane = iota((128, 128), 1)
    row = iota((128, 128), 0)
    spread = dot(sums, ones_where(row - 2 * R == lane % M) * ones_where(row >= 2 * R) * ones_where(row < 3 * R))
    spread = jnp.where(iota((G, CH), 1) // M == iota((G, CH), 0), spread, 0.0)
    skip_ref[...] = jnp.sum(spread, axis=0, keepdims=True) * (1.0 / math.sqrt(L * NP * NZ))


def gather_kernel(part_ref, residue_ref, time_ref):
    rows = part_ref[...].reshape(PEERS, 128)
    lane = iota((128, 4 * G), 0)
    group = iota((128, 4 * G), 1)
    spread = jnp.concatenate([rows, jnp.zeros((128 - PEERS, 128), F32)], axis=0)
    out = jnp.zeros((2 * R, 4 * G), F32)
    for b in range(2):
        pick = ones_where(iota((2 * R, 128), 1) == iota((2 * R, 128), 0) + 2 * R * b)
        part = dot(pick, spread, 1, 1)
        out = out + dot(part, ones_where(group == 2 * lane + b))
    residue_ref[...] = out[:R]
    time_ref[...] = out[R:]


def gather_groups():
    groups = []
    index = lambda zh, z, y, core: ((zh * NZ + z) * 4 + y) * 2 + core
    for z in range(NZ):
        planes = {0: z, 1: (z + 4) % NZ}
        groups.append([index(zh, planes[zh], y, core) for zh in range(2) for core in range(2) for y in range(4)])
    return groups


def output_kernel(
    q_hbm, k_hbm, v_hbm, ct_hbm, fwd_ref, bwd_ref, head_ref, tail_ref, carry_ref,
    out_ref, gq_ref, gk_ref, gv_ref, q_ref, k_ref, v_ref, ct_ref, sems,
):
    fetch(((q_hbm, q_ref), (k_hbm, k_ref), (v_hbm, v_ref), (ct_hbm, ct_ref)), sems)
    mixed = fwd_ref[...] + dot(spread_states(carry_ref[:R]), head_ref[...], 0, 0)
    grad_product = bwd_ref[...] + dot(spread_states(carry_ref[R:]), tail_ref[...], 0, 0)
    out_ref[...] = (v_ref[...].astype(F32) * mixed).astype(jnp.bfloat16)
    gv_ref[...] = (ct_ref[...].astype(F32) * mixed).astype(jnp.bfloat16)
    gq_ref[...] = (grad_product * k_ref[...].astype(F32)).astype(jnp.bfloat16)
    gk_ref[...] = (grad_product * q_ref[...].astype(F32)).astype(jnp.bfloat16)


def shape(*dims, dtype=F32):
    return jax.ShapeDtypeStruct(dims, dtype)


def call(kernel, outs, flops, name, vmem=32 * 1024 * 1024, **options):
    return pl.pallas_call(
        kernel,
        out_shape=outs,
        name=name,
        cost_estimate=pl.CostEstimate(flops=flops, bytes_accessed=500_000, transcendentals=0),
        compiler_params=pltpu.CompilerParams(vmem_limit_bytes=vmem),
        **options,
    )


def per_device(queries, key_inputs, value_inputs, skip_gain, residue, timescale, cotangent):
    arrays = (queries, key_inputs, value_inputs, cotangent)
    hbm = pl.BlockSpec(memory_space=pltpu.HBM)
    local = pl.BlockSpec(memory_space=pltpu.VMEM)
    blocks = [pltpu.VMEM((CH, L), jnp.bfloat16)] * 4
    small = pltpu.VMEM((G, R), F32)
    message, table = call(
        local_kernel,
        (shape(NP, ROWS, 128), shape(2, G, R)),
        10**8,
        "local_states",
        vmem=62914560,
        in_specs=[hbm] * 6,
        scratch_shapes=[*blocks, small, small, pltpu.SemaphoreType.DMA((6,))],
    )(*arrays, timescale, residue)
    plane_states = lax.all_to_all(message, ("y", "x"), 0, 0)
    tables = call(
        conv_kernel,
        (shape(128, 128),) * 4,
        10**8,
        "local_conv",
        in_specs=[hbm] * 5 + [local],
        scratch_shapes=[*blocks, pltpu.VMEM((1, CH), F32), pltpu.SemaphoreType.DMA((5,))],
    )(*arrays, skip_gain.reshape(1, CH), table)
    totals, plane_carry = call(plane_kernel, (shape(NZ, Z_ROWS, 128), shape(2 * R, CH)), 10**7, "plane_scan")(
        plane_states, table
    )
    z_states = lax.all_to_all(totals, "z", 0, 0)
    carry, params, grad_skip = call(
        final_kernel, (shape(2 * R, CH), shape(PEERS, 1, 128), shape(1, CH)), 10**7, "z_scan"
    )(z_states, table, plane_carry)
    params = lax.all_to_all(params, ("zh", "z", "y", "core"), 0, 0, axis_index_groups=gather_groups())
    output, grad_queries, grad_keys, grad_values = call(
        output_kernel,
        (shape(CH, L, dtype=jnp.bfloat16),) * 4,
        10**8,
        "outputs",
        in_specs=[hbm] * 4 + [local] * 5,
        scratch_shapes=[*blocks, pltpu.SemaphoreType.DMA((4,))],
    )(*arrays, *tables, carry)
    grad_residue, grad_time = call(gather_kernel, (shape(R, 4 * G),) * 2, 10**6, "gather")(params)
    return (
        output,
        grad_queries,
        grad_keys,
        grad_values,
        grad_skip.reshape(CH),
        grad_residue.T,
        grad_time.T,
    )


def solution(mesh):
    grid = Mesh(mesh.devices.reshape(NZ, 4, 4, 2, 2), ("z", "y", "x", "zh", "core"))
    seq = ("z", "y", "x")
    ch = ("zh", "core")
    return jax.shard_map(
        per_device,
        mesh=grid,
        in_specs=(P(ch, seq), P(ch, seq), P(ch, seq), P(ch), P(ch, None), P(ch, None), P(ch, seq)),
        out_specs=(P(ch, seq), P(ch, seq), P(ch, seq), P(ch, seq), P(ch), P(), P()),
        check_vma=False,
    )
```

time: 78.2 us -> 63 us (0.81)
  starting transfers between devices: 14.7 us -> 6.51 us
  blocking collectives: 47.3 us -> 39.5 us
  local copies, waits for them, and re-layouts: 5.15 us -> 0.63 us
  Pallas kernels: 6.6 us -> 9.91 us
  waiting for transfers between devices: 3.13 us -> 5.35 us
    ppermute x2 -> x0, starting transfers between devices: 14.7 us -> none  [the longest x1 8.06 us: per_device(): other = lax.ppermute(params, 'zh', swap)]
    all_to_all x0 -> x1, starting transfers between devices: none -> 6.51 us  [per_device(): lax.all_to_all(params, ('zh', 'z', 'y', 'core'), 0, 0, axis_index_groups=...]
    all_to_all x1, blocking collectives: 29.5 us -> 23.7 us  [per_device(): z_states = lax.all_to_all(totals, 'z', 0, 0)]
    all_to_all x0 -> x1, waiting for transfers between devices: none -> 5.35 us  [per_device(): lax.all_to_all(params, ('zh', 'z', 'y', 'core'), 0, 0, axis_index_groups=...]
    unnamed x26 -> x12, local copies, waits for them, and re-layouts: 5.08 us -> 0.63 us
    ppermute x2 -> x0, waiting for transfers between devices: 3.13 us -> none  [the longest x1 3.13 us: per_device(): other = lax.ppermute(params, 'zh', swap)]
    pallas_call x4 -> x5, Pallas kernels: 5.63 us -> 8.73 us  [the longest x1 3.79 us: per_device(): call(local_kernel, (shape(NP, ROWS, 128), shape(2, G, R)), 10 ** 8, 'loca...]
    all_to_all x1, blocking collectives: 17.8 us -> 15.8 us  [per_device(): plane_states = lax.all_to_all(message, ('y', 'x'), 0, 0)]
  transfers between devices with their start and end apart: 2 -> 1, of which waited for: 1 -> 1; matrix products, arithmetic and copies ran while one was open for 0% -> 0% of each run, Pallas kernels for 4% -> 5%
where the time goes in v2:
time: 63 us; the launch traced here: 62.6 us
  blocking collectives  39.5 us (63%)
  Pallas kernels  9.91 us (16%)
  starting transfers between devices  6.51 us (10%)
  waiting for transfers between devices  5.35 us (8%)
  between operations  0.71 us (1%)
  local copies, waits for them, and re-layouts  0.63 us (1%)
    all_to_all x1, blocking collectives, per_device(): z_states = lax.all_to_all(totals, 'z', 0, 0)  23.7 us
    all_to_all x1, blocking collectives, per_device(): plane_states = lax.all_to_all(message, ('y', 'x'), 0, 0)  15.8 us
    all_to_all x1, starting transfers between devices, per_device(): lax.all_to_all(params, ('zh', 'z', 'y', 'core'), 0, 0, axis_index_groups=...  6.51 us
    all_to_all x1, waiting for transfers between devices, per_device(): lax.all_to_all(params, ('zh', 'z', 'y', 'core'), 0, 0, axis_index_groups=...  5.35 us
    pallas_call x1, Pallas kernels, per_device(): call(local_kernel, (shape(NP, ROWS, 128), shape(2, G, R)), 10 ** 8, 'loca...  3.79 us
    pallas_call x1, Pallas kernels, per_device(): call(conv_kernel, (shape(128, 128),) * 4, 10 ** 8, 'local_conv', in_specs...  2.13 us
    pallas_call x1, Pallas kernels, per_device(): call(final_kernel, (shape(2 * R, CH), shape(PEERS, 1, 128), shape(1, CH))...  1.37 us
  transfers between devices with their start and end apart: 1, of which 1 were waited for; matrix products, arithmetic and copies ran while one was open for 0% of the time, Pallas kernels for 5%

profile of v2, /device:TPU:1, one launch (start us, length us, event | category | flops | bytes accessed | tf_op | source)
XLA Modules:
  0.0 62.6 jit_solution(4516865128709696918)
XLA Ops:
  0.6 3.8 %local_states.1 = (f32[16,48,128]{2,1,0:T(8,128)}, f32[2,8,16]{2,1,0:T(8,128)}) custom-call(bf16[128,128]{1,0:T(8,128)(2,1)} %q_hbm.5, bf16[128,128]{1,0:T(8,128)(2,1)} %k_hbm.5, bf16[128,128]{1,0:T(8,128)(2,1)} %v_hbm.5, bf16[128,128]{1,0:T(8,128)(2,1)} %ct_hbm.5, f32[8,16]{1,0:T(8,128)} %tau_hbm.1, f32[8,16]{1,0:T(8,128)} %res_hbm.1), custom_call_target="tpu_custom_call" | custom-call | flops 100000000 | bytes 500000 | tf_op jit(solution)/shard_map/local_states/pallas_call | solution.py:329
  4.4 0.0 copy-start.4
  4.4 15.8 %all_to_all.15.msg_ref = f32[16,48,128]{2,1,0:T(8,128)S(1)} all-to-all(f32[16,48,128]{2,1,0:T(8,128)} %get-tuple-element.29), channel_id=1, replica_groups=mesh['z'=8,'y'=4,'x'=4,'zh'=2,'core'=2] {'y','x'}, dimensions={0} | all-to-all | bytes 786432 | tf_op jit(solution)/shard_map/all_to_all | solution.py:338
  20.3 0.0 copy-done.4
  20.3 0.5 plane_scan.1
  20.7 23.7 %all_to_all.16.msg_ref = f32[8,40,128]{2,1,0:T(8,128)S(1)} all-to-all(f32[8,40,128]{2,1,0:T(8,128)S(1)} %get-tuple-element.30), channel_id=1, replica_groups=mesh['z'=8,'y'=4,'x'=4,'zh'=2,'core'=2] {'z'}, dimensions={0} | all-to-all | bytes 327680 | tf_op jit(solution)/shard_map/all_to_all | solution.py:350
  44.4 0.0 copy-start
  44.4 0.0 copy-start.1
  44.4 0.0 copy-start.2
  44.4 0.0 copy-start.3
  44.4 1.4 %z_scan.1 = (f32[32,128]{1,0:T(8,128)S(1)}, f32[16,1,128]{2,1,0:T(1,128)}, f32[1,128]{1,0:T(1,128)}) custom-call(f32[8,40,128]{2,1,0:T(8,128)S(1)} %all_to_all.16.msg_ref, f32[2,8,16]{2,1,0:T(8,128)S(1)} %copy-done.4, f32[32,128]{1,0:T(8,128)S(1)} %get-tuple-element.31.plane_ref), custom_call_target="tpu_custom_call" | custom-call | flops 10000000 | bytes 500000 | tf_op jit(solution)/shard_map/z_scan/pallas_call | solution.py:351
  45.8 6.5 %all-to-all-start.2 = ((f32[16,1,128]{2,1,0:T(1,128)}), f32[16,1,128]{2,1,0:T(1,128)S(1)}, u32[]{:S(2)}, u32[]{:S(2)}) async-start(f32[16,1,128]{2,1,0:T(1,128)} %get-tuple-element.38), calls=%async_computation.2 | async-start | bytes 16384 | tf_op jit(solution)/shard_map/all_to_all | solution.py:354
  52.3 0.0 copy-start.5
  52.3 0.0 copy-done
  52.3 0.0 copy-done.1
  52.3 0.0 copy-done.2
  52.4 0.0 copy-done.3
  52.4 0.6 copy-done.5
  53.0 2.1 %local_conv.1 = (f32[128,128]{1,0:T(8,128)S(1)}, f32[128,128]{1,0:T(8,128)S(1)}, f32[128,128]{1,0:T(8,128)S(1)}, f32[128,128]{1,0:T(8,128)S(1)}) custom-call(bf16[128,128]{1,0:T(8,128)(2,1)S(1)} %copy-done, bf16[128,128]{1,0:T(8,128)(2,1)S(1)} %copy-done.1, bf16[128,128]{1,0:T(8,128)(2,1)S(1)} %copy-done.2, bf16[128,128]{1,0:T(8,128)(2,1)S(1)} %copy-done.3, ...), custom_call_target="tpu_custom_call" | custom-call | flops 100000000 | bytes 500000 | tf_op jit(solution)/shard_map/local_conv/pallas_call | solution.py:339
  55.1 1.2 %outputs.1 = (bf16[128,128]{1,0:T(8,128)(2,1)}, bf16[128,128]{1,0:T(8,128)(2,1)}, bf16[128,128]{1,0:T(8,128)(2,1)}, bf16[128,128]{1,0:T(8,128)(2,1)}) custom-call(bf16[128,128]{1,0:T(8,128)(2,1)S(1)} %copy-done, bf16[128,128]{1,0:T(8,128)(2,1)S(1)} %copy-done.1, bf16[128,128]{1,0:T(8,128)(2,1)S(1)} %copy-done.2, bf16[128,128]{1,0:T(8,128)(2,1)S(1)} %copy-done.3, ...), custom_call_target="tpu_custom_call" | custom-call | flops 100000000 | bytes 500000 | tf_op jit(solution)/shard_map/outputs/pallas_call | solution.py:355
  56.3 5.4 %all-to-all-done.2.part_ref = f32[16,1,128]{2,1,0:T(1,128)S(1)} async-done(((f32[16,1,128]{2,1,0:T(1,128)}), f32[16,1,128]{2,1,0:T(1,128)S(1)}, u32[]{:S(2)}, u32[]{:S(2)}) %all-to-all-start.2) | async-done | bytes 8224 | tf_op jit(solution)/shard_map/all_to_all | solution.py:354
  61.7 1.0 %gather.1 = (f32[16,32]{1,0:T(8,128)}, f32[16,32]{1,0:T(8,128)}) custom-call(f32[16,1,128]{2,1,0:T(1,128)S(1)} %all-to-all-done.2.part_ref), custom_call_target="tpu_custom_call" | custom-call | flops 1000000 | bytes 500000 | tf_op jit(solution)/shard_map/gather/pallas_call | solution.py:363
Async XLA Ops:
  4.4 15.8 %copy-start.4 = (f32[2,8,16]{2,1,0:T(8,128)S(1)}, f32[2,8,16]{2,1,0:T(8,128)}, u32[]{:S(2)}) copy-start(f32[2,8,16]{2,1,0:T(8,128)} %get-tuple-element.24.table_ref) | copy-start | bytes 3076
  44.4 7.9 %copy-start = (bf16[128,128]{1,0:T(8,128)(2,1)S(1)}, bf16[128,128]{1,0:T(8,128)(2,1)}, u32[]{:S(2)}) copy-start(bf16[128,128]{1,0:T(8,128)(2,1)} %q_hbm.5) | copy-start | bytes 98308
  44.4 7.9 %copy-start.1 = (bf16[128,128]{1,0:T(8,128)(2,1)S(1)}, bf16[128,128]{1,0:T(8,128)(2,1)}, u32[]{:S(2)}) copy-start(bf16[128,128]{1,0:T(8,128)(2,1)} %k_hbm.5) | copy-start | bytes 98308
  44.4 7.9 %copy-start.2 = (bf16[128,128]{1,0:T(8,128)(2,1)S(1)}, bf16[128,128]{1,0:T(8,128)(2,1)}, u32[]{:S(2)}) copy-start(bf16[128,128]{1,0:T(8,128)(2,1)} %v_hbm.5) | copy-start | bytes 98308
  44.4 7.9 %copy-start.3 = (bf16[128,128]{1,0:T(8,128)(2,1)S(1)}, bf16[128,128]{1,0:T(8,128)(2,1)}, u32[]{:S(2)}) copy-start(bf16[128,128]{1,0:T(8,128)(2,1)} %ct_hbm.5) | copy-start | bytes 98308
  45.8 15.9 %all-to-all-start.2 = ((f32[16,1,128]{2,1,0:T(1,128)}), f32[16,1,128]{2,1,0:T(1,128)S(1)}, u32[]{:S(2)}, u32[]{:S(2)}) async-start(f32[16,1,128]{2,1,0:T(1,128)} %get-tuple-element.38), calls=%async_computation.2 | async-start | bytes 16384 | tf_op jit(solution)/shard_map/all_to_all | solution.py:354
  52.3 0.7 %copy-start.5 = (f32[128]{0:T(128)S(1)}, f32[128]{0:T(128)}, u32[]{:S(2)}) copy-start(f32[128]{0:T(128)} %param.10) | copy-start | bytes 1540

commit v3 on v2

v3 whole, which is shorter than its diff:
```python
import math

import jax
import jax.numpy as jnp
from jax import lax
from jax.experimental import pallas as pl
from jax.experimental.pallas import tpu as pltpu
from jax.sharding import Mesh, PartitionSpec as P

F32 = jnp.float32
HI = lax.Precision.HIGHEST
L = 128
CH = 128
G = 8
R = 16
M = 16
MOMENT_ROW = 2 * R
SUM_ROW = MOMENT_ROW + R // 2
ROWS = SUM_ROW + G
NP = 16
NZ = 8
SHARE = CH // 4
Z_ROWS = 2 * R + G
PEERS = 16
PLANE_FIRST = 15
Z_FIRST = (7, 4)


def dot(a, b, ca=1, cb=0):
    return lax.dot_general(a, b, (((ca,), (cb,)), ((), ())), precision=HI, preferred_element_type=F32)


def halves(value):
    high = value.astype(jnp.bfloat16)
    return high, (value - high.astype(F32)).astype(jnp.bfloat16)


def dot3(a, b, ca=1, cb=0):
    (a_high, a_low), (b_high, b_low) = halves(a), halves(b)
    left = jnp.concatenate([a_high, a_high, a_low], axis=ca)
    right = jnp.concatenate([b_high, b_low, b_high], axis=cb)
    return lax.dot_general(left, right, (((ca,), (cb,)), ((), ())), preferred_element_type=F32)


def pick_dot(pick, b, ca=1, cb=0):
    pick = pick.astype(jnp.bfloat16)
    left = jnp.concatenate([pick, pick], axis=ca)
    right = jnp.concatenate(halves(b), axis=cb)
    return lax.dot_general(left, right, (((ca,), (cb,)), ((), ())), preferred_element_type=F32)


def pick_dot_right(a, pick):
    pick = pick.astype(jnp.bfloat16)
    left = jnp.concatenate(halves(a), axis=1)
    right = jnp.concatenate([pick, pick], axis=0)
    return lax.dot_general(left, right, (((1,), (0,)), ((), ())), preferred_element_type=F32)


def iota(shape, axis):
    return lax.broadcasted_iota(jnp.int32, shape, axis)


def ones_where(cond):
    return jnp.where(cond, jnp.float32(1), jnp.float32(0))


def by_mode_and_channel(table):
    pick = ones_where(iota((G, CH), 1) // M == iota((G, CH), 0))
    return dot(table, pick, 0, 0)


def by_group_mode(table):
    rows = jnp.concatenate([jnp.broadcast_to(table[g : g + 1], (R, R)) for g in range(G)], axis=0)
    rows = jnp.where(iota((G * R, R), 0) % R == iota((G * R, R), 1), rows, 0.0)
    return jnp.sum(rows, axis=1, keepdims=True)


def same_group():
    return iota((128, 128), 0) // M == iota((128, 128), 1) // M


def fold_states(full):
    own = jnp.where(same_group(), full, 0.0)
    return jnp.sum(own.reshape(G, R, CH), axis=0)


def spread_states(state):
    return jnp.where(same_group(), jnp.concatenate([state] * G, axis=0), 0.0)


def group_sums(h0, h1):
    pick = ones_where(iota((G, CH), 1) // M == iota((G, CH), 0))
    rows = jnp.concatenate([h0, h1, jnp.zeros((CH - 2 * R, CH), F32)], axis=0)
    return pick_dot(pick, rows, 1, 1)


def fetch(pairs, sems):
    copies = [pltpu.make_async_copy(src, dst, sems.at[i]) for i, (src, dst) in enumerate(pairs)]
    for copy in copies:
        copy.start()
    for copy in copies:
        copy.wait()


def local_kernel(
    q_hbm, k_hbm, v_hbm, ct_hbm, tau_hbm, res_hbm, msg_hbm, table_ref,
    q_ref, k_ref, v_ref, ct_ref, states_ref, packed_ref, sums_ref, sems, out_sems,
):
    fetch(
        (
            (tau_hbm, table_ref.at[0]),
            (q_hbm, q_ref),
            (k_hbm, k_ref),
            (v_hbm, v_ref),
            (ct_hbm, ct_ref),
            (res_hbm, table_ref.at[1]),
        ),
        sems,
    )
    product = q_ref[...].astype(F32) * k_ref[...].astype(F32)
    grad_mixed = ct_ref[...].astype(F32) * v_ref[...].astype(F32)
    rate = by_group_mode(1.0 / table_ref[0])
    lane = iota((128, 128), 1)
    row = iota((128, 128), 0)
    step = lane.astype(F32)
    decay = jnp.exp(-step * rate)
    left = jnp.float32(L) - step
    decay_end = jnp.exp(-left * rate)
    fwd = dot3(jnp.concatenate([decay_end, left * decay_end], axis=0), product, 1, 1)
    bwd = dot3(jnp.concatenate([decay, step * decay], axis=0), grad_mixed, 1, 1)
    states_ref[:R] = fold_states(fwd[:128])
    states_ref[R:] = fold_states(bwd[:128])
    copies = []

    def send(source, i, rows):
        copies.append(pltpu.make_async_copy(source, msg_hbm.at[plane_slot(i), rows], out_sems.at[len(copies)]))
        copies[-1].start()

    for i in range(NP):
        send(states_ref, i, slice(0, MOMENT_ROW))
    moments = (fold_states(fwd[128:]), fold_states(bwd[128:]))
    quarters = (moments[0][:8], moments[0][8:], moments[1][:8], moments[1][8:])
    for y in range(4):
        packed = jnp.zeros((8, CH), F32)
        for k, quarter in enumerate(quarters):
            packed = jnp.where(lane[:8] // SHARE == k, pltpu.roll(quarter, (k - y) % 4 * SHARE, 1), packed)
        packed_ref[y] = packed
    for i in range(NP):
        send(packed_ref.at[i // 4], i, slice(MOMENT_ROW, SUM_ROW))
    flipped = pick_dot_right(product, ones_where(lane + row == L - 1))
    inside = lane + row >= L - 1
    lags = []
    for g in range(G):
        c = slice(g * M, (g + 1) * M)
        outer = jnp.where(inside, dot3(flipped[c], grad_mixed[c], 0, 0), 0.0)
        lags.append(jnp.sum(pltpu.roll(outer, 1, 1, stride=1, stride_axis=0), axis=0, keepdims=True))
    lags = jnp.concatenate(lags, axis=0)
    lags = jnp.concatenate([lags, lags * step[:G]], axis=0)
    modal = dot3(lags, decay, 1, 1)
    modal = jnp.where(iota((2 * G, G * R), 0) % G == iota((2 * G, G * R), 1) // R, modal, 0.0)
    modal = jnp.concatenate([modal[:G], modal[G:]], axis=1)
    fold = iota((2 * G * R, 128), 0)
    fold = ones_where(fold % R + fold // (G * R) * R == iota((2 * G * R, 128), 1))
    skip = jnp.sum(grad_mixed * product, axis=1, keepdims=True)
    skip = jnp.where(row % M == lane - 2 * R, skip, 0.0)
    pick = ones_where(iota((G, CH), 1) // M == iota((G, CH), 0))
    sums_ref[...] = pick_dot_right(modal, fold) + pick_dot(pick, skip)
    for i in range(NP):
        send(sums_ref, i, slice(SUM_ROW, ROWS))
    for copy in copies:
        copy.wait()


def conv_kernel(
    q_hbm, k_hbm, v_hbm, ct_hbm, skip_hbm, table_ref, fwd_ref, bwd_ref, head_ref, tail_ref, q_ref, k_ref, v_ref, ct_ref, skip_ref, sems
):
    fetch(((q_hbm, q_ref), (k_hbm, k_ref), (v_hbm, v_ref), (ct_hbm, ct_ref), (skip_hbm, skip_ref)), sems)
    product = q_ref[...].astype(F32) * k_ref[...].astype(F32)
    grad_mixed = ct_ref[...].astype(F32) * v_ref[...].astype(F32)
    inv = 1.0 / table_ref[0]
    rate = by_group_mode(inv)
    gain = by_group_mode(table_ref[1] * jnp.sqrt(2.0 * inv) * (1.0 / math.sqrt(R)))
    lane = iota((128, 128), 1)
    row = iota((128, 128), 0)
    step = lane.astype(F32)
    head = gain * jnp.exp(-step * rate)
    head_ref[...] = head
    tail_ref[...] = gain * jnp.exp(-(jnp.float32(L) - step) * rate)
    taps = jnp.sum(head.reshape(G, R, L), axis=1)
    skip = jnp.sum(jnp.where(lane == row, skip_ref[...], 0.0), axis=1, keepdims=True)
    for g in range(G):
        c = slice(g * M, (g + 1) * M)
        table = pltpu.roll(jnp.broadcast_to(taps[g : g + 1], (L, L)), 0, 1, stride=1, stride_axis=0)
        table = jnp.where(lane >= row, table, 0.0)
        fwd_ref[c] = dot(product[c], table) + skip[c] * product[c]
        bwd_ref[c] = dot(grad_mixed[c], table, 1, 1) + skip[c] * grad_mixed[c]


def plane_index():
    return lax.axis_index("y") * 4 + lax.axis_index("x")


def plane_kernel(msg_ref, table_ref, out_ref, carry_ref):
    rate = by_mode_and_channel(1.0 / table_ref[0])
    me = plane_index()
    y = lax.axis_index("y")
    span = jnp.float32(L)
    decay = jnp.exp(-span * rate)
    zero = jnp.zeros((R, CH), F32)

    def moments(i):
        packed = msg_ref[plane_slot(i), MOMENT_ROW:SUM_ROW]
        moved = [pltpu.roll(packed, lax.rem(y + 4 - k, 4) * SHARE, 1) for k in range(4)]
        return jnp.concatenate(moved[:2], axis=0), jnp.concatenate(moved[2:], axis=0)

    f, f1, h0, h1, own_f = zero, zero, zero, zero, zero
    sums = jnp.zeros((G, 128), F32)
    back_moments = []
    for i in range(NP):
        own_f = jnp.where(me == i, f, own_f)
        fwd, bwd = msg_ref[plane_slot(i), :R], msg_ref[plane_slot(i), R : 2 * R]
        fwd1, bwd1 = moments(i)
        back_moments.append(bwd1)
        h0 = h0 + f * bwd
        h1 = h1 + f * bwd1 + f1 * bwd
        f1 = decay * (f1 + span * f) + fwd1
        f = decay * f + fwd
        sums = sums + msg_ref[plane_slot(i), SUM_ROW:]
    b, b1, own_b = zero, zero, zero
    for i in reversed(range(NP)):
        own_b = jnp.where(me == i, b, own_b)
        b1 = decay * (b1 + span * b) + back_moments[i]
        b = decay * b + msg_ref[plane_slot(i), R : 2 * R]
    carry_ref[:R] = own_f
    carry_ref[R : 2 * R] = own_b
    carry_ref[2 * R :] = rate
    mine = iota((R, CH), 1) // SHARE == y
    sums = sums + group_sums(jnp.where(mine, h0, 0.0), jnp.where(mine, h1, 0.0))
    share = share_of(f, b, f1, b1)
    z = lax.axis_index("z")
    for i in range(NZ):
        out_ref[z_slot(i), :R] = jnp.where(z < i, f, b)
        out_ref[z_slot(i), R : 2 * R] = share
        out_ref[z_slot(i), 2 * R :] = sums


def share_of(f, b, f1, b1):
    start = lax.axis_index("y") * SHARE
    lane = iota((R, CH), 1)
    out = jnp.zeros((R, CH), F32)
    for k, state in enumerate((f, b, f1, b1)):
        moved = pltpu.roll(state, lax.rem(k * SHARE + CH - start, CH), 1)
        out = jnp.where(lane // SHARE == k, moved, out)
    return out


def final_kernel(msg_ref, table_ref, plane_ref, param_ref):
    inv = 1.0 / table_ref[0]
    y = lax.axis_index("y")
    span = jnp.float32(L * NP)
    decay = jnp.exp(-span * pltpu.roll(plane_ref[2 * R :], lax.rem(CH - y * SHARE, CH), 1))
    zero = jnp.zeros((R, CH), F32)
    f, f1, h0, h1 = zero, zero, zero, zero
    sums = jnp.zeros((G, 128), F32)
    for i in range(NZ):
        part = msg_ref[z_slot(i), R : 2 * R]
        back = pltpu.roll(part, CH - SHARE, 1)
        f1_part = pltpu.roll(part, CH - 2 * SHARE, 1)
        b1_part = pltpu.roll(part, CH - 3 * SHARE, 1)
        h0 = h0 + f * back
        h1 = h1 + f * b1_part + f1 * back
        f1 = decay * (f1 + span * f) + f1_part
        f = decay * f + part
        sums = sums + msg_ref[z_slot(i), 2 * R :]
    pick = ones_where(iota((G, CH), 1) // M + y * (SHARE // M) == iota((G, CH), 0)) * ones_where(iota((G, CH), 1) < SHARE)
    mine = iota((R, CH), 1) < SHARE
    pairs = jnp.concatenate([jnp.where(mine, h0, 0.0), jnp.where(mine, h1, 0.0)], axis=0)
    whole = pick_dot(pick, pairs, 1, 1) + sums[:, : 2 * R]
    scale = 1.0 / math.sqrt(L * NP * NZ * M)
    h0, h1 = whole[:, :R], whole[:, R:]
    root = jnp.sqrt(2.0 * inv) * (scale / math.sqrt(R))
    params = jnp.concatenate(
        [h0 * root, table_ref[1] * root * (h1 * inv - 0.5 * h0), jnp.zeros((G, 128 - 2 * R), F32)], axis=1
    )
    group = iota((G, 128), 0) - 2 * y
    params = jnp.where(group == 0, params, 0.0) + jnp.where(group == 1, pltpu.roll(params, 2 * R, 1), 0.0)
    params = jnp.sum(params, axis=0, keepdims=True)
    for i in range(PEERS):
        param_ref[i] = params


def gather_kernel(part_ref, residue_ref, time_ref):
    rows = part_ref[...].reshape(PEERS, 128)
    columns = jnp.concatenate([rows, jnp.zeros((128 - PEERS, 128), F32)], axis=0).T
    peer = iota((128, 4 * G), 0)
    group = iota((128, 4 * G), 1)
    y, core, zh = peer % 4, peer // 4 % 2, 1 - peer // 8
    first = (zh * 2 + core) * G + 2 * y
    out = jnp.zeros((2 * R, 4 * G), F32)
    for b in range(2):
        place = ones_where((group == first + b) & (peer < PEERS)).astype(jnp.bfloat16)
        for half in halves(columns[2 * R * b : 2 * R * (b + 1)]):
            out = out + lax.dot_general(half, place, (((1,), (0,)), ((), ())), preferred_element_type=F32)
    residue_ref[...] = out[:R]
    time_ref[...] = out[R:]


def plane_slot(p):
    return (p - PLANE_FIRST) % NP


def z_slot(z):
    first = jnp.where(lax.axis_index("zh") == 1, Z_FIRST[1], Z_FIRST[0])
    return lax.rem(z + NZ - first, NZ)


def plane_groups():
    return [[(PLANE_FIRST + i) % NP for i in range(NP)]]


def z_groups():
    return [[zh * NZ + (first + i) % NZ for i in range(NZ)] for zh, first in enumerate(Z_FIRST)]


def gather_groups():
    groups = []
    index = lambda zh, z, y, core: ((zh * NZ + z) * 4 + y) * 2 + core
    for z in range(NZ):
        planes = {0: z, 1: (z + 4) % NZ}
        groups.append([index(zh, planes[zh], y, core) for zh in (1, 0) for core in range(2) for y in range(4)])
    return groups


def output_kernel(
    q_hbm, k_hbm, v_hbm, ct_hbm, fwd_ref, bwd_ref, head_ref, tail_ref, msg_ref, plane_ref,
    out_ref, gq_ref, gk_ref, gv_ref, skip_ref, q_ref, k_ref, v_ref, ct_ref, sems,
):
    fetch(((q_hbm, q_ref), (k_hbm, k_ref), (v_hbm, v_ref), (ct_hbm, ct_ref)), sems)
    rate = plane_ref[2 * R :]
    z = lax.axis_index("z")
    me = plane_index().astype(F32)
    decay = jnp.exp(-jnp.float32(L * NP) * rate)
    own_f = jnp.zeros((R, CH), F32)
    own_b = own_f
    sums = jnp.zeros((G, 128), F32)
    for i in range(NZ):
        own_f = jnp.where(i < z, decay * own_f + msg_ref[z_slot(i), :R], own_f)
        sums = sums + msg_ref[z_slot(i), 2 * R :]
    for i in reversed(range(NZ)):
        own_b = jnp.where(i > z, decay * own_b + msg_ref[z_slot(i), :R], own_b)
    own_f = plane_ref[:R] + jnp.exp(-(L * me) * rate) * own_f
    own_b = plane_ref[R : 2 * R] + jnp.exp(-(L * (NP - 1 - me)) * rate) * own_b
    lane = iota((128, 128), 1)
    row = iota((128, 128), 0)
    spread = dot(sums, ones_where((row - 2 * R == lane % M) & (row >= 2 * R) & (row < 3 * R)))
    spread = jnp.where(iota((G, CH), 1) // M == iota((G, CH), 0), spread, 0.0)
    skip_ref[...] = jnp.sum(spread, axis=0, keepdims=True) * (1.0 / math.sqrt(L * NP * NZ))
    mixed = fwd_ref[...] + dot3(spread_states(own_f), head_ref[...], 0, 0)
    grad_product = bwd_ref[...] + dot3(spread_states(own_b), tail_ref[...], 0, 0)
    out_ref[...] = (v_ref[...].astype(F32) * mixed).astype(jnp.bfloat16)
    gv_ref[...] = (ct_ref[...].astype(F32) * mixed).astype(jnp.bfloat16)
    gq_ref[...] = (grad_product * k_ref[...].astype(F32)).astype(jnp.bfloat16)
    gk_ref[...] = (grad_product * q_ref[...].astype(F32)).astype(jnp.bfloat16)


def shape(*dims, dtype=F32):
    return jax.ShapeDtypeStruct(dims, dtype)


def call(kernel, outs, flops, name, vmem=32 * 1024 * 1024, **options):
    return pl.pallas_call(
        kernel,
        out_shape=outs,
        name=name,
        cost_estimate=pl.CostEstimate(flops=flops, bytes_accessed=500_000, transcendentals=0),
        compiler_params=pltpu.CompilerParams(vmem_limit_bytes=vmem),
        **options,
    )


def per_device(queries, key_inputs, value_inputs, skip_gain, residue, timescale, cotangent):
    arrays = (queries, key_inputs, value_inputs, cotangent)
    hbm = pl.BlockSpec(memory_space=pltpu.HBM)
    local = pl.BlockSpec(memory_space=pltpu.VMEM)
    blocks = [pltpu.VMEM((CH, L), jnp.bfloat16)] * 4
    message, table = call(
        local_kernel,
        (shape(NP, ROWS, 128), shape(2, G, R)),
        10**8,
        "local_states",
        vmem=60 * 1024 * 1024,
        in_specs=[hbm] * 6,
        out_specs=(hbm, local),
        scratch_shapes=[
            *blocks,
            pltpu.VMEM((2 * R, CH), F32),
            pltpu.VMEM((4, 8, CH), F32),
            pltpu.VMEM((G, CH), F32),
            pltpu.SemaphoreType.DMA((6,)),
            pltpu.SemaphoreType.DMA((3 * NP,)),
        ],
    )(*arrays, timescale, residue)
    plane_states = lax.all_to_all(message, ("y", "x"), 0, 0, axis_index_groups=plane_groups())
    tables = call(
        conv_kernel,
        (shape(128, 128),) * 4,
        10**8,
        "local_conv",
        in_specs=[hbm] * 5 + [local],
        scratch_shapes=[*blocks, pltpu.VMEM((1, CH), F32), pltpu.SemaphoreType.DMA((5,))],
    )(*arrays, skip_gain.reshape(1, CH), table)
    totals, plane_carry = call(plane_kernel, (shape(NZ, Z_ROWS, 128), shape(3 * R, CH)), 10**7, "plane_scan")(
        plane_states, table
    )
    z_states = lax.all_to_all(totals, ("zh", "z"), 0, 0, axis_index_groups=z_groups())
    params = call(final_kernel, shape(PEERS, 1, 128), 10**7, "z_scan")(z_states, table, plane_carry)
    params = lax.all_to_all(params, ("zh", "z", "y", "core"), 0, 0, axis_index_groups=gather_groups())
    output, grad_queries, grad_keys, grad_values, grad_skip = call(
        output_kernel,
        (*(shape(CH, L, dtype=jnp.bfloat16),) * 4, shape(1, CH)),
        10**8,
        "outputs",
        in_specs=[hbm] * 4 + [local] * 6,
        scratch_shapes=[*blocks, pltpu.SemaphoreType.DMA((4,))],
    )(*arrays, *tables, z_states, plane_carry)
    grad_residue, grad_time = call(gather_kernel, (shape(R, 4 * G),) * 2, 10**6, "gather")(params)
    return (
        output,
        grad_queries,
        grad_keys,
        grad_values,
        grad_skip.reshape(CH),
        grad_residue.T,
        grad_time.T,
    )


def solution(mesh):
    grid = Mesh(mesh.devices.reshape(NZ, 4, 4, 2, 2), ("z", "y", "x", "zh", "core"))
    seq = ("z", "y", "x")
    ch = ("zh", "core")
    return jax.shard_map(
        per_device,
        mesh=grid,
        in_specs=(P(ch, seq), P(ch, seq), P(ch, seq), P(ch), P(ch, None), P(ch, None), P(ch, seq)),
        out_specs=(P(ch, seq), P(ch, seq), P(ch, seq), P(ch, seq), P(ch), P(), P()),
        check_vma=False,
    )
```

time: 63 us -> 57.2 us (0.908)
  blocking collectives: 39.5 us -> 34.3 us
  starting transfers between devices: 6.51 us -> 11.4 us
  waiting for transfers between devices: 5.35 us -> 0.76 us
  Pallas kernels: 9.91 us -> 8.89 us
    all_to_all x2, blocking collectives: 39.5 us -> 34.3 us  [the longest x1 20.7 us: per_device(): lax.all_to_all(totals, ('zh', 'z'), 0, 0, axis_index_groups=z_groups())]
    all_to_all x1, starting transfers between devices: 6.51 us -> 11.4 us  [per_device(): lax.all_to_all(params, ('zh', 'z', 'y', 'core'), 0, 0, axis_index_groups=...]
    all_to_all x1, waiting for transfers between devices: 5.35 us -> 0.76 us  [per_device(): lax.all_to_all(params, ('zh', 'z', 'y', 'core'), 0, 0, axis_index_groups=...]
where the time goes in v3:
time: 57.2 us; the launch traced here: 56.8 us
  blocking collectives  34.3 us (60%)
  starting transfers between devices  11.4 us (20%)
  Pallas kernels  8.89 us (16%)
  waiting for transfers between devices  0.76 us (1%)
  between operations  0.72 us (1%)
  local copies, waits for them, and re-layouts  0.63 us (1%)
    all_to_all x1, blocking collectives, per_device(): lax.all_to_all(totals, ('zh', 'z'), 0, 0, axis_index_groups=z_groups())  20.7 us
    all_to_all x1, blocking collectives, per_device(): lax.all_to_all(message, ('y', 'x'), 0, 0, axis_index_groups=plane_groups())  13.6 us
    all_to_all x1, starting transfers between devices, per_device(): lax.all_to_all(params, ('zh', 'z', 'y', 'core'), 0, 0, axis_index_groups=...  11.4 us
    pallas_call x1, Pallas kernels, per_device(): call(local_kernel, (shape(NP, ROWS, 128), shape(2, G, R)), 10 ** 8, 'loca...  3.58 us
    pallas_call x1, Pallas kernels, per_device(): call(conv_kernel, (shape(128, 128),) * 4, 10 ** 8, 'local_conv', in_specs...  1.73 us
    pallas_call x1, Pallas kernels, per_device(): call(output_kernel, (*(shape(CH, L, dtype=jnp.bfloat16),) * 4, shape(1, C...  1.15 us
    pallas_call x1, Pallas kernels, per_device(): call(final_kernel, shape(PEERS, 1, 128), 10 ** 7, 'z_scan')  1.14 us
  transfers between devices with their start and end apart: 1, of which 1 were waited for; matrix products, arithmetic and copies ran while one was open for 0% of the time, Pallas kernels for 5%

profile of v3, /device:TPU:1, one launch (start us, length us, event | category | flops | bytes accessed | tf_op | source)
XLA Modules:
  0.0 56.8 jit_solution(524581505739085504)
XLA Ops:
  0.6 3.6 %local_states.1 = (f32[16,48,128]{2,1,0:T(8,128)}, f32[2,8,16]{2,1,0:T(8,128)}) custom-call(bf16[128,128]{1,0:T(8,128)(2,1)} %q_hbm.5, bf16[128,128]{1,0:T(8,128)(2,1)} %k_hbm.5, bf16[128,128]{1,0:T(8,128)(2,1)} %v_hbm.5, bf16[128,128]{1,0:T(8,128)(2,1)} %ct_hbm.5, f32[8,16]{1,0:T(8,128)} %tau_hbm.1, f32[8,16]{1,0:T(8,128)} %res_hbm.1), custom_call_target="tpu_custom_call" | custom-call | flops 100000000 | bytes 500000 | tf_op jit(solution)/shard_map/local_states/pallas_call | solution.py:386
  4.2 0.0 copy-start.4
  4.2 13.6 %all_to_all.15.msg_ref = f32[16,48,128]{2,1,0:T(8,128)S(1)} all-to-all(f32[16,48,128]{2,1,0:T(8,128)} %get-tuple-element.27), channel_id=1, replica_groups={{60,0,4,8,12,16,20,24,28,32,36,40,44,48,52,56},{61,1,5,9,13,17,21,25,29..., dimensions={0} | all-to-all | bytes 786432 | tf_op jit(solution)/shard_map/all_to_all | solution.py:403
  17.9 0.0 copy-done.4
  17.9 0.5 plane_scan.1
  18.3 20.7 %all_to_all.16.msg_ref = f32[8,40,128]{2,1,0:T(8,128)S(1)} all-to-all(f32[8,40,128]{2,1,0:T(8,128)S(1)} %get-tuple-element.28), channel_id=1, replica_groups={{448,0,64,128,192,256,320,384},{258,322,386,450,2,66,130,194},{449,1,65..., dimensions={0} | all-to-all | bytes 327680 | tf_op jit(solution)/shard_map/all_to_all | solution.py:415
  39.1 0.0 copy-start
  39.1 0.0 copy-start.1
  39.1 0.0 copy-start.2
  39.1 0.0 copy-start.3
  39.1 1.1 %z_scan.1 = f32[16,1,128]{2,1,0:T(1,128)} custom-call(f32[8,40,128]{2,1,0:T(8,128)S(1)} %all_to_all.16.msg_ref, f32[2,8,16]{2,1,0:T(8,128)S(1)} %copy-done.4, f32[48,128]{1,0:T(8,128)S(1)} %get-tuple-element.29.plane_ref), custom_call_target="tpu_custom_call" | custom-call | flops 10000000 | bytes 500000 | tf_op jit(solution)/shard_map/z_scan/pallas_call | solution.py:416
  40.2 11.4 %all-to-all-start.2 = ((f32[16,1,128]{2,1,0:T(1,128)}), f32[16,1,128]{2,1,0:T(1,128)S(1)}, u32[]{:S(2)}, u32[]{:S(2)}) async-start(f32[16,1,128]{2,1,0:T(1,128)} %z_scan.1), calls=%async_computation.2 | async-start | bytes 16384 | tf_op jit(solution)/shard_map/all_to_all | solution.py:417
  51.6 0.0 copy-start.5
  51.6 0.0 copy-done
  51.7 0.0 copy-done.1
  51.7 0.0 copy-done.2
  51.7 0.0 copy-done.3
  51.7 0.6 %copy-done.5 = f32[128]{0:T(128)S(1)} copy-done((f32[128]{0:T(128)S(1)}, f32[128]{0:T(128)}, u32[]{:S(2)}) %copy-start.5) | copy-done | bytes 536
  52.3 1.7 %local_conv.1 = (f32[128,128]{1,0:T(8,128)S(1)}, f32[128,128]{1,0:T(8,128)S(1)}, f32[128,128]{1,0:T(8,128)S(1)}, f32[128,128]{1,0:T(8,128)S(1)}) custom-call(bf16[128,128]{1,0:T(8,128)(2,1)S(1)} %copy-done, bf16[128,128]{1,0:T(8,128)(2,1)S(1)} %copy-done.1, bf16[128,128]{1,0:T(8,128)(2,1)S(1)} %copy-done.2, bf16[128,128]{1,0:T(8,128)(2,1)S(1)} %copy-done.3, ...), custom_call_target="tpu_custom_call" | custom-call | flops 100000000 | bytes 500000 | tf_op jit(solution)/shard_map/local_conv/pallas_call | solution.py:404
  54.0 1.1 %outputs.1 = (bf16[128,128]{1,0:T(8,128)(2,1)}, bf16[128,128]{1,0:T(8,128)(2,1)}, bf16[128,128]{1,0:T(8,128)(2,1)}, bf16[128,128]{1,0:T(8,128)(2,1)}, f32[1,128]{1,0:T(1,128)}) custom-call(bf16[128,128]{1,0:T(8,128)(2,1)S(1)} %copy-done, bf16[128,128]{1,0:T(8,128)(2,1)S(1)} %copy-done.1, bf16[128,128]{1,0:T(8,128)(2,1)S(1)} %copy-done.2, ...), custom_call_target="tpu_custom_call" | custom-call | flops 100000000 | bytes 500000 | tf_op jit(solution)/shard_map/outputs/pallas_call | solution.py:418
  55.2 0.8 %all-to-all-done.2.part_ref = f32[16,1,128]{2,1,0:T(1,128)S(1)} async-done(((f32[16,1,128]{2,1,0:T(1,128)}), f32[16,1,128]{2,1,0:T(1,128)S(1)}, u32[]{:S(2)}, u32[]{:S(2)}) %all-to-all-start.2) | async-done | bytes 8224 | tf_op jit(solution)/shard_map/all_to_all | solution.py:417
  56.0 0.8 %gather.1 = (f32[16,32]{1,0:T(8,128)}, f32[16,32]{1,0:T(8,128)}) custom-call(f32[16,1,128]{2,1,0:T(1,128)S(1)} %all-to-all-done.2.part_ref), custom_call_target="tpu_custom_call" | custom-call | flops 1000000 | bytes 500000 | tf_op jit(solution)/shard_map/gather/pallas_call | solution.py:426
Async XLA Ops:
  4.2 13.6 %copy-start.4 = (f32[2,8,16]{2,1,0:T(8,128)S(1)}, f32[2,8,16]{2,1,0:T(8,128)}, u32[]{:S(2)}) copy-start(f32[2,8,16]{2,1,0:T(8,128)} %get-tuple-element.22.table_ref) | copy-start | bytes 3076
  39.1 12.6 %copy-start = (bf16[128,128]{1,0:T(8,128)(2,1)S(1)}, bf16[128,128]{1,0:T(8,128)(2,1)}, u32[]{:S(2)}) copy-start(bf16[128,128]{1,0:T(8,128)(2,1)} %q_hbm.5) | copy-start | bytes 98308
  39.1 12.6 %copy-start.1 = (bf16[128,128]{1,0:T(8,128)(2,1)S(1)}, bf16[128,128]{1,0:T(8,128)(2,1)}, u32[]{:S(2)}) copy-start(bf16[128,128]{1,0:T(8,128)(2,1)} %k_hbm.5) | copy-start | bytes 98308
  39.1 12.6 %copy-start.2 = (bf16[128,128]{1,0:T(8,128)(2,1)S(1)}, bf16[128,128]{1,0:T(8,128)(2,1)}, u32[]{:S(2)}) copy-start(bf16[128,128]{1,0:T(8,128)(2,1)} %v_hbm.5) | copy-start | bytes 98308
  39.1 12.6 %copy-start.3 = (bf16[128,128]{1,0:T(8,128)(2,1)S(1)}, bf16[128,128]{1,0:T(8,128)(2,1)}, u32[]{:S(2)}) copy-start(bf16[128,128]{1,0:T(8,128)(2,1)} %ct_hbm.5) | copy-start | bytes 98308
  40.2 15.7 %all-to-all-start.2 = ((f32[16,1,128]{2,1,0:T(1,128)}), f32[16,1,128]{2,1,0:T(1,128)S(1)}, u32[]{:S(2)}, u32[]{:S(2)}) async-start(f32[16,1,128]{2,1,0:T(1,128)} %z_scan.1), calls=%async_computation.2 | async-start | bytes 16384 | tf_op jit(solution)/shard_map/all_to_all | solution.py:417
  51.6 0.7 %copy-start.5 = (f32[128]{0:T(128)S(1)}, f32[128]{0:T(128)}, u32[]{:S(2)}) copy-start(f32[128]{0:T(128)} %param.10) | copy-start | bytes 1540

commit v4 on v3

--- a/solution.py
+++ b/solution.py
@@ -15,15 +15,15 @@
 R = 16
 M = 16
 MOMENT_ROW = 2 * R
-SUM_ROW = MOMENT_ROW + R // 2
+SUM_ROW = MOMENT_ROW + R
 ROWS = SUM_ROW + G
 NP = 16
 NZ = 8
-SHARE = CH // 4
-Z_ROWS = 2 * R + G
-PEERS = 16
+SHARE = CH // 2
+Z_ROWS = 3 * R
+PEERS = 8
 PLANE_FIRST = 15
-Z_FIRST = (7, 4)
+Z_FIRST = (7, 3)
 
 
 def dot(a, b, ca=1, cb=0):
@@ -88,10 +88,12 @@
     return jnp.where(same_group(), jnp.concatenate([state] * G, axis=0), 0.0)
 
 
-def group_sums(h0, h1):
-    pick = ones_where(iota((G, CH), 1) // M == iota((G, CH), 0))
-    rows = jnp.concatenate([h0, h1, jnp.zeros((CH - 2 * R, CH), F32)], axis=0)
-    return pick_dot(pick, rows, 1, 1)
+def front_sums(h0, h1, half):
+    lane = iota((G, CH), 1)
+    pick = ones_where((lane // M + half * (SHARE // M) == iota((G, CH), 0)) & (lane < SHARE))
+    front = iota((R, CH), 1) < SHARE
+    rows = [jnp.where(front, h0, 0.0), jnp.where(front, h1, 0.0), jnp.zeros((CH - 2 * R, CH), F32)]
+    return pick_dot(pick, jnp.concatenate(rows, axis=0), 1, 1)
 
 
 def fetch(pairs, sems):
@@ -102,24 +104,28 @@
         copy.wait()
 
 
+def side_by_side(a, b, half):
+    a, b = (a, pltpu.roll(b, SHARE, 1)) if half == 0 else (pltpu.roll(a, SHARE, 1), b)
+    return jnp.where(iota((R, CH), 1) < SHARE, a, b)
+
+
 def local_kernel(
-    q_hbm, k_hbm, v_hbm, ct_hbm, tau_hbm, res_hbm, msg_hbm, table_ref,
-    q_ref, k_ref, v_ref, ct_ref, states_ref, packed_ref, sums_ref, sems, out_sems,
+    q_hbm, k_hbm, v_hbm, ct_hbm, tau_hbm, msg_hbm,
+    q_ref, k_ref, v_ref, ct_ref, tau_ref, states_ref, packed_ref, sums_ref, sems, out_sems,
 ):
     fetch(
         (
-            (tau_hbm, table_ref.at[0]),
+            (tau_hbm, tau_ref),
             (q_hbm, q_ref),
             (k_hbm, k_ref),
             (v_hbm, v_ref),
             (ct_hbm, ct_ref),
-            (res_hbm, table_ref.at[1]),
         ),
         sems,
     )
     product = q_ref[...].astype(F32) * k_ref[...].astype(F32)
     grad_mixed = ct_ref[...].astype(F32) * v_ref[...].astype(F32)
-    rate = by_group_mode(1.0 / table_ref[0])
+    rate = by_group_mode(1.0 / tau_ref[...])
     lane = iota((128, 128), 1)
     row = iota((128, 128), 0)
     step = lane.astype(F32)
@@ -139,14 +145,10 @@
     for i in range(NP):
         send(states_ref, i, slice(0, MOMENT_ROW))
     moments = (fold_states(fwd[128:]), fold_states(bwd[128:]))
-    quarters = (moments[0][:8], moments[0][8:], moments[1][:8], moments[1][8:])
-    for y in range(4):
-        packed = jnp.zeros((8, CH), F32)
-        for k, quarter in enumerate(quarters):
-            packed = jnp.where(lane[:8] // SHARE == k, pltpu.roll(quarter, (k - y) % 4 * SHARE, 1), packed)
-        packed_ref[y] = packed
+    for half in range(2):
+        packed_ref[half] = side_by_side(*moments, half)
     for i in range(NP):
-        send(packed_ref.at[i // 4], i, slice(MOMENT_ROW, SUM_ROW))
+        send(packed_ref.at[i // 4 % 2], i, slice(MOMENT_ROW, SUM_ROW))
     flipped = pick_dot_right(product, ones_where(lane + row == L - 1))
     inside = lane + row >= L - 1
     lags = []
@@ -172,14 +174,15 @@
 
 
 def conv_kernel(
-    q_hbm, k_hbm, v_hbm, ct_hbm, skip_hbm, table_ref, fwd_ref, bwd_ref, head_ref, tail_ref, q_ref, k_ref, v_ref, ct_ref, skip_ref, sems
+    q_hbm, k_hbm, v_hbm, ct_hbm, skip_hbm, tau_ref, res_ref, fwd_ref, bwd_ref, head_ref, tail_ref, rate_ref, q_ref, k_ref, v_ref, ct_ref, skip_ref, sems
 ):
     fetch(((q_hbm, q_ref), (k_hbm, k_ref), (v_hbm, v_ref), (ct_hbm, ct_ref), (skip_hbm, skip_ref)), sems)
     product = q_ref[...].astype(F32) * k_ref[...].astype(F32)
     grad_mixed = ct_ref[...].astype(F32) * v_ref[...].astype(F32)
-    inv = 1.0 / table_ref[0]
+    inv = 1.0 / tau_ref[...]
+    rate_ref[...] = by_mode_and_channel(inv)
     rate = by_group_mode(inv)
-    gain = by_group_mode(table_ref[1] * jnp.sqrt(2.0 * inv) * (1.0 / math.sqrt(R)))
+    gain = by_group_mode(res_ref[...] * jnp.sqrt(2.0 * inv) * (1.0 / math.sqrt(R)))
     lane = iota((128, 128), 1)
     row = iota((128, 128), 0)
     step = lane.astype(F32)
@@ -200,93 +203,89 @@
     return lax.axis_index("y") * 4 + lax.axis_index("x")
 
 
-def plane_kernel(msg_ref, table_ref, out_ref, carry_ref):
-    rate = by_mode_and_channel(1.0 / table_ref[0])
+def to_front(state, half):
+    return pltpu.roll(state, half * SHARE, 1)
+
+
+def plane_kernel(msg_ref, rate_ref, out_ref, carry_ref):
+    rate = rate_ref[...]
     me = plane_index()
-    y = lax.axis_index("y")
+    half = lax.rem(lax.axis_index("y"), 2)
     span = jnp.float32(L)
     decay = jnp.exp(-span * rate)
     zero = jnp.zeros((R, CH), F32)
-
-    def moments(i):
-        packed = msg_ref[plane_slot(i), MOMENT_ROW:SUM_ROW]
-        moved = [pltpu.roll(packed, lax.rem(y + 4 - k, 4) * SHARE, 1) for k in range(4)]
-        return jnp.concatenate(moved[:2], axis=0), jnp.concatenate(moved[2:], axis=0)
-
-    f, f1, h0, h1, own_f = zero, zero, zero, zero, zero
+    front_decay = to_front(decay, half)
+    f, g, f1, h0, h1, own_f = zero, zero, zero, zero, zero, zero
     sums = jnp.zeros((G, 128), F32)
-    back_moments = []
+    fronts = []
     for i in range(NP):
+        at = plane_slot(i)
         own_f = jnp.where(me == i, f, own_f)
-        fwd, bwd = msg_ref[plane_slot(i), :R], msg_ref[plane_slot(i), R : 2 * R]
-        fwd1, bwd1 = moments(i)
-        back_moments.append(bwd1)
-        h0 = h0 + f * bwd
-        h1 = h1 + f * bwd1 + f1 * bwd
-        f1 = decay * (f1 + span * f) + fwd1
+        fwd, fwd1 = msg_ref[at, :R], msg_ref[at, MOMENT_ROW:SUM_ROW]
+        bwd, bwd1 = to_front(msg_ref[at, R : 2 * R], half), pltpu.roll(fwd1, SHARE, 1)
+        fronts.append((bwd, bwd1))
+        h0 = h0 + g * bwd
+        h1 = h1 + g * bwd1 + f1 * bwd
+        f1 = front_decay * (f1 + span * g) + fwd1
+        g = front_decay * g + to_front(fwd, half)
         f = decay * f + fwd
-        sums = sums + msg_ref[plane_slot(i), SUM_ROW:]
-    b, b1, own_b = zero, zero, zero
+        sums = sums + msg_ref[at, SUM_ROW:]
+    b, e, b1, own_b = zero, zero, zero, zero
     for i in reversed(range(NP)):
+        bwd, bwd1 = fronts[i]
         own_b = jnp.where(me == i, b, own_b)
-        b1 = decay * (b1 + span * b) + back_moments[i]
+        b1 = front_decay * (b1 + span * e) + bwd1
+        e = front_decay * e + bwd
         b = decay * b + msg_ref[plane_slot(i), R : 2 * R]
     carry_ref[:R] = own_f
     carry_ref[R : 2 * R] = own_b
-    carry_ref[2 * R :] = rate
-    mine = iota((R, CH), 1) // SHARE == y
-    sums = sums + group_sums(jnp.where(mine, h0, 0.0), jnp.where(mine, h1, 0.0))
-    share = share_of(f, b, f1, b1)
+    sums = sums + front_sums(h0, h1, half)
+    front = iota((R, CH), 1) < SHARE
+    f1 = pltpu.roll(f1, SHARE, 1)
+    sums = jnp.concatenate([pltpu.roll(sums, SHARE, 1), jnp.zeros((R - G, CH), F32)], axis=0)
+    last = jnp.where(front, b1, sums)
     z = lax.axis_index("z")
     for i in range(NZ):
-        out_ref[z_slot(i), :R] = jnp.where(z < i, f, b)
-        out_ref[z_slot(i), R : 2 * R] = share
-        out_ref[z_slot(i), 2 * R :] = sums
-
-
-def share_of(f, b, f1, b1):
-    start = lax.axis_index("y") * SHARE
-    lane = iota((R, CH), 1)
-    out = jnp.zeros((R, CH), F32)
-    for k, state in enumerate((f, b, f1, b1)):
-        moved = pltpu.roll(state, lax.rem(k * SHARE + CH - start, CH), 1)
-        out = jnp.where(lane // SHARE == k, moved, out)
-    return out
-
-
-def final_kernel(msg_ref, table_ref, plane_ref, param_ref):
-    inv = 1.0 / table_ref[0]
-    y = lax.axis_index("y")
+        above = z < i
+        out_ref[z_slot(i), :R] = jnp.where(above, f, b)
+        out_ref[z_slot(i), R : 2 * R] = jnp.where(front, jnp.where(above, e, g), f1)
+        out_ref[z_slot(i), 2 * R :] = last
+
+
+def final_kernel(msg_ref, tau_ref, res_ref, rate_ref, param_ref):
+    inv = 1.0 / tau_ref[...]
+    half = lax.rem(lax.axis_index("y"), 2)
+    z = lax.axis_index("z")
     span = jnp.float32(L * NP)
-    decay = jnp.exp(-span * pltpu.roll(plane_ref[2 * R :], lax.rem(CH - y * SHARE, CH), 1))
+    decay = jnp.exp(-span * to_front(rate_ref[...], half))
     zero = jnp.zeros((R, CH), F32)
     f, f1, h0, h1 = zero, zero, zero, zero
     sums = jnp.zeros((G, 128), F32)
     for i in range(NZ):
-        part = msg_ref[z_slot(i), R : 2 * R]
-        back = pltpu.roll(part, CH - SHARE, 1)
-        f1_part = pltpu.roll(part, CH - 2 * SHARE, 1)
-        b1_part = pltpu.roll(part, CH - 3 * SHARE, 1)
-        h0 = h0 + f * back
-        h1 = h1 + f * b1_part + f1 * back
-        f1 = decay * (f1 + span * f) + f1_part
-        f = decay * f + part
-        sums = sums + msg_ref[z_slot(i), 2 * R :]
-    pick = ones_where(iota((G, CH), 1) // M + y * (SHARE // M) == iota((G, CH), 0)) * ones_where(iota((G, CH), 1) < SHARE)
-    mine = iota((R, CH), 1) < SHARE
-    pairs = jnp.concatenate([jnp.where(mine, h0, 0.0), jnp.where(mine, h1, 0.0)], axis=0)
-    whole = pick_dot(pick, pairs, 1, 1) + sums[:, : 2 * R]
+        at = z_slot(i)
+        carry = to_front(msg_ref[at, :R], half)
+        part = msg_ref[at, R : 2 * R]
+        fwd, bwd = jnp.where(i < z, carry, part), jnp.where(i < z, part, carry)
+        bwd1 = msg_ref[at, 2 * R :]
+        h0 = h0 + f * bwd
+        h1 = h1 + f * bwd1 + f1 * bwd
+        f1 = decay * (f1 + span * f) + pltpu.roll(part, SHARE, 1)
+        f = decay * f + fwd
+        sums = sums + msg_ref[at, 2 * R : 2 * R + G]
+    whole = front_sums(h0, h1, half) + pltpu.roll(sums, SHARE, 1)
     scale = 1.0 / math.sqrt(L * NP * NZ * M)
-    h0, h1 = whole[:, :R], whole[:, R:]
+    h0, h1 = whole[:, :R], whole[:, R : 2 * R]
     root = jnp.sqrt(2.0 * inv) * (scale / math.sqrt(R))
     params = jnp.concatenate(
-        [h0 * root, table_ref[1] * root * (h1 * inv - 0.5 * h0), jnp.zeros((G, 128 - 2 * R), F32)], axis=1
-    )
-    group = iota((G, 128), 0) - 2 * y
-    params = jnp.where(group == 0, params, 0.0) + jnp.where(group == 1, pltpu.roll(params, 2 * R, 1), 0.0)
-    params = jnp.sum(params, axis=0, keepdims=True)
+        [h0 * root, res_ref[...] * root * (h1 * inv - 0.5 * h0), jnp.zeros((G, 128 - 2 * R), F32)], axis=1
+    )
+    group = iota((G, 128), 0) - half * (G // 2)
+    row = jnp.where(group == 0, params, 0.0)
+    for k in range(1, G // 2):
+        row = row + jnp.where(group == k, pltpu.roll(params, 2 * R * k, 1), 0.0)
+    row = jnp.sum(row, axis=0, keepdims=True)
     for i in range(PEERS):
-        param_ref[i] = params
+        param_ref[i] = row
 
 
 def gather_kernel(part_ref, residue_ref, time_ref):
@@ -294,13 +293,13 @@
     columns = jnp.concatenate([rows, jnp.zeros((128 - PEERS, 128), F32)], axis=0).T
     peer = iota((128, 4 * G), 0)
     group = iota((128, 4 * G), 1)
-    y, core, zh = peer % 4, peer // 4 % 2, 1 - peer // 8
-    first = (zh * 2 + core) * G + 2 * y
+    half, core, zh = 1 - peer % 2, peer // 2 % 2, 1 - peer // 4
+    first = (zh * 2 + core) * G + half * (G // 2)
     out = jnp.zeros((2 * R, 4 * G), F32)
-    for b in range(2):
-        place = ones_where((group == first + b) & (peer < PEERS)).astype(jnp.bfloat16)
-        for half in halves(columns[2 * R * b : 2 * R * (b + 1)]):
-            out = out + lax.dot_general(half, place, (((1,), (0,)), ((), ())), preferred_element_type=F32)
+    for k in range(G // 2):
+        place = ones_where((group == first + k) & (peer < PEERS)).astype(jnp.bfloat16)
+        for part in halves(columns[2 * R * k : 2 * R * (k + 1)]):
+            out = out + lax.dot_general(part, place, (((1,), (0,)), ((), ())), preferred_element_type=F32)
     residue_ref[...] = out[:R]
     time_ref[...] = out[R:]
 
@@ -327,16 +326,17 @@
     index = lambda zh, z, y, core: ((zh * NZ + z) * 4 + y) * 2 + core
     for z in range(NZ):
         planes = {0: z, 1: (z + 4) % NZ}
-        groups.append([index(zh, planes[zh], y, core) for zh in (1, 0) for core in range(2) for y in range(4)])
+        for pair in (0, 2):
+            groups.append([index(zh, planes[zh], pair + half, core) for zh in (1, 0) for core in (0, 1) for half in (1, 0)])
     return groups
 
 
 def output_kernel(
-    q_hbm, k_hbm, v_hbm, ct_hbm, fwd_ref, bwd_ref, head_ref, tail_ref, msg_ref, plane_ref,
+    q_hbm, k_hbm, v_hbm, ct_hbm, fwd_ref, bwd_ref, head_ref, tail_ref, msg_ref, plane_ref, rate_ref,
     out_ref, gq_ref, gk_ref, gv_ref, skip_ref, q_ref, k_ref, v_ref, ct_ref, sems,
 ):
     fetch(((q_hbm, q_ref), (k_hbm, k_ref), (v_hbm, v_ref), (ct_hbm, ct_ref)), sems)
-    rate = plane_ref[2 * R :]
+    rate = rate_ref[...]
     z = lax.axis_index("z")
     me = plane_index().astype(F32)
     decay = jnp.exp(-jnp.float32(L * NP) * rate)
@@ -345,14 +345,14 @@
     sums = jnp.zeros((G, 128), F32)
     for i in range(NZ):
         own_f = jnp.where(i < z, decay * own_f + msg_ref[z_slot(i), :R], own_f)
-        sums = sums + msg_ref[z_slot(i), 2 * R :]
+        sums = sums + msg_ref[z_slot(i), 2 * R : 2 * R + G]
     for i in reversed(range(NZ)):
         own_b = jnp.where(i > z, decay * own_b + msg_ref[z_slot(i), :R], own_b)
     own_f = plane_ref[:R] + jnp.exp(-(L * me) * rate) * own_f
     own_b = plane_ref[R : 2 * R] + jnp.exp(-(L * (NP - 1 - me)) * rate) * own_b
     lane = iota((128, 128), 1)
     row = iota((128, 128), 0)
-    spread = dot(sums, ones_where((row - 2 * R == lane % M) & (row >= 2 * R) & (row < 3 * R)))
+    spread = dot(sums, ones_where((row - 2 * R - SHARE == lane % M) & (row >= 2 * R + SHARE) & (row < 3 * R + SHARE)))
     spread = jnp.where(iota((G, CH), 1) // M == iota((G, CH), 0), spread, 0.0)
     skip_ref[...] = jnp.sum(spread, axis=0, keepdims=True) * (1.0 / math.sqrt(L * NP * NZ))
     mixed = fwd_ref[...] + dot3(spread_states(own_f), head_ref[...], 0, 0)
@@ -383,46 +383,47 @@
     hbm = pl.BlockSpec(memory_space=pltpu.HBM)
     local = pl.BlockSpec(memory_space=pltpu.VMEM)
     blocks = [pltpu.VMEM((CH, L), jnp.bfloat16)] * 4
-    message, table = call(
+    message = call(
         local_kernel,
-        (shape(NP, ROWS, 128), shape(2, G, R)),
+        shape(NP, ROWS, 128),
         10**8,
         "local_states",
         vmem=60 * 1024 * 1024,
-        in_specs=[hbm] * 6,
-        out_specs=(hbm, local),
+        in_specs=[hbm] * 5,
+        out_specs=hbm,
         scratch_shapes=[
             *blocks,
+            pltpu.VMEM((G, R), F32),
             pltpu.VMEM((2 * R, CH), F32),
-            pltpu.VMEM((4, 8, CH), F32),
+            pltpu.VMEM((2, R, CH), F32),
             pltpu.VMEM((G, CH), F32),
-            pltpu.SemaphoreType.DMA((6,)),
+            pltpu.SemaphoreType.DMA((5,)),
             pltpu.SemaphoreType.DMA((3 * NP,)),
         ],
-    )(*arrays, timescale, residue)
+    )(*arrays, timescale)
     plane_states = lax.all_to_all(message, ("y", "x"), 0, 0, axis_index_groups=plane_groups())
-    tables = call(
+    *tables, rate = call(
         conv_kernel,
-        (shape(128, 128),) * 4,
+        (*(shape(128, 128),) * 4, shape(R, CH)),
         10**8,
         "local_conv",
-        in_specs=[hbm] * 5 + [local],
+        in_specs=[hbm] * 5 + [local] * 2,
         scratch_shapes=[*blocks, pltpu.VMEM((1, CH), F32), pltpu.SemaphoreType.DMA((5,))],
-    )(*arrays, skip_gain.reshape(1, CH), table)
-    totals, plane_carry = call(plane_kernel, (shape(NZ, Z_ROWS, 128), shape(3 * R, CH)), 10**7, "plane_scan")(
-        plane_states, table
+    )(*arrays, skip_gain.reshape(1, CH), timescale, residue)
+    totals, plane_carry = call(plane_kernel, (shape(NZ, Z_ROWS, 128), shape(2 * R, CH)), 10**7, "plane_scan")(
+        plane_states, rate
     )
     z_states = lax.all_to_all(totals, ("zh", "z"), 0, 0, axis_index_groups=z_groups())
-    params = call(final_kernel, shape(PEERS, 1, 128), 10**7, "z_scan")(z_states, table, plane_carry)
+    params = call(final_kernel, shape(PEERS, 1, 128), 10**7, "z_scan")(z_states, timescale, residue, rate)
     params = lax.all_to_all(params, ("zh", "z", "y", "core"), 0, 0, axis_index_groups=gather_groups())
     output, grad_queries, grad_keys, grad_values, grad_skip = call(
         output_kernel,
         (*(shape(CH, L, dtype=jnp.bfloat16),) * 4, shape(1, CH)),
         10**8,
         "outputs",
-        in_specs=[hbm] * 4 + [local] * 6,
+        in_specs=[hbm] * 4 + [local] * 7,
         scratch_shapes=[*blocks, pltpu.SemaphoreType.DMA((4,))],
-    )(*arrays, *tables, z_states, plane_carry)
+    )(*arrays, *tables, z_states, plane_carry, rate)
     grad_residue, grad_time = call(gather_kernel, (shape(R, 4 * G),) * 2, 10**6, "gather")(params)
     return (
         output,

time: 57.2 us -> 55.5 us (0.970)
  blocking collectives: 34.3 us -> 21.6 us
  starting transfers between devices: 11.4 us -> 20.6 us
  waiting for transfers between devices: 0.76 us -> 3.19 us
  Pallas kernels: 8.89 us -> 8.27 us
    all_to_all x1 -> x0, blocking collectives: 13.6 us -> none  [per_device(): lax.all_to_all(message, ('y', 'x'), 0, 0, axis_index_groups=plane_groups())]
    all_to_all x0 -> x1, starting transfers between devices: none -> 9.25 us  [per_device(): lax.all_to_all(message, ('y', 'x'), 0, 0, axis_index_groups=plane_groups())]
    all_to_all x0 -> x1, waiting for transfers between devices: none -> 2.47 us  [per_device(): lax.all_to_all(message, ('y', 'x'), 0, 0, axis_index_groups=plane_groups())]
    all_to_all x1, blocking collectives: 20.7 us -> 21.6 us  [per_device(): lax.all_to_all(totals, ('zh', 'z'), 0, 0, axis_index_groups=z_groups())]
    pallas_call x3, Pallas kernels: 5.78 us -> 5.14 us  [the longest x1 2.97 us: per_device(): call(local_kernel, shape(NP, ROWS, 128), 10 ** 8, 'local_states', vmem=60...]
  transfers between devices with their start and end apart: 1 -> 2, of which waited for: 1 -> 2; matrix products, arithmetic and copies ran while one was open for 0% -> 0% of each run, Pallas kernels for 5% -> 5%
where the time goes in v4:
time: 55.5 us; the launch traced here: 55.1 us
  blocking collectives  21.6 us (39%)
  starting transfers between devices  20.6 us (37%)
  Pallas kernels  8.27 us (15%)
  waiting for transfers between devices  3.19 us (6%)
  between operations  0.77 us (1%)
  local copies, waits for them, and re-layouts  0.63 us (1%)
    all_to_all x1, blocking collectives, per_device(): lax.all_to_all(totals, ('zh', 'z'), 0, 0, axis_index_groups=z_groups())  21.6 us
    all_to_all x1, starting transfers between devices, per_device(): lax.all_to_all(params, ('zh', 'z', 'y', 'core'), 0, 0, axis_index_groups=...  11.4 us
    all_to_all x1, starting transfers between devices, per_device(): lax.all_to_all(message, ('y', 'x'), 0, 0, axis_index_groups=plane_groups())  9.25 us
    pallas_call x1, Pallas kernels, per_device(): call(local_kernel, shape(NP, ROWS, 128), 10 ** 8, 'local_states', vmem=60...  2.97 us
    all_to_all x1, waiting for transfers between devices, per_device(): lax.all_to_all(message, ('y', 'x'), 0, 0, axis_index_groups=plane_groups())  2.47 us
    pallas_call x1, Pallas kernels, per_device(): call(conv_kernel, (*(shape(128, 128),) * 4, shape(R, CH)), 10 ** 8, 'loca...  1.76 us
    pallas_call x1, Pallas kernels, per_device(): call(output_kernel, (*(shape(CH, L, dtype=jnp.bfloat16),) * 4, shape(1, C...  1.15 us
    pallas_call x1, Pallas kernels, per_device(): call(final_kernel, shape(PEERS, 1, 128), 10 ** 7, 'z_scan')  1.14 us
  transfers between devices with their start and end apart: 2, of which 2 were waited for; matrix products, arithmetic and copies ran while one was open for 0% of the time, Pallas kernels for 5%

profile of v4, /device:TPU:1, one launch (start us, length us, event | category | flops | bytes accessed | tf_op | source)
XLA Modules:
  0.0 55.1 jit_solution(5578212063646211344)
XLA Ops:
  0.6 3.0 %local_states.1 = f32[16,56,128]{2,1,0:T(8,128)} custom-call(bf16[128,128]{1,0:T(8,128)(2,1)} %q_hbm.5, bf16[128,128]{1,0:T(8,128)(2,1)} %k_hbm.5, bf16[128,128]{1,0:T(8,128)(2,1)} %v_hbm.5, bf16[128,128]{1,0:T(8,128)(2,1)} %ct_hbm.5, f32[8,16]{1,0:T(8,128)} %tau_ref.3), custom_call_target="tpu_custom_call" | custom-call | flops 100000000 | bytes 500000 | tf_op jit(solution)/shard_map/local_states/pallas_call | solution.py:386
  3.6 0.0 copy-start
  3.6 0.0 copy-start.1
  3.6 0.0 copy-start.2
  3.6 0.0 copy-start.3
  3.7 0.0 copy-start.4
  3.7 0.0 copy-start.5
  3.7 9.3 %all-to-all-start = ((f32[16,56,128]{2,1,0:T(8,128)}), f32[16,56,128]{2,1,0:T(8,128)S(1)}, u32[]{:S(2)}, u32[]{:S(2)}) async-start(f32[16,56,128]{2,1,0:T(8,128)} %local_states.1), calls=%async_computation | async-start | bytes 917504 | tf_op jit(solution)/shard_map/all_to_all | solution.py:404
  12.9 0.0 copy-done
  13.0 0.0 copy-done.1
  13.0 0.0 copy-done.2
  13.0 0.0 copy-done.3
  13.0 0.0 copy-done.4
  13.0 0.0 copy-done.5
  13.0 0.6 %copy-done.6 = f32[128]{0:T(128)S(1)} copy-done((f32[128]{0:T(128)S(1)}, f32[128]{0:T(128)}, u32[]{:S(2)}) %copy-start.6) | copy-done | bytes 536
  13.6 1.8 %local_conv.1 = (f32[128,128]{1,0:T(8,128)S(1)}, f32[128,128]{1,0:T(8,128)S(1)}, f32[128,128]{1,0:T(8,128)S(1)}, f32[128,128]{1,0:T(8,128)S(1)}, f32[16,128]{1,0:T(8,128)S(1)}) custom-call(bf16[128,128]{1,0:T(8,128)(2,1)S(1)} %copy-done, bf16[128,128]{1,0:T(8,128)(2,1)S(1)} %copy-done.1, bf16[128,128]{1,0:T(8,128)(2,1)S(1)} %copy-done.2, ...), custom_call_target="tpu_custom_call" | custom-call | flops 100000000 | bytes 500000 | tf_op jit(solution)/shard_map/local_conv/pallas_call | solution.py:405
  15.4 2.5 %all-to-all-done.msg_ref = f32[16,56,128]{2,1,0:T(8,128)S(1)} async-done(((f32[16,56,128]{2,1,0:T(8,128)}), f32[16,56,128]{2,1,0:T(8,128)S(1)}, u32[]{:S(2)}, u32[]{:S(2)}) %all-to-all-start) | async-done | bytes 458784 | tf_op jit(solution)/shard_map/all_to_all | solution.py:404
  17.8 0.4 plane_scan.1
  18.2 21.6 %all_to_all.15.msg_ref = f32[8,48,128]{2,1,0:T(8,128)S(1)} all-to-all(f32[8,48,128]{2,1,0:T(8,128)S(1)} %get-tuple-element.26), channel_id=1, replica_groups={{448,0,64,128,192,256,320,384},{194,258,322,386,450,2,66,130},{449,1,65..., dimensions={0} | all-to-all | bytes 393216 | tf_op jit(solution)/shard_map/all_to_all | solution.py:416
  39.8 1.1 %z_scan.1 = f32[8,1,128]{2,1,0:T(1,128)} custom-call(f32[8,48,128]{2,1,0:T(8,128)S(1)} %all_to_all.15.msg_ref, f32[8,16]{1,0:T(8,128)S(1)} %copy-done.4, f32[8,16]{1,0:T(8,128)S(1)} %copy-done.5, f32[16,128]{1,0:T(8,128)S(1)} %get-tuple-element.25.rate_ref), custom_call_target="tpu_custom_call" | custom-call | flops 10000000 | bytes 500000 | tf_op jit(solution)/shard_map/z_scan/pallas_call | solution.py:417
  41.0 11.4 %all-to-all-start.2 = ((f32[8,1,128]{2,1,0:T(1,128)}), f32[8,1,128]{2,1,0:T(1,128)S(1)}, u32[]{:S(2)}, u32[]{:S(2)}) async-start(f32[8,1,128]{2,1,0:T(1,128)} %z_scan.1), calls=%async_computation.2 | async-start | bytes 8192 | tf_op jit(solution)/shard_map/all_to_all | solution.py:418
  52.4 1.2 %outputs.1 = (bf16[128,128]{1,0:T(8,128)(2,1)}, bf16[128,128]{1,0:T(8,128)(2,1)}, bf16[128,128]{1,0:T(8,128)(2,1)}, bf16[128,128]{1,0:T(8,128)(2,1)}, f32[1,128]{1,0:T(1,128)}) custom-call(bf16[128,128]{1,0:T(8,128)(2,1)S(1)} %copy-done, bf16[128,128]{1,0:T(8,128)(2,1)S(1)} %copy-done.1, bf16[128,128]{1,0:T(8,128)(2,1)S(1)} %copy-done.2, ...), custom_call_target="tpu_custom_call" | custom-call | flops 100000000 | bytes 500000 | tf_op jit(solution)/shard_map/outputs/pallas_call | solution.py:419
  53.5 0.7 %all-to-all-done.2.part_ref = f32[8,1,128]{2,1,0:T(1,128)S(1)} async-done(((f32[8,1,128]{2,1,0:T(1,128)}), f32[8,1,128]{2,1,0:T(1,128)S(1)}, u32[]{:S(2)}, u32[]{:S(2)}) %all-to-all-start.2) | async-done | bytes 4128 | tf_op jit(solution)/shard_map/all_to_all | solution.py:418
  54.3 0.8 %gather.1 = (f32[16,32]{1,0:T(8,128)}, f32[16,32]{1,0:T(8,128)}) custom-call(f32[8,1,128]{2,1,0:T(1,128)S(1)} %all-to-all-done.2.part_ref), custom_call_target="tpu_custom_call" | custom-call | flops 1000000 | bytes 500000 | tf_op jit(solution)/shard_map/gather/pallas_call | solution.py:427
  (1 shorter events, 0.0 us)
Async XLA Ops:
  3.6 9.3 %copy-start = (bf16[128,128]{1,0:T(8,128)(2,1)S(1)}, bf16[128,128]{1,0:T(8,128)(2,1)}, u32[]{:S(2)}) copy-start(bf16[128,128]{1,0:T(8,128)(2,1)} %q_hbm.5) | copy-start | bytes 98308
  3.6 9.3 %copy-start.1 = (bf16[128,128]{1,0:T(8,128)(2,1)S(1)}, bf16[128,128]{1,0:T(8,128)(2,1)}, u32[]{:S(2)}) copy-start(bf16[128,128]{1,0:T(8,128)(2,1)} %k_hbm.5) | copy-start | bytes 98308
  3.6 9.3 %copy-start.2 = (bf16[128,128]{1,0:T(8,128)(2,1)S(1)}, bf16[128,128]{1,0:T(8,128)(2,1)}, u32[]{:S(2)}) copy-start(bf16[128,128]{1,0:T(8,128)(2,1)} %v_hbm.5) | copy-start | bytes 98308
  3.6 9.3 %copy-start.3 = (bf16[128,128]{1,0:T(8,128)(2,1)S(1)}, bf16[128,128]{1,0:T(8,128)(2,1)}, u32[]{:S(2)}) copy-start(bf16[128,128]{1,0:T(8,128)(2,1)} %ct_hbm.5) | copy-start | bytes 98308
  3.7 9.3 %copy-start.4 = (f32[8,16]{1,0:T(8,128)S(1)}, f32[8,16]{1,0:T(8,128)}, u32[]{:S(2)}) copy-start(f32[8,16]{1,0:T(8,128)} %tau_ref.3) | copy-start | bytes 1540
  3.7 9.3 %copy-start.5 = (f32[8,16]{1,0:T(8,128)S(1)}, f32[8,16]{1,0:T(8,128)}, u32[]{:S(2)}) copy-start(f32[8,16]{1,0:T(8,128)} %res_ref.3) | copy-start | bytes 1540
  3.7 14.1 %all-to-all-start = ((f32[16,56,128]{2,1,0:T(8,128)}), f32[16,56,128]{2,1,0:T(8,128)S(1)}, u32[]{:S(2)}, u32[]{:S(2)}) async-start(f32[16,56,128]{2,1,0:T(8,128)} %local_states.1), calls=%async_computation | async-start | bytes 917504 | tf_op jit(solution)/shard_map/all_to_all | solution.py:404
  12.9 0.7 %copy-start.6 = (f32[128]{0:T(128)S(1)}, f32[128]{0:T(128)}, u32[]{:S(2)}) copy-start(f32[128]{0:T(128)} %param.10) | copy-start | bytes 1540
  41.0 13.3 %all-to-all-start.2 = ((f32[8,1,128]{2,1,0:T(1,128)}), f32[8,1,128]{2,1,0:T(1,128)S(1)}, u32[]{:S(2)}, u32[]{:S(2)}) async-start(f32[8,1,128]{2,1,0:T(1,128)} %z_scan.1), calls=%async_computation.2 | async-start | bytes 8192 | tf_op jit(solution)/shard_map/all_to_all | solution.py:418

commit v5 on v4

--- a/solution.py
+++ b/solution.py
@@ -15,13 +15,13 @@
 R = 16
 M = 16
 MOMENT_ROW = 2 * R
-SUM_ROW = MOMENT_ROW + R
+SUM_ROW = MOMENT_ROW + R // 2
 ROWS = SUM_ROW + G
 NP = 16
 NZ = 8
-SHARE = CH // 2
-Z_ROWS = 3 * R
-PEERS = 8
+SHARE = CH // 4
+Z_ROWS = 2 * R
+PEERS = 16
 PLANE_FIRST = 15
 Z_FIRST = (7, 3)
 
@@ -88,9 +88,9 @@
     return jnp.where(same_group(), jnp.concatenate([state] * G, axis=0), 0.0)
 
 
-def front_sums(h0, h1, half):
+def front_sums(h0, h1, quarter):
     lane = iota((G, CH), 1)
-    pick = ones_where((lane // M + half * (SHARE // M) == iota((G, CH), 0)) & (lane < SHARE))
+    pick = ones_where((lane // M + quarter * (SHARE // M) == iota((G, CH), 0)) & (lane < SHARE))
     front = iota((R, CH), 1) < SHARE
     rows = [jnp.where(front, h0, 0.0), jnp.where(front, h1, 0.0), jnp.zeros((CH - 2 * R, CH), F32)]
     return pick_dot(pick, jnp.concatenate(rows, axis=0), 1, 1)
@@ -104,9 +104,20 @@
         copy.wait()
 
 
-def side_by_side(a, b, half):
-    a, b = (a, pltpu.roll(b, SHARE, 1)) if half == 0 else (pltpu.roll(a, SHARE, 1), b)
-    return jnp.where(iota((R, CH), 1) < SHARE, a, b)
+def quarter_of(y, x):
+    return y % 2 * 2 + x % 2
+
+
+def pack_moments(a, b, quarter):
+    packed = jnp.zeros((8, CH), F32)
+    for k, piece in enumerate((a[:8], a[8:], b[:8], b[8:])):
+        packed = jnp.where(iota((8, CH), 1) // SHARE == k, pltpu.roll(piece, (k - quarter) % 4 * SHARE, 1), packed)
+    return packed
+
+
+def unpack_moments(packed):
+    moved = [packed] + [pltpu.roll(packed, CH - k * SHARE, 1) for k in range(1, 4)]
+    return jnp.concatenate(moved[:2], axis=0), jnp.concatenate(moved[2:], axis=0)
 
 
 def local_kernel(
@@ -145,10 +156,10 @@
     for i in range(NP):
         send(states_ref, i, slice(0, MOMENT_ROW))
     moments = (fold_states(fwd[128:]), fold_states(bwd[128:]))
-    for half in range(2):
-        packed_ref[half] = side_by_side(*moments, half)
+    for quarter in range(4):
+        packed_ref[quarter] = pack_moments(*moments, quarter)
     for i in range(NP):
-        send(packed_ref.at[i // 4 % 2], i, slice(MOMENT_ROW, SUM_ROW))
+        send(packed_ref.at[quarter_of(i // 4, i % 4)], i, slice(MOMENT_ROW, SUM_ROW))
     flipped = pick_dot_right(product, ones_where(lane + row == L - 1))
     inside = lane + row >= L - 1
     lags = []
@@ -203,31 +214,35 @@
     return lax.axis_index("y") * 4 + lax.axis_index("x")
 
 
-def to_front(state, half):
-    return pltpu.roll(state, half * SHARE, 1)
+def to_front(state, quarter):
+    return pltpu.roll(state, lax.rem(4 - quarter, 4) * SHARE, 1)
+
+
+def my_quarter():
+    return lax.rem(lax.axis_index("y"), 2) * 2 + lax.rem(lax.axis_index("x"), 2)
 
 
 def plane_kernel(msg_ref, rate_ref, out_ref, carry_ref):
     rate = rate_ref[...]
     me = plane_index()
-    half = lax.rem(lax.axis_index("y"), 2)
+    quarter = my_quarter()
     span = jnp.float32(L)
     decay = jnp.exp(-span * rate)
     zero = jnp.zeros((R, CH), F32)
-    front_decay = to_front(decay, half)
+    front_decay = to_front(decay, quarter)
     f, g, f1, h0, h1, own_f = zero, zero, zero, zero, zero, zero
     sums = jnp.zeros((G, 128), F32)
     fronts = []
     for i in range(NP):
         at = plane_slot(i)
         own_f = jnp.where(me == i, f, own_f)
-        fwd, fwd1 = msg_ref[at, :R], msg_ref[at, MOMENT_ROW:SUM_ROW]
-        bwd, bwd1 = to_front(msg_ref[at, R : 2 * R], half), pltpu.roll(fwd1, SHARE, 1)
+        fwd, bwd = msg_ref[at, :R], to_front(msg_ref[at, R : 2 * R], quarter)
+        fwd1, bwd1 = unpack_moments(msg_ref[at, MOMENT_ROW:SUM_ROW])
         fronts.append((bwd, bwd1))
         h0 = h0 + g * bwd
         h1 = h1 + g * bwd1 + f1 * bwd
         f1 = front_decay * (f1 + span * g) + fwd1
-        g = front_decay * g + to_front(fwd, half)
+        g = front_decay * g + to_front(fwd, quarter)
         f = decay * f + fwd
         sums = sums + msg_ref[at, SUM_ROW:]
     b, e, b1, own_b = zero, zero, zero, zero
@@ -239,49 +254,47 @@
         b = decay * b + msg_ref[plane_slot(i), R : 2 * R]
     carry_ref[:R] = own_f
     carry_ref[R : 2 * R] = own_b
-    sums = sums + front_sums(h0, h1, half)
-    front = iota((R, CH), 1) < SHARE
-    f1 = pltpu.roll(f1, SHARE, 1)
-    sums = jnp.concatenate([pltpu.roll(sums, SHARE, 1), jnp.zeros((R - G, CH), F32)], axis=0)
-    last = jnp.where(front, b1, sums)
+    sums = sums + front_sums(h0, h1, quarter)
+    sums = jnp.concatenate([pltpu.roll(sums, 3 * SHARE, 1), pltpu.roll(sums, 2 * SHARE, 1)], axis=0)
+    place = iota((R, CH), 1) // SHARE
+    rest = jnp.where(place == 1, pltpu.roll(f1, SHARE, 1), jnp.where(place == 2, pltpu.roll(b1, 2 * SHARE, 1), sums))
     z = lax.axis_index("z")
     for i in range(NZ):
         above = z < i
         out_ref[z_slot(i), :R] = jnp.where(above, f, b)
-        out_ref[z_slot(i), R : 2 * R] = jnp.where(front, jnp.where(above, e, g), f1)
-        out_ref[z_slot(i), 2 * R :] = last
+        out_ref[z_slot(i), R:] = jnp.where(place == 0, jnp.where(above, e, g), rest)
 
 
 def final_kernel(msg_ref, tau_ref, res_ref, rate_ref, param_ref):
     inv = 1.0 / tau_ref[...]
-    half = lax.rem(lax.axis_index("y"), 2)
+    quarter = my_quarter()
     z = lax.axis_index("z")
     span = jnp.float32(L * NP)
-    decay = jnp.exp(-span * to_front(rate_ref[...], half))
+    decay = jnp.exp(-span * to_front(rate_ref[...], quarter))
     zero = jnp.zeros((R, CH), F32)
     f, f1, h0, h1 = zero, zero, zero, zero
-    sums = jnp.zeros((G, 128), F32)
+    total = zero
     for i in range(NZ):
         at = z_slot(i)
-        carry = to_front(msg_ref[at, :R], half)
-        part = msg_ref[at, R : 2 * R]
+        carry = to_front(msg_ref[at, :R], quarter)
+        part = msg_ref[at, R:]
         fwd, bwd = jnp.where(i < z, carry, part), jnp.where(i < z, part, carry)
-        bwd1 = msg_ref[at, 2 * R :]
+        bwd1 = pltpu.roll(part, 2 * SHARE, 1)
         h0 = h0 + f * bwd
         h1 = h1 + f * bwd1 + f1 * bwd
-        f1 = decay * (f1 + span * f) + pltpu.roll(part, SHARE, 1)
+        f1 = decay * (f1 + span * f) + pltpu.roll(part, 3 * SHARE, 1)
         f = decay * f + fwd
-        sums = sums + msg_ref[at, 2 * R : 2 * R + G]
-    whole = front_sums(h0, h1, half) + pltpu.roll(sums, SHARE, 1)
+        total = total + part
+    whole = front_sums(h0, h1, quarter) + pltpu.roll(total[:G], SHARE, 1)
     scale = 1.0 / math.sqrt(L * NP * NZ * M)
     h0, h1 = whole[:, :R], whole[:, R : 2 * R]
     root = jnp.sqrt(2.0 * inv) * (scale / math.sqrt(R))
     params = jnp.concatenate(
         [h0 * root, res_ref[...] * root * (h1 * inv - 0.5 * h0), jnp.zeros((G, 128 - 2 * R), F32)], axis=1
     )
-    group = iota((G, 128), 0) - half * (G // 2)
+    group = iota((G, 128), 0) - quarter * (G // 4)
     row = jnp.where(group == 0, params, 0.0)
-    for k in range(1, G // 2):
+    for k in range(1, G // 4):
         row = row + jnp.where(group == k, pltpu.roll(params, 2 * R * k, 1), 0.0)
     row = jnp.sum(row, axis=0, keepdims=True)
     for i in range(PEERS):
@@ -293,10 +306,10 @@
     columns = jnp.concatenate([rows, jnp.zeros((128 - PEERS, 128), F32)], axis=0).T
     peer = iota((128, 4 * G), 0)
     group = iota((128, 4 * G), 1)
-    half, core, zh = 1 - peer % 2, peer // 2 % 2, 1 - peer // 4
-    first = (zh * 2 + core) * G + half * (G // 2)
+    quarter, core, zh = 3 - peer % 4, peer // 4 % 2, 1 - peer // 8
+    first = (zh * 2 + core) * G + quarter * (G // 4)
     out = jnp.zeros((2 * R, 4 * G), F32)
-    for k in range(G // 2):
+    for k in range(G // 4):
         place = ones_where((group == first + k) & (peer < PEERS)).astype(jnp.bfloat16)
         for part in halves(columns[2 * R * k : 2 * R * (k + 1)]):
             out = out + lax.dot_general(part, place, (((1,), (0,)), ((), ())), preferred_element_type=F32)
@@ -323,11 +336,13 @@
 
 def gather_groups():
     groups = []
-    index = lambda zh, z, y, core: ((zh * NZ + z) * 4 + y) * 2 + core
+    index = lambda zh, z, y, x, core: (((zh * NZ + z) * 4 + y) * 4 + x) * 2 + core
+    block = [(zh, core, y, x) for zh in (1, 0) for core in (0, 1) for y in (1, 0) for x in (1, 0)]
     for z in range(NZ):
         planes = {0: z, 1: (z + 4) % NZ}
-        for pair in (0, 2):
-            groups.append([index(zh, planes[zh], pair + half, core) for zh in (1, 0) for core in (0, 1) for half in (1, 0)])
+        for top in (0, 2):
+            for left in (0, 2):
+                groups.append([index(zh, planes[zh], top + y, left + x, core) for zh, core, y, x in block])
     return groups
 
 
@@ -345,14 +360,14 @@
     sums = jnp.zeros((G, 128), F32)
     for i in range(NZ):
         own_f = jnp.where(i < z, decay * own_f + msg_ref[z_slot(i), :R], own_f)
-        sums = sums + msg_ref[z_slot(i), 2 * R : 2 * R + G]
+        sums = sums + msg_ref[z_slot(i), R + G :]
     for i in reversed(range(NZ)):
         own_b = jnp.where(i > z, decay * own_b + msg_ref[z_slot(i), :R], own_b)
     own_f = plane_ref[:R] + jnp.exp(-(L * me) * rate) * own_f
     own_b = plane_ref[R : 2 * R] + jnp.exp(-(L * (NP - 1 - me)) * rate) * own_b
     lane = iota((128, 128), 1)
     row = iota((128, 128), 0)
-    spread = dot(sums, ones_where((row - 2 * R - SHARE == lane % M) & (row >= 2 * R + SHARE) & (row < 3 * R + SHARE)))
+    spread = dot(sums, ones_where((row - 3 * SHARE == lane % M) & (row >= 3 * SHARE) & (row < 3 * SHARE + M)))
     spread = jnp.where(iota((G, CH), 1) // M == iota((G, CH), 0), spread, 0.0)
     skip_ref[...] = jnp.sum(spread, axis=0, keepdims=True) * (1.0 / math.sqrt(L * NP * NZ))
     mixed = fwd_ref[...] + dot3(spread_states(own_f), head_ref[...], 0, 0)
@@ -395,7 +410,7 @@
             *blocks,
             pltpu.VMEM((G, R), F32),
             pltpu.VMEM((2 * R, CH), F32),
-            pltpu.VMEM((2, R, CH), F32),
+            pltpu.VMEM((4, 8, CH), F32),
             pltpu.VMEM((G, CH), F32),
             pltpu.SemaphoreType.DMA((5,)),
             pltpu.SemaphoreType.DMA((3 * NP,)),
@@ -415,7 +430,7 @@
     )
     z_states = lax.all_to_all(totals, ("zh", "z"), 0, 0, axis_index_groups=z_groups())
     params = call(final_kernel, shape(PEERS, 1, 128), 10**7, "z_scan")(z_states, timescale, residue, rate)
-    params = lax.all_to_all(params, ("zh", "z", "y", "core"), 0, 0, axis_index_groups=gather_groups())
+    params = lax.all_to_all(params, ("zh", "z", "y", "x", "core"), 0, 0, axis_index_groups=gather_groups())
     output, grad_queries, grad_keys, grad_values, grad_skip = call(
         output_kernel,
         (*(shape(CH, L, dtype=jnp.bfloat16),) * 4, shape(1, CH)),

time: 55.5 us -> 53.1 us (0.957)
  blocking collectives: 21.6 us -> 19.7 us
    all_to_all x1, blocking collectives: 21.6 us -> 19.7 us  [per_device(): lax.all_to_all(totals, ('zh', 'z'), 0, 0, axis_index_groups=z_groups())]
  transfers between devices with their start and end apart: 2 -> 2, of which waited for: 2 -> 2; matrix products, arithmetic and copies ran while one was open for 0% -> 0% of each run, Pallas kernels for 5% -> 6%
where the time goes in v5:
time: 53.1 us; the launch traced here: 52.7 us
  starting transfers between devices  20.4 us (38%)
  blocking collectives  19.7 us (37%)
  Pallas kernels  8.28 us (16%)
  waiting for transfers between devices  2.87 us (5%)
  between operations  0.77 us (1%)
  local copies, waits for them, and re-layouts  0.63 us (1%)
    all_to_all x1, blocking collectives, per_device(): lax.all_to_all(totals, ('zh', 'z'), 0, 0, axis_index_groups=z_groups())  19.7 us
    all_to_all x1, starting transfers between devices, per_device(): lax.all_to_all(params, ('zh', 'z', 'y', 'x', 'core'), 0, 0, axis_index_gr...  11.2 us
    all_to_all x1, starting transfers between devices, per_device(): lax.all_to_all(message, ('y', 'x'), 0, 0, axis_index_groups=plane_groups())  9.24 us
    pallas_call x1, Pallas kernels, per_device(): call(local_kernel, shape(NP, ROWS, 128), 10 ** 8, 'local_states', vmem=60...  2.97 us
    all_to_all x1, waiting for transfers between devices, per_device(): lax.all_to_all(message, ('y', 'x'), 0, 0, axis_index_groups=plane_groups())  2.12 us
    pallas_call x1, Pallas kernels, per_device(): call(conv_kernel, (*(shape(128, 128),) * 4, shape(R, CH)), 10 ** 8, 'loca...  1.76 us
    pallas_call x1, Pallas kernels, per_device(): call(output_kernel, (*(shape(CH, L, dtype=jnp.bfloat16),) * 4, shape(1, C...  1.16 us
    pallas_call x1, Pallas kernels, per_device(): call(final_kernel, shape(PEERS, 1, 128), 10 ** 7, 'z_scan')  1.16 us
  transfers between devices with their start and end apart: 2, of which 2 were waited for; matrix products, arithmetic and copies ran while one was open for 0% of the time, Pallas kernels for 6%

profile of v5, /device:TPU:1, one launch (start us, length us, event | category | flops | bytes accessed | tf_op | source)
XLA Modules:
  0.0 52.7 jit_solution(9541624411548796772)
XLA Ops:
  0.6 3.0 %local_states.1 = f32[16,48,128]{2,1,0:T(8,128)} custom-call(bf16[128,128]{1,0:T(8,128)(2,1)} %q_hbm.5, bf16[128,128]{1,0:T(8,128)(2,1)} %k_hbm.5, bf16[128,128]{1,0:T(8,128)(2,1)} %v_hbm.5, bf16[128,128]{1,0:T(8,128)(2,1)} %ct_hbm.5, f32[8,16]{1,0:T(8,128)} %tau_ref.3), custom_call_target="tpu_custom_call" | custom-call | flops 100000000 | bytes 500000 | tf_op jit(solution)/shard_map/local_states/pallas_call | solution.py:401
  3.6 0.0 copy-start
  3.6 0.0 copy-start.1
  3.6 0.0 copy-start.2
  3.6 0.0 copy-start.3
  3.7 0.0 copy-start.4
  3.7 0.0 copy-start.5
  3.7 9.2 %all-to-all-start = ((f32[16,48,128]{2,1,0:T(8,128)}), f32[16,48,128]{2,1,0:T(8,128)S(1)}, u32[]{:S(2)}, u32[]{:S(2)}) async-start(f32[16,48,128]{2,1,0:T(8,128)} %local_states.1), calls=%async_computation | async-start | bytes 786432 | tf_op jit(solution)/shard_map/all_to_all | solution.py:419
  12.9 0.0 copy-done
  12.9 0.0 copy-done.1
  12.9 0.0 copy-done.2
  13.0 0.0 copy-done.3
  13.0 0.0 copy-done.4
  13.0 0.0 copy-done.5
  13.0 0.6 %copy-done.6 = f32[128]{0:T(128)S(1)} copy-done((f32[128]{0:T(128)S(1)}, f32[128]{0:T(128)}, u32[]{:S(2)}) %copy-start.6) | copy-done | bytes 536
  13.6 1.8 %local_conv.1 = (f32[128,128]{1,0:T(8,128)S(1)}, f32[128,128]{1,0:T(8,128)S(1)}, f32[128,128]{1,0:T(8,128)S(1)}, f32[128,128]{1,0:T(8,128)S(1)}, f32[16,128]{1,0:T(8,128)S(1)}) custom-call(bf16[128,128]{1,0:T(8,128)(2,1)S(1)} %copy-done, bf16[128,128]{1,0:T(8,128)(2,1)S(1)} %copy-done.1, bf16[128,128]{1,0:T(8,128)(2,1)S(1)} %copy-done.2, ...), custom_call_target="tpu_custom_call" | custom-call | flops 100000000 | bytes 500000 | tf_op jit(solution)/shard_map/local_conv/pallas_call | solution.py:420
  15.3 2.1 %all-to-all-done.msg_ref = f32[16,48,128]{2,1,0:T(8,128)S(1)} async-done(((f32[16,48,128]{2,1,0:T(8,128)}), f32[16,48,128]{2,1,0:T(8,128)S(1)}, u32[]{:S(2)}, u32[]{:S(2)}) %all-to-all-start) | async-done | bytes 393248 | tf_op jit(solution)/shard_map/all_to_all | solution.py:419
  17.5 0.4 plane_scan.1
  17.9 19.7 %all_to_all.15.msg_ref = f32[8,32,128]{2,1,0:T(8,128)S(1)} all-to-all(f32[8,32,128]{2,1,0:T(8,128)S(1)} %get-tuple-element.26), channel_id=1, replica_groups={{448,0,64,128,192,256,320,384},{194,258,322,386,450,2,66,130},{449,1,65..., dimensions={0} | all-to-all | bytes 262144 | tf_op jit(solution)/shard_map/all_to_all | solution.py:431
  37.6 1.2 %z_scan.1 = f32[16,1,128]{2,1,0:T(1,128)} custom-call(f32[8,32,128]{2,1,0:T(8,128)S(1)} %all_to_all.15.msg_ref, f32[8,16]{1,0:T(8,128)S(1)} %copy-done.4, f32[8,16]{1,0:T(8,128)S(1)} %copy-done.5, f32[16,128]{1,0:T(8,128)S(1)} %get-tuple-element.25.rate_ref), custom_call_target="tpu_custom_call" | custom-call | flops 10000000 | bytes 500000 | tf_op jit(solution)/shard_map/z_scan/pallas_call | solution.py:432
  38.8 11.2 %all-to-all-start.2 = ((f32[16,1,128]{2,1,0:T(1,128)}), f32[16,1,128]{2,1,0:T(1,128)S(1)}, u32[]{:S(2)}, u32[]{:S(2)}) async-start(f32[16,1,128]{2,1,0:T(1,128)} %z_scan.1), calls=%async_computation.2 | async-start | bytes 16384 | tf_op jit(solution)/shard_map/all_to_all | solution.py:433
  49.9 1.2 %outputs.1 = (bf16[128,128]{1,0:T(8,128)(2,1)}, bf16[128,128]{1,0:T(8,128)(2,1)}, bf16[128,128]{1,0:T(8,128)(2,1)}, bf16[128,128]{1,0:T(8,128)(2,1)}, f32[1,128]{1,0:T(1,128)}) custom-call(bf16[128,128]{1,0:T(8,128)(2,1)S(1)} %copy-done, bf16[128,128]{1,0:T(8,128)(2,1)S(1)} %copy-done.1, bf16[128,128]{1,0:T(8,128)(2,1)S(1)} %copy-done.2, ...), custom_call_target="tpu_custom_call" | custom-call | flops 100000000 | bytes 500000 | tf_op jit(solution)/shard_map/outputs/pallas_call | solution.py:434
  51.1 0.8 %all-to-all-done.2.part_ref = f32[16,1,128]{2,1,0:T(1,128)S(1)} async-done(((f32[16,1,128]{2,1,0:T(1,128)}), f32[16,1,128]{2,1,0:T(1,128)S(1)}, u32[]{:S(2)}, u32[]{:S(2)}) %all-to-all-start.2) | async-done | bytes 8224 | tf_op jit(solution)/shard_map/all_to_all | solution.py:433
  51.8 0.8 %gather.1 = (f32[16,32]{1,0:T(8,128)}, f32[16,32]{1,0:T(8,128)}) custom-call(f32[16,1,128]{2,1,0:T(1,128)S(1)} %all-to-all-done.2.part_ref), custom_call_target="tpu_custom_call" | custom-call | flops 1000000 | bytes 500000 | tf_op jit(solution)/shard_map/gather/pallas_call | solution.py:442
  (1 shorter events, 0.0 us)
Async XLA Ops:
  3.6 9.3 %copy-start = (bf16[128,128]{1,0:T(8,128)(2,1)S(1)}, bf16[128,128]{1,0:T(8,128)(2,1)}, u32[]{:S(2)}) copy-start(bf16[128,128]{1,0:T(8,128)(2,1)} %q_hbm.5) | copy-start | bytes 98308
  3.6 9.3 %copy-start.1 = (bf16[128,128]{1,0:T(8,128)(2,1)S(1)}, bf16[128,128]{1,0:T(8,128)(2,1)}, u32[]{:S(2)}) copy-start(bf16[128,128]{1,0:T(8,128)(2,1)} %k_hbm.5) | copy-start | bytes 98308
  3.6 9.3 %copy-start.2 = (bf16[128,128]{1,0:T(8,128)(2,1)S(1)}, bf16[128,128]{1,0:T(8,128)(2,1)}, u32[]{:S(2)}) copy-start(bf16[128,128]{1,0:T(8,128)(2,1)} %v_hbm.5) | copy-start | bytes 98308
  3.6 9.3 %copy-start.3 = (bf16[128,128]{1,0:T(8,128)(2,1)S(1)}, bf16[128,128]{1,0:T(8,128)(2,1)}, u32[]{:S(2)}) copy-start(bf16[128,128]{1,0:T(8,128)(2,1)} %ct_hbm.5) | copy-start | bytes 98308
  3.7 9.3 %copy-start.4 = (f32[8,16]{1,0:T(8,128)S(1)}, f32[8,16]{1,0:T(8,128)}, u32[]{:S(2)}) copy-start(f32[8,16]{1,0:T(8,128)} %tau_ref.3) | copy-start | bytes 1540
  3.7 9.3 %copy-start.5 = (f32[8,16]{1,0:T(8,128)S(1)}, f32[8,16]{1,0:T(8,128)}, u32[]{:S(2)}) copy-start(f32[8,16]{1,0:T(8,128)} %res_ref.3) | copy-start | bytes 1540
  3.7 13.8 %all-to-all-start = ((f32[16,48,128]{2,1,0:T(8,128)}), f32[16,48,128]{2,1,0:T(8,128)S(1)}, u32[]{:S(2)}, u32[]{:S(2)}) async-start(f32[16,48,128]{2,1,0:T(8,128)} %local_states.1), calls=%async_computation | async-start | bytes 786432 | tf_op jit(solution)/shard_map/all_to_all | solution.py:419
  12.9 0.7 %copy-start.6 = (f32[128]{0:T(128)S(1)}, f32[128]{0:T(128)}, u32[]{:S(2)}) copy-start(f32[128]{0:T(128)} %param.10) | copy-start | bytes 1540
  38.8 13.1 %all-to-all-start.2 = ((f32[16,1,128]{2,1,0:T(1,128)}), f32[16,1,128]{2,1,0:T(1,128)S(1)}, u32[]{:S(2)}, u32[]{:S(2)}) async-start(f32[16,1,128]{2,1,0:T(1,128)} %z_scan.1), calls=%async_computation.2 | async-start | bytes 16384 | tf_op jit(solution)/shard_map/all_to_all | solution.py:433

commit v6 on v5

--- a/solution.py
+++ b/solution.py
@@ -23,7 +23,8 @@
 Z_ROWS = 2 * R
 PEERS = 16
 PLANE_FIRST = 15
-Z_FIRST = (7, 3)
+Z_ORDER = ((7, 0, 6, 1, 5, 2, 4, 3), (3, 4, 2, 5, 1, 6, 0, 7))
+Z_PARTNER = (7, 5, 4, 6, 0, 1, 2, 3)
 
 
 def dot(a, b, ca=1, cb=0):
@@ -322,8 +323,7 @@
 
 
 def z_slot(z):
-    first = jnp.where(lax.axis_index("zh") == 1, Z_FIRST[1], Z_FIRST[0])
-    return lax.rem(z + NZ - first, NZ)
+    return jnp.where(lax.axis_index("zh") == 1, Z_ORDER[1].index(z), Z_ORDER[0].index(z))
 
 
 def plane_groups():
@@ -331,7 +331,7 @@
 
 
 def z_groups():
-    return [[zh * NZ + (first + i) % NZ for i in range(NZ)] for zh, first in enumerate(Z_FIRST)]
+    return [[zh * NZ + z for z in order] for zh, order in enumerate(Z_ORDER)]
 
 
 def gather_groups():
@@ -339,7 +339,7 @@
     index = lambda zh, z, y, x, core: (((zh * NZ + z) * 4 + y) * 4 + x) * 2 + core
     block = [(zh, core, y, x) for zh in (1, 0) for core in (0, 1) for y in (1, 0) for x in (1, 0)]
     for z in range(NZ):
-        planes = {0: z, 1: (z + 4) % NZ}
+        planes = {0: z, 1: Z_PARTNER[z]}
         for top in (0, 2):
             for left in (0, 2):
                 groups.append([index(zh, planes[zh], top + y, left + x, core) for zh, core, y, x in block])

time: 53.1 us -> 51 us (0.960)
  starting transfers between devices: 20.4 us -> 17.9 us
    all_to_all x1, starting transfers between devices: 11.2 us -> 8.63 us  [per_device(): lax.all_to_all(params, ('zh', 'z', 'y', 'x', 'core'), 0, 0, axis_index_gr...]
where the time goes in v6:
time: 51 us; the launch traced here: 50.6 us
  blocking collectives  20.2 us (40%)
  starting transfers between devices  17.9 us (35%)
  Pallas kernels  8.27 us (16%)
  waiting for transfers between devices  2.85 us (6%)
  between operations  0.77 us (2%)
  local copies, waits for them, and re-layouts  0.63 us (1%)
    all_to_all x1, blocking collectives, per_device(): lax.all_to_all(totals, ('zh', 'z'), 0, 0, axis_index_groups=z_groups())  20.2 us
    all_to_all x1, starting transfers between devices, per_device(): lax.all_to_all(message, ('y', 'x'), 0, 0, axis_index_groups=plane_groups())  9.24 us
    all_to_all x1, starting transfers between devices, per_device(): lax.all_to_all(params, ('zh', 'z', 'y', 'x', 'core'), 0, 0, axis_index_gr...  8.63 us
    pallas_call x1, Pallas kernels, per_device(): call(local_kernel, shape(NP, ROWS, 128), 10 ** 8, 'local_states', vmem=60...  2.97 us
    all_to_all x1, waiting for transfers between devices, per_device(): lax.all_to_all(message, ('y', 'x'), 0, 0, axis_index_groups=plane_groups())  2.12 us
    pallas_call x1, Pallas kernels, per_device(): call(conv_kernel, (*(shape(128, 128),) * 4, shape(R, CH)), 10 ** 8, 'loca...  1.76 us
    pallas_call x1, Pallas kernels, per_device(): call(final_kernel, shape(PEERS, 1, 128), 10 ** 7, 'z_scan')  1.16 us
    pallas_call x1, Pallas kernels, per_device(): call(output_kernel, (*(shape(CH, L, dtype=jnp.bfloat16),) * 4, shape(1, C...  1.15 us
  transfers between devices with their start and end apart: 2, of which 2 were waited for; matrix products, arithmetic and copies ran while one was open for 0% of the time, Pallas kernels for 6%

profile of v6, /device:TPU:1, one launch (start us, length us, event | category | flops | bytes accessed | tf_op | source)
XLA Modules:
  0.0 50.6 jit_solution(18154114710762186893)
XLA Ops:
  0.6 3.0 %local_states.1 = f32[16,48,128]{2,1,0:T(8,128)} custom-call(bf16[128,128]{1,0:T(8,128)(2,1)} %q_hbm.5, bf16[128,128]{1,0:T(8,128)(2,1)} %k_hbm.5, bf16[128,128]{1,0:T(8,128)(2,1)} %v_hbm.5, bf16[128,128]{1,0:T(8,128)(2,1)} %ct_hbm.5, f32[8,16]{1,0:T(8,128)} %tau_ref.3), custom_call_target="tpu_custom_call" | custom-call | flops 100000000 | bytes 500000 | tf_op jit(solution)/shard_map/local_states/pallas_call | solution.py:401
  3.6 0.0 copy-start
  3.6 0.0 copy-start.1
  3.6 0.0 copy-start.2
  3.6 0.0 copy-start.3
  3.7 0.0 copy-start.4
  3.7 0.0 copy-start.5
  3.7 9.2 %all-to-all-start = ((f32[16,48,128]{2,1,0:T(8,128)}), f32[16,48,128]{2,1,0:T(8,128)S(1)}, u32[]{:S(2)}, u32[]{:S(2)}) async-start(f32[16,48,128]{2,1,0:T(8,128)} %local_states.1), calls=%async_computation | async-start | bytes 786432 | tf_op jit(solution)/shard_map/all_to_all | solution.py:419
  12.9 0.0 copy-done
  12.9 0.0 copy-done.1
  12.9 0.0 copy-done.2
  13.0 0.0 copy-done.3
  13.0 0.0 copy-done.4
  13.0 0.0 copy-done.5
  13.0 0.6 %copy-done.6 = f32[128]{0:T(128)S(1)} copy-done((f32[128]{0:T(128)S(1)}, f32[128]{0:T(128)}, u32[]{:S(2)}) %copy-start.6) | copy-done | bytes 536
  13.6 1.8 %local_conv.1 = (f32[128,128]{1,0:T(8,128)S(1)}, f32[128,128]{1,0:T(8,128)S(1)}, f32[128,128]{1,0:T(8,128)S(1)}, f32[128,128]{1,0:T(8,128)S(1)}, f32[16,128]{1,0:T(8,128)S(1)}) custom-call(bf16[128,128]{1,0:T(8,128)(2,1)S(1)} %copy-done, bf16[128,128]{1,0:T(8,128)(2,1)S(1)} %copy-done.1, bf16[128,128]{1,0:T(8,128)(2,1)S(1)} %copy-done.2, ...), custom_call_target="tpu_custom_call" | custom-call | flops 100000000 | bytes 500000 | tf_op jit(solution)/shard_map/local_conv/pallas_call | solution.py:420
  15.3 2.1 %all-to-all-done.msg_ref = f32[16,48,128]{2,1,0:T(8,128)S(1)} async-done(((f32[16,48,128]{2,1,0:T(8,128)}), f32[16,48,128]{2,1,0:T(8,128)S(1)}, u32[]{:S(2)}, u32[]{:S(2)}) %all-to-all-start) | async-done | bytes 393248 | tf_op jit(solution)/shard_map/all_to_all | solution.py:419
  17.5 0.4 plane_scan.1
  17.9 20.2 %all_to_all.15.msg_ref = f32[8,32,128]{2,1,0:T(8,128)S(1)} all-to-all(f32[8,32,128]{2,1,0:T(8,128)S(1)} %get-tuple-element.26), channel_id=1, replica_groups={{448,0,384,64,320,128,256,192},{194,258,130,322,66,386,2,450},{449,1,38..., dimensions={0} | all-to-all | bytes 262144 | tf_op jit(solution)/shard_map/all_to_all | solution.py:431
  38.1 1.2 %z_scan.1 = f32[16,1,128]{2,1,0:T(1,128)} custom-call(f32[8,32,128]{2,1,0:T(8,128)S(1)} %all_to_all.15.msg_ref, f32[8,16]{1,0:T(8,128)S(1)} %copy-done.4, f32[8,16]{1,0:T(8,128)S(1)} %copy-done.5, f32[16,128]{1,0:T(8,128)S(1)} %get-tuple-element.25.rate_ref), custom_call_target="tpu_custom_call" | custom-call | flops 10000000 | bytes 500000 | tf_op jit(solution)/shard_map/z_scan/pallas_call | solution.py:432
  39.2 8.6 %all-to-all-start.2 = ((f32[16,1,128]{2,1,0:T(1,128)}), f32[16,1,128]{2,1,0:T(1,128)S(1)}, u32[]{:S(2)}, u32[]{:S(2)}) async-start(f32[16,1,128]{2,1,0:T(1,128)} %z_scan.1), calls=%async_computation.2 | async-start | bytes 16384 | tf_op jit(solution)/shard_map/all_to_all | solution.py:433
  47.9 1.1 %outputs.1 = (bf16[128,128]{1,0:T(8,128)(2,1)}, bf16[128,128]{1,0:T(8,128)(2,1)}, bf16[128,128]{1,0:T(8,128)(2,1)}, bf16[128,128]{1,0:T(8,128)(2,1)}, f32[1,128]{1,0:T(1,128)}) custom-call(bf16[128,128]{1,0:T(8,128)(2,1)S(1)} %copy-done, bf16[128,128]{1,0:T(8,128)(2,1)S(1)} %copy-done.1, bf16[128,128]{1,0:T(8,128)(2,1)S(1)} %copy-done.2, ...), custom_call_target="tpu_custom_call" | custom-call | flops 100000000 | bytes 500000 | tf_op jit(solution)/shard_map/outputs/pallas_call | solution.py:434
  49.0 0.7 %all-to-all-done.2.part_ref = f32[16,1,128]{2,1,0:T(1,128)S(1)} async-done(((f32[16,1,128]{2,1,0:T(1,128)}), f32[16,1,128]{2,1,0:T(1,128)S(1)}, u32[]{:S(2)}, u32[]{:S(2)}) %all-to-all-start.2) | async-done | bytes 8224 | tf_op jit(solution)/shard_map/all_to_all | solution.py:433
  49.7 0.8 %gather.1 = (f32[16,32]{1,0:T(8,128)}, f32[16,32]{1,0:T(8,128)}) custom-call(f32[16,1,128]{2,1,0:T(1,128)S(1)} %all-to-all-done.2.part_ref), custom_call_target="tpu_custom_call" | custom-call | flops 1000000 | bytes 500000 | tf_op jit(solution)/shard_map/gather/pallas_call | solution.py:442
  (1 shorter events, 0.0 us)
Async XLA Ops:
  3.6 9.3 %copy-start = (bf16[128,128]{1,0:T(8,128)(2,1)S(1)}, bf16[128,128]{1,0:T(8,128)(2,1)}, u32[]{:S(2)}) copy-start(bf16[128,128]{1,0:T(8,128)(2,1)} %q_hbm.5) | copy-start | bytes 98308
  3.6 9.3 %copy-start.1 = (bf16[128,128]{1,0:T(8,128)(2,1)S(1)}, bf16[128,128]{1,0:T(8,128)(2,1)}, u32[]{:S(2)}) copy-start(bf16[128,128]{1,0:T(8,128)(2,1)} %k_hbm.5) | copy-start | bytes 98308
  3.6 9.3 %copy-start.2 = (bf16[128,128]{1,0:T(8,128)(2,1)S(1)}, bf16[128,128]{1,0:T(8,128)(2,1)}, u32[]{:S(2)}) copy-start(bf16[128,128]{1,0:T(8,128)(2,1)} %v_hbm.5) | copy-start | bytes 98308
  3.6 9.3 %copy-start.3 = (bf16[128,128]{1,0:T(8,128)(2,1)S(1)}, bf16[128,128]{1,0:T(8,128)(2,1)}, u32[]{:S(2)}) copy-start(bf16[128,128]{1,0:T(8,128)(2,1)} %ct_hbm.5) | copy-start | bytes 98308
  3.7 9.3 %copy-start.4 = (f32[8,16]{1,0:T(8,128)S(1)}, f32[8,16]{1,0:T(8,128)}, u32[]{:S(2)}) copy-start(f32[8,16]{1,0:T(8,128)} %tau_ref.3) | copy-start | bytes 1540
  3.7 9.3 %copy-start.5 = (f32[8,16]{1,0:T(8,128)S(1)}, f32[8,16]{1,0:T(8,128)}, u32[]{:S(2)}) copy-start(f32[8,16]{1,0:T(8,128)} %res_ref.3) | copy-start | bytes 1540
  3.7 13.8 %all-to-all-start = ((f32[16,48,128]{2,1,0:T(8,128)}), f32[16,48,128]{2,1,0:T(8,128)S(1)}, u32[]{:S(2)}, u32[]{:S(2)}) async-start(f32[16,48,128]{2,1,0:T(8,128)} %local_states.1), calls=%async_computation | async-start | bytes 786432 | tf_op jit(solution)/shard_map/all_to_all | solution.py:419
  12.9 0.7 %copy-start.6 = (f32[128]{0:T(128)S(1)}, f32[128]{0:T(128)}, u32[]{:S(2)}) copy-start(f32[128]{0:T(128)} %param.10) | copy-start | bytes 1540
  39.2 10.5 %all-to-all-start.2 = ((f32[16,1,128]{2,1,0:T(1,128)}), f32[16,1,128]{2,1,0:T(1,128)S(1)}, u32[]{:S(2)}, u32[]{:S(2)}) async-start(f32[16,1,128]{2,1,0:T(1,128)} %z_scan.1), calls=%async_computation.2 | async-start | bytes 16384 | tf_op jit(solution)/shard_map/all_to_all | solution.py:433

commit v7 on v6

--- a/solution.py
+++ b/solution.py
@@ -22,9 +22,9 @@
 SHARE = CH // 4
 Z_ROWS = 2 * R
 PEERS = 16
-PLANE_FIRST = 15
+PLANE_ORDER = (15, 14, 11, 13, 10, 7, 12, 9, 6, 3, 8, 5, 2, 4, 1, 0)
 Z_ORDER = ((7, 0, 6, 1, 5, 2, 4, 3), (3, 4, 2, 5, 1, 6, 0, 7))
-Z_PARTNER = (7, 5, 4, 6, 0, 1, 2, 3)
+Z_PARTNER = (6, 7, 5, 0, 1, 2, 3, 4)
 
 
 def dot(a, b, ca=1, cb=0):
@@ -125,18 +125,11 @@
     q_hbm, k_hbm, v_hbm, ct_hbm, tau_hbm, msg_hbm,
     q_ref, k_ref, v_ref, ct_ref, tau_ref, states_ref, packed_ref, sums_ref, sems, out_sems,
 ):
-    fetch(
-        (
-            (tau_hbm, tau_ref),
-            (q_hbm, q_ref),
-            (k_hbm, k_ref),
-            (v_hbm, v_ref),
-            (ct_hbm, ct_ref),
-        ),
-        sems,
-    )
-    product = q_ref[...].astype(F32) * k_ref[...].astype(F32)
-    grad_mixed = ct_ref[...].astype(F32) * v_ref[...].astype(F32)
+    pairs = ((tau_hbm, tau_ref), (q_hbm, q_ref), (k_hbm, k_ref), (v_hbm, v_ref), (ct_hbm, ct_ref))
+    fetches = [pltpu.make_async_copy(source, target, sems.at[i]) for i, (source, target) in enumerate(pairs)]
+    for copy in fetches:
+        copy.start()
+    fetches[0].wait()
     rate = by_group_mode(1.0 / tau_ref[...])
     lane = iota((128, 128), 1)
     row = iota((128, 128), 0)
@@ -144,6 +137,10 @@
     decay = jnp.exp(-step * rate)
     left = jnp.float32(L) - step
     decay_end = jnp.exp(-left * rate)
+    for copy in fetches[1:]:
+        copy.wait()
+    product = q_ref[...].astype(F32) * k_ref[...].astype(F32)
+    grad_mixed = ct_ref[...].astype(F32) * v_ref[...].astype(F32)
     fwd = dot3(jnp.concatenate([decay_end, left * decay_end], axis=0), product, 1, 1)
     bwd = dot3(jnp.concatenate([decay, step * decay], axis=0), grad_mixed, 1, 1)
     states_ref[:R] = fold_states(fwd[:128])
@@ -186,13 +183,19 @@
 
 
 def conv_kernel(
-    q_hbm, k_hbm, v_hbm, ct_hbm, skip_hbm, tau_ref, res_ref, fwd_ref, bwd_ref, head_ref, tail_ref, rate_ref, q_ref, k_ref, v_ref, ct_ref, skip_ref, sems
+    q_hbm, k_hbm, v_hbm, ct_hbm, skip_hbm, tau_ref, res_ref, fwd_ref, bwd_ref, head_ref, tail_ref, rate_ref, factor_ref, q_ref, k_ref, v_ref, ct_ref, skip_ref, sems
 ):
     fetch(((q_hbm, q_ref), (k_hbm, k_ref), (v_hbm, v_ref), (ct_hbm, ct_ref), (skip_hbm, skip_ref)), sems)
     product = q_ref[...].astype(F32) * k_ref[...].astype(F32)
     grad_mixed = ct_ref[...].astype(F32) * v_ref[...].astype(F32)
     inv = 1.0 / tau_ref[...]
     rate_ref[...] = by_mode_and_channel(inv)
+    root = jnp.sqrt(2.0 * inv) * (1.0 / math.sqrt(L * NP * NZ * M * R))
+    slope = res_ref[...] * root
+    none = jnp.zeros((G, R), F32)
+    rest = jnp.zeros((G, 128 - 2 * R), F32)
+    factor_ref[0] = jnp.concatenate([root, slope * inv, rest], axis=1)
+    factor_ref[1] = jnp.concatenate([none, -0.5 * slope, rest], axis=1)
     rate = by_group_mode(inv)
     gain = by_group_mode(res_ref[...] * jnp.sqrt(2.0 * inv) * (1.0 / math.sqrt(R)))
     lane = iota((128, 128), 1)
@@ -266,8 +269,7 @@
         out_ref[z_slot(i), R:] = jnp.where(place == 0, jnp.where(above, e, g), rest)
 
 
-def final_kernel(msg_ref, tau_ref, res_ref, rate_ref, param_ref):
-    inv = 1.0 / tau_ref[...]
+def final_kernel(msg_ref, rate_ref, factor_ref, param_ref):
     quarter = my_quarter()
     z = lax.axis_index("z")
     span = jnp.float32(L * NP)
@@ -287,12 +289,7 @@
         f = decay * f + fwd
         total = total + part
     whole = front_sums(h0, h1, quarter) + pltpu.roll(total[:G], SHARE, 1)
-    scale = 1.0 / math.sqrt(L * NP * NZ * M)
-    h0, h1 = whole[:, :R], whole[:, R : 2 * R]
-    root = jnp.sqrt(2.0 * inv) * (scale / math.sqrt(R))
-    params = jnp.concatenate(
-        [h0 * root, res_ref[...] * root * (h1 * inv - 0.5 * h0), jnp.zeros((G, 128 - 2 * R), F32)], axis=1
-    )
+    params = whole * factor_ref[0] + pltpu.roll(whole, R, 1) * factor_ref[1]
     group = iota((G, 128), 0) - quarter * (G // 4)
     row = jnp.where(group == 0, params, 0.0)
     for k in range(1, G // 4):
@@ -319,7 +316,7 @@
 
 
 def plane_slot(p):
-    return (p - PLANE_FIRST) % NP
+    return PLANE_ORDER.index(p)
 
 
 def z_slot(z):
@@ -327,7 +324,7 @@
 
 
 def plane_groups():
-    return [[(PLANE_FIRST + i) % NP for i in range(NP)]]
+    return [list(PLANE_ORDER)]
 
 
 def z_groups():
@@ -417,9 +414,9 @@
         ],
     )(*arrays, timescale)
     plane_states = lax.all_to_all(message, ("y", "x"), 0, 0, axis_index_groups=plane_groups())
-    *tables, rate = call(
+    *tables, rate, factors = call(
         conv_kernel,
-        (*(shape(128, 128),) * 4, shape(R, CH)),
+        (*(shape(128, 128),) * 4, shape(R, CH), shape(2, G, 128)),
         10**8,
         "local_conv",
         in_specs=[hbm] * 5 + [local] * 2,
@@ -429,7 +426,7 @@
         plane_states, rate
     )
     z_states = lax.all_to_all(totals, ("zh", "z"), 0, 0, axis_index_groups=z_groups())
-    params = call(final_kernel, shape(PEERS, 1, 128), 10**7, "z_scan")(z_states, timescale, residue, rate)
+    params = call(final_kernel, shape(PEERS, 1, 128), 10**7, "z_scan")(z_states, rate, factors)
     params = lax.all_to_all(params, ("zh", "z", "y", "x", "core"), 0, 0, axis_index_groups=gather_groups())
     output, grad_queries, grad_keys, grad_values, grad_skip = call(
         output_kernel,

time: 51 us -> 51.1 us (level)
  the two profiles are of different devices: /device:TPU:1 before, /device:TPU:384 now
where the time goes in v7:
time: 51.1 us; the launch traced here: 50.7 us
  starting transfers between devices  17.4 us (34%)
  waiting for transfers between devices  12.4 us (24%)
  blocking collectives  11.4 us (22%)
  Pallas kernels  8.07 us (16%)
  between operations  0.77 us (2%)
  local copies, waits for them, and re-layouts  0.63 us (1%)
    all_to_all x1, blocking collectives, per_device(): lax.all_to_all(totals, ('zh', 'z'), 0, 0, axis_index_groups=z_groups())  11.4 us
    all_to_all x1, starting transfers between devices, per_device(): lax.all_to_all(message, ('y', 'x'), 0, 0, axis_index_groups=plane_groups())  8.78 us
    all_to_all x1, starting transfers between devices, per_device(): lax.all_to_all(params, ('zh', 'z', 'y', 'x', 'core'), 0, 0, axis_index_gr...  8.61 us
    all_to_all x1, waiting for transfers between devices, per_device(): lax.all_to_all(params, ('zh', 'z', 'y', 'x', 'core'), 0, 0, axis_index_gr...  8 us
    all_to_all x1, waiting for transfers between devices, per_device(): lax.all_to_all(message, ('y', 'x'), 0, 0, axis_index_groups=plane_groups())  4.43 us
    pallas_call x1, Pallas kernels, per_device(): call(local_kernel, shape(NP, ROWS, 128), 10 ** 8, 'local_states', vmem=60...  2.91 us
    pallas_call x1, Pallas kernels, per_device(): call(conv_kernel, (*(shape(128, 128),) * 4, shape(R, CH), shape(2, G, 128...  1.76 us
    pallas_call x1, Pallas kernels, per_device(): call(output_kernel, (*(shape(CH, L, dtype=jnp.bfloat16),) * 4, shape(1, C...  1.15 us
  transfers between devices with their start and end apart: 2, of which 2 were waited for; matrix products, arithmetic and copies ran while one was open for 0% of the time, Pallas kernels for 6%

profile of v7, /device:TPU:384, one launch (start us, length us, event | category | flops | bytes accessed | tf_op | source)
XLA Modules:
  0.0 50.7 jit_solution(6786328259673498166)
XLA Ops:
  0.6 2.9 %local_states.1 = f32[16,48,128]{2,1,0:T(8,128)} custom-call(bf16[128,128]{1,0:T(8,128)(2,1)} %q_hbm.5, bf16[128,128]{1,0:T(8,128)(2,1)} %k_hbm.5, bf16[128,128]{1,0:T(8,128)(2,1)} %v_hbm.5, bf16[128,128]{1,0:T(8,128)(2,1)} %ct_hbm.5, f32[8,16]{1,0:T(8,128)} %tau_hbm.1), custom_call_target="tpu_custom_call" | custom-call | flops 100000000 | bytes 500000 | tf_op jit(solution)/shard_map/local_states/pallas_call | solution.py:398
  3.5 0.0 copy-start
  3.6 0.0 copy-start.1
  3.6 0.0 copy-start.2
  3.6 0.0 copy-start.3
  3.6 0.0 copy-start.4
  3.6 0.0 copy-start.5
  3.6 8.8 %all-to-all-start = ((f32[16,48,128]{2,1,0:T(8,128)}), f32[16,48,128]{2,1,0:T(8,128)S(1)}, u32[]{:S(2)}, u32[]{:S(2)}) async-start(f32[16,48,128]{2,1,0:T(8,128)} %local_states.1), calls=%async_computation | async-start | bytes 786432 | tf_op jit(solution)/shard_map/all_to_all | solution.py:416
  12.4 0.0 copy-done
  12.4 0.0 copy-done.1
  12.4 0.0 copy-done.2
  12.4 0.0 copy-done.3
  12.5 0.0 copy-done.4
  12.5 0.0 copy-done.5
  12.5 0.6 %copy-done.6 = f32[128]{0:T(128)S(1)} copy-done((f32[128]{0:T(128)S(1)}, f32[128]{0:T(128)}, u32[]{:S(2)}) %copy-start.6) | copy-done | bytes 536
  13.1 1.8 %local_conv.1 = (f32[128,128]{1,0:T(8,128)S(1)}, f32[128,128]{1,0:T(8,128)S(1)}, f32[128,128]{1,0:T(8,128)S(1)}, f32[128,128]{1,0:T(8,128)S(1)}, f32[16,128]{1,0:T(8,128)S(1)}, /*index=5*/f32[2,8,128]{2,1,0:T(8,128)S(1)}) custom-call(bf16[128,128]{1,0:T(8,128)(2,1)S(1)} %copy-done, bf16[128,128]{1,0:T(8,128)(2,1)S(1)} %copy-done.1, ...), custom_call_target="tpu_custom_call" | custom-call | flops 100000000 | bytes 500000 | tf_op jit(solution)/shard_map/local_conv/pallas_call | solution.py:417
  14.8 4.4 %all-to-all-done.msg_ref = f32[16,48,128]{2,1,0:T(8,128)S(1)} async-done(((f32[16,48,128]{2,1,0:T(8,128)}), f32[16,48,128]{2,1,0:T(8,128)S(1)}, u32[]{:S(2)}, u32[]{:S(2)}) %all-to-all-start) | async-done | bytes 393248 | tf_op jit(solution)/shard_map/all_to_all | solution.py:416
  19.3 0.4 plane_scan.1
  19.7 11.4 %all_to_all.15.msg_ref = f32[8,32,128]{2,1,0:T(8,128)S(1)} all-to-all(f32[8,32,128]{2,1,0:T(8,128)S(1)} %get-tuple-element.27), channel_id=1, replica_groups={{448,0,384,64,320,128,256,192},{194,258,130,322,66,386,2,450},{449,1,38..., dimensions={0} | all-to-all | bytes 262144 | tf_op jit(solution)/shard_map/all_to_all | solution.py:428
  31.1 1.0 %z_scan.1 = f32[16,1,128]{2,1,0:T(1,128)} custom-call(f32[8,32,128]{2,1,0:T(8,128)S(1)} %all_to_all.15.msg_ref, f32[16,128]{1,0:T(8,128)S(1)} %get-tuple-element.26.rate_ref, f32[2,8,128]{2,1,0:T(8,128)S(1)} %get-tuple-element.34.factor_ref), custom_call_target="tpu_custom_call" | custom-call | flops 10000000 | bytes 500000 | tf_op jit(solution)/shard_map/z_scan/pallas_call | solution.py:429
  32.1 8.6 %all-to-all-start.2 = ((f32[16,1,128]{2,1,0:T(1,128)}), f32[16,1,128]{2,1,0:T(1,128)S(1)}, u32[]{:S(2)}, u32[]{:S(2)}) async-start(f32[16,1,128]{2,1,0:T(1,128)} %z_scan.1), calls=%async_computation.2 | async-start | bytes 16384 | tf_op jit(solution)/shard_map/all_to_all | solution.py:430
  40.7 1.1 %outputs.1 = (bf16[128,128]{1,0:T(8,128)(2,1)}, bf16[128,128]{1,0:T(8,128)(2,1)}, bf16[128,128]{1,0:T(8,128)(2,1)}, bf16[128,128]{1,0:T(8,128)(2,1)}, f32[1,128]{1,0:T(1,128)}) custom-call(bf16[128,128]{1,0:T(8,128)(2,1)S(1)} %copy-done, bf16[128,128]{1,0:T(8,128)(2,1)S(1)} %copy-done.1, bf16[128,128]{1,0:T(8,128)(2,1)S(1)} %copy-done.2, ...), custom_call_target="tpu_custom_call" | custom-call | flops 100000000 | bytes 500000 | tf_op jit(solution)/shard_map/outputs/pallas_call | solution.py:431
  41.8 8.0 %all-to-all-done.2.part_ref = f32[16,1,128]{2,1,0:T(1,128)S(1)} async-done(((f32[16,1,128]{2,1,0:T(1,128)}), f32[16,1,128]{2,1,0:T(1,128)S(1)}, u32[]{:S(2)}, u32[]{:S(2)}) %all-to-all-start.2) | async-done | bytes 8224 | tf_op jit(solution)/shard_map/all_to_all | solution.py:430
  49.8 0.8 %gather.1 = (f32[16,32]{1,0:T(8,128)}, f32[16,32]{1,0:T(8,128)}) custom-call(f32[16,1,128]{2,1,0:T(1,128)S(1)} %all-to-all-done.2.part_ref), custom_call_target="tpu_custom_call" | custom-call | flops 1000000 | bytes 500000 | tf_op jit(solution)/shard_map/gather/pallas_call | solution.py:439
  (1 shorter events, 0.0 us)
Async XLA Ops:
  3.5 8.9 %copy-start = (bf16[128,128]{1,0:T(8,128)(2,1)S(1)}, bf16[128,128]{1,0:T(8,128)(2,1)}, u32[]{:S(2)}) copy-start(bf16[128,128]{1,0:T(8,128)(2,1)} %q_hbm.5) | copy-start | bytes 98308
  3.6 8.9 %copy-start.1 = (bf16[128,128]{1,0:T(8,128)(2,1)S(1)}, bf16[128,128]{1,0:T(8,128)(2,1)}, u32[]{:S(2)}) copy-start(bf16[128,128]{1,0:T(8,128)(2,1)} %k_hbm.5) | copy-start | bytes 98308
  3.6 8.9 %copy-start.2 = (bf16[128,128]{1,0:T(8,128)(2,1)S(1)}, bf16[128,128]{1,0:T(8,128)(2,1)}, u32[]{:S(2)}) copy-start(bf16[128,128]{1,0:T(8,128)(2,1)} %v_hbm.5) | copy-start | bytes 98308
  3.6 8.9 %copy-start.3 = (bf16[128,128]{1,0:T(8,128)(2,1)S(1)}, bf16[128,128]{1,0:T(8,128)(2,1)}, u32[]{:S(2)}) copy-start(bf16[128,128]{1,0:T(8,128)(2,1)} %ct_hbm.5) | copy-start | bytes 98308
  3.6 8.9 %copy-start.4 = (f32[8,16]{1,0:T(8,128)S(1)}, f32[8,16]{1,0:T(8,128)}, u32[]{:S(2)}) copy-start(f32[8,16]{1,0:T(8,128)} %tau_hbm.1) | copy-start | bytes 1540
  3.6 8.9 %copy-start.5 = (f32[8,16]{1,0:T(8,128)S(1)}, f32[8,16]{1,0:T(8,128)}, u32[]{:S(2)}) copy-start(f32[8,16]{1,0:T(8,128)} %res_ref.1) | copy-start | bytes 1540
  3.6 15.6 %all-to-all-start = ((f32[16,48,128]{2,1,0:T(8,128)}), f32[16,48,128]{2,1,0:T(8,128)S(1)}, u32[]{:S(2)}, u32[]{:S(2)}) async-start(f32[16,48,128]{2,1,0:T(8,128)} %local_states.1), calls=%async_computation | async-start | bytes 786432 | tf_op jit(solution)/shard_map/all_to_all | solution.py:416
  12.4 0.7 %copy-start.6 = (f32[128]{0:T(128)S(1)}, f32[128]{0:T(128)}, u32[]{:S(2)}) copy-start(f32[128]{0:T(128)} %param.10) | copy-start | bytes 1540
  32.1 17.8 %all-to-all-start.2 = ((f32[16,1,128]{2,1,0:T(1,128)}), f32[16,1,128]{2,1,0:T(1,128)S(1)}, u32[]{:S(2)}, u32[]{:S(2)}) async-start(f32[16,1,128]{2,1,0:T(1,128)} %z_scan.1), calls=%async_computation.2 | async-start | bytes 16384 | tf_op jit(solution)/shard_map/all_to_all | solution.py:430

commit v8 on v7

--- a/solution.py
+++ b/solution.py
@@ -25,6 +25,7 @@
 PLANE_ORDER = (15, 14, 11, 13, 10, 7, 12, 9, 6, 3, 8, 5, 2, 4, 1, 0)
 Z_ORDER = ((7, 0, 6, 1, 5, 2, 4, 3), (3, 4, 2, 5, 1, 6, 0, 7))
 Z_PARTNER = (6, 7, 5, 0, 1, 2, 3, 4)
+LOWER_FIRST = 7
 
 
 def dot(a, b, ca=1, cb=0):
@@ -304,7 +305,10 @@
     columns = jnp.concatenate([rows, jnp.zeros((128 - PEERS, 128), F32)], axis=0).T
     peer = iota((128, 4 * G), 0)
     group = iota((128, 4 * G), 1)
-    quarter, core, zh = 3 - peer % 4, peer // 4 % 2, 1 - peer // 8
+    lower = jnp.where(lax.axis_index("zh") == 1, Z_PARTNER[LOWER_FIRST], LOWER_FIRST)
+    lower_first = jnp.where(lax.axis_index("z") == lower, 1, 0)
+    quarter, core = 3 - peer % 4, peer // 4 % 2
+    zh = lower_first + (1 - 2 * lower_first) * (1 - peer // 8)
     first = (zh * 2 + core) * G + quarter * (G // 4)
     out = jnp.zeros((2 * R, 4 * G), F32)
     for k in range(G // 4):
@@ -334,12 +338,13 @@
 def gather_groups():
     groups = []
     index = lambda zh, z, y, x, core: (((zh * NZ + z) * 4 + y) * 4 + x) * 2 + core
-    block = [(zh, core, y, x) for zh in (1, 0) for core in (0, 1) for y in (1, 0) for x in (1, 0)]
+    block = [(core, y, x) for core in (0, 1) for y in (1, 0) for x in (1, 0)]
     for z in range(NZ):
         planes = {0: z, 1: Z_PARTNER[z]}
         for top in (0, 2):
             for left in (0, 2):
-                groups.append([index(zh, planes[zh], top + y, left + x, core) for zh, core, y, x in block])
+                order = (0, 1) if z == LOWER_FIRST else (1, 0)
+                groups.append([index(zh, planes[zh], top + y, left + x, core) for zh in order for core, y, x in block])
     return groups
 
 

time: 51.1 us -> 51.1 us (level)
  the two profiles are of different devices: /device:TPU:384 before, /device:TPU:224 now
where the time goes in v8:
time: 51.1 us; the launch traced here: 50.7 us
  starting transfers between devices  15.5 us (30%)
  blocking collectives  13.2 us (26%)
  waiting for transfers between devices  12.4 us (24%)
  Pallas kernels  8.07 us (16%)
  between operations  0.77 us (2%)
  local copies, waits for them, and re-layouts  0.63 us (1%)
    all_to_all x1, blocking collectives, per_device(): lax.all_to_all(totals, ('zh', 'z'), 0, 0, axis_index_groups=z_groups())  13.2 us
    all_to_all x1, starting transfers between devices, per_device(): lax.all_to_all(message, ('y', 'x'), 0, 0, axis_index_groups=plane_groups())  8.78 us
    all_to_all x1, waiting for transfers between devices, per_device(): lax.all_to_all(params, ('zh', 'z', 'y', 'x', 'core'), 0, 0, axis_index_gr...  8 us
    all_to_all x1, starting transfers between devices, per_device(): lax.all_to_all(params, ('zh', 'z', 'y', 'x', 'core'), 0, 0, axis_index_gr...  6.73 us
    all_to_all x1, waiting for transfers between devices, per_device(): lax.all_to_all(message, ('y', 'x'), 0, 0, axis_index_groups=plane_groups())  4.42 us
    pallas_call x1, Pallas kernels, per_device(): call(local_kernel, shape(NP, ROWS, 128), 10 ** 8, 'local_states', vmem=60...  2.91 us
    pallas_call x1, Pallas kernels, per_device(): call(conv_kernel, (*(shape(128, 128),) * 4, shape(R, CH), shape(2, G, 128...  1.76 us
    pallas_call x1, Pallas kernels, per_device(): call(output_kernel, (*(shape(CH, L, dtype=jnp.bfloat16),) * 4, shape(1, C...  1.15 us
  transfers between devices with their start and end apart: 2, of which 2 were waited for; matrix products, arithmetic and copies ran while one was open for 0% of the time, Pallas kernels for 6%

profile of v8, /device:TPU:224, one launch (start us, length us, event | category | flops | bytes accessed | tf_op | source)
XLA Modules:
  0.0 50.7 jit_solution(8709065709672222956)
XLA Ops:
  0.6 2.9 %local_states.1 = f32[16,48,128]{2,1,0:T(8,128)} custom-call(bf16[128,128]{1,0:T(8,128)(2,1)} %q_hbm.5, bf16[128,128]{1,0:T(8,128)(2,1)} %k_hbm.5, bf16[128,128]{1,0:T(8,128)(2,1)} %v_hbm.5, bf16[128,128]{1,0:T(8,128)(2,1)} %ct_hbm.5, f32[8,16]{1,0:T(8,128)} %tau_hbm.1), custom_call_target="tpu_custom_call" | custom-call | flops 100000000 | bytes 500000 | tf_op jit(solution)/shard_map/local_states/pallas_call | solution.py:403
  3.5 0.0 copy-start
  3.6 0.0 copy-start.1
  3.6 0.0 copy-start.2
  3.6 0.0 copy-start.3
  3.6 0.0 copy-start.4
  3.6 0.0 copy-start.5
  3.6 8.8 %all-to-all-start = ((f32[16,48,128]{2,1,0:T(8,128)}), f32[16,48,128]{2,1,0:T(8,128)S(1)}, u32[]{:S(2)}, u32[]{:S(2)}) async-start(f32[16,48,128]{2,1,0:T(8,128)} %local_states.1), calls=%async_computation | async-start | bytes 786432 | tf_op jit(solution)/shard_map/all_to_all | solution.py:421
  12.4 0.0 copy-done
  12.4 0.0 copy-done.1
  12.4 0.0 copy-done.2
  12.4 0.0 copy-done.3
  12.5 0.0 copy-done.4
  12.5 0.0 copy-done.5
  12.5 0.6 %copy-done.6 = f32[128]{0:T(128)S(1)} copy-done((f32[128]{0:T(128)S(1)}, f32[128]{0:T(128)}, u32[]{:S(2)}) %copy-start.6) | copy-done | bytes 536
  13.1 1.8 %local_conv.1 = (f32[128,128]{1,0:T(8,128)S(1)}, f32[128,128]{1,0:T(8,128)S(1)}, f32[128,128]{1,0:T(8,128)S(1)}, f32[128,128]{1,0:T(8,128)S(1)}, f32[16,128]{1,0:T(8,128)S(1)}, /*index=5*/f32[2,8,128]{2,1,0:T(8,128)S(1)}) custom-call(bf16[128,128]{1,0:T(8,128)(2,1)S(1)} %copy-done, bf16[128,128]{1,0:T(8,128)(2,1)S(1)} %copy-done.1, ...), custom_call_target="tpu_custom_call" | custom-call | flops 100000000 | bytes 500000 | tf_op jit(solution)/shard_map/local_conv/pallas_call | solution.py:422
  14.8 4.4 %all-to-all-done.msg_ref = f32[16,48,128]{2,1,0:T(8,128)S(1)} async-done(((f32[16,48,128]{2,1,0:T(8,128)}), f32[16,48,128]{2,1,0:T(8,128)S(1)}, u32[]{:S(2)}, u32[]{:S(2)}) %all-to-all-start) | async-done | bytes 393248 | tf_op jit(solution)/shard_map/all_to_all | solution.py:421
  19.2 0.4 plane_scan.1
  19.7 13.2 %all_to_all.15.msg_ref = f32[8,32,128]{2,1,0:T(8,128)S(1)} all-to-all(f32[8,32,128]{2,1,0:T(8,128)S(1)} %get-tuple-element.27), channel_id=1, replica_groups={{448,0,384,64,320,128,256,192},{194,258,130,322,66,386,2,450},{449,1,38..., dimensions={0} | all-to-all | bytes 262144 | tf_op jit(solution)/shard_map/all_to_all | solution.py:433
  32.9 1.0 %z_scan.1 = f32[16,1,128]{2,1,0:T(1,128)} custom-call(f32[8,32,128]{2,1,0:T(8,128)S(1)} %all_to_all.15.msg_ref, f32[16,128]{1,0:T(8,128)S(1)} %get-tuple-element.26.rate_ref, f32[2,8,128]{2,1,0:T(8,128)S(1)} %get-tuple-element.34.factor_ref), custom_call_target="tpu_custom_call" | custom-call | flops 10000000 | bytes 500000 | tf_op jit(solution)/shard_map/z_scan/pallas_call | solution.py:434
  33.9 6.7 %all-to-all-start.2 = ((f32[16,1,128]{2,1,0:T(1,128)}), f32[16,1,128]{2,1,0:T(1,128)S(1)}, u32[]{:S(2)}, u32[]{:S(2)}) async-start(f32[16,1,128]{2,1,0:T(1,128)} %z_scan.1), calls=%async_computation.2 | async-start | bytes 16384 | tf_op jit(solution)/shard_map/all_to_all | solution.py:435
  40.7 1.1 %outputs.1 = (bf16[128,128]{1,0:T(8,128)(2,1)}, bf16[128,128]{1,0:T(8,128)(2,1)}, bf16[128,128]{1,0:T(8,128)(2,1)}, bf16[128,128]{1,0:T(8,128)(2,1)}, f32[1,128]{1,0:T(1,128)}) custom-call(bf16[128,128]{1,0:T(8,128)(2,1)S(1)} %copy-done, bf16[128,128]{1,0:T(8,128)(2,1)S(1)} %copy-done.1, bf16[128,128]{1,0:T(8,128)(2,1)S(1)} %copy-done.2, ...), custom_call_target="tpu_custom_call" | custom-call | flops 100000000 | bytes 500000 | tf_op jit(solution)/shard_map/outputs/pallas_call | solution.py:436
  41.8 8.0 %all-to-all-done.2.part_ref = f32[16,1,128]{2,1,0:T(1,128)S(1)} async-done(((f32[16,1,128]{2,1,0:T(1,128)}), f32[16,1,128]{2,1,0:T(1,128)S(1)}, u32[]{:S(2)}, u32[]{:S(2)}) %all-to-all-start.2) | async-done | bytes 8224 | tf_op jit(solution)/shard_map/all_to_all | solution.py:435
  49.8 0.8 %gather.1 = (f32[16,32]{1,0:T(8,128)}, f32[16,32]{1,0:T(8,128)}) custom-call(f32[16,1,128]{2,1,0:T(1,128)S(1)} %all-to-all-done.2.part_ref), custom_call_target="tpu_custom_call" | custom-call | flops 1000000 | bytes 500000 | tf_op jit(solution)/shard_map/gather/pallas_call | solution.py:444
  (1 shorter events, 0.0 us)
Async XLA Ops:
  3.5 8.9 %copy-start = (bf16[128,128]{1,0:T(8,128)(2,1)S(1)}, bf16[128,128]{1,0:T(8,128)(2,1)}, u32[]{:S(2)}) copy-start(bf16[128,128]{1,0:T(8,128)(2,1)} %q_hbm.5) | copy-start | bytes 98308
  3.6 8.9 %copy-start.1 = (bf16[128,128]{1,0:T(8,128)(2,1)S(1)}, bf16[128,128]{1,0:T(8,128)(2,1)}, u32[]{:S(2)}) copy-start(bf16[128,128]{1,0:T(8,128)(2,1)} %k_hbm.5) | copy-start | bytes 98308
  3.6 8.9 %copy-start.2 = (bf16[128,128]{1,0:T(8,128)(2,1)S(1)}, bf16[128,128]{1,0:T(8,128)(2,1)}, u32[]{:S(2)}) copy-start(bf16[128,128]{1,0:T(8,128)(2,1)} %v_hbm.5) | copy-start | bytes 98308
  3.6 8.9 %copy-start.3 = (bf16[128,128]{1,0:T(8,128)(2,1)S(1)}, bf16[128,128]{1,0:T(8,128)(2,1)}, u32[]{:S(2)}) copy-start(bf16[128,128]{1,0:T(8,128)(2,1)} %ct_hbm.5) | copy-start | bytes 98308
  3.6 8.9 %copy-start.4 = (f32[8,16]{1,0:T(8,128)S(1)}, f32[8,16]{1,0:T(8,128)}, u32[]{:S(2)}) copy-start(f32[8,16]{1,0:T(8,128)} %tau_hbm.1) | copy-start | bytes 1540
  3.6 8.9 %copy-start.5 = (f32[8,16]{1,0:T(8,128)S(1)}, f32[8,16]{1,0:T(8,128)}, u32[]{:S(2)}) copy-start(f32[8,16]{1,0:T(8,128)} %res_ref.1) | copy-start | bytes 1540
  3.6 15.6 %all-to-all-start = ((f32[16,48,128]{2,1,0:T(8,128)}), f32[16,48,128]{2,1,0:T(8,128)S(1)}, u32[]{:S(2)}, u32[]{:S(2)}) async-start(f32[16,48,128]{2,1,0:T(8,128)} %local_states.1), calls=%async_computation | async-start | bytes 786432 | tf_op jit(solution)/shard_map/all_to_all | solution.py:421
  12.4 0.7 %copy-start.6 = (f32[128]{0:T(128)S(1)}, f32[128]{0:T(128)}, u32[]{:S(2)}) copy-start(f32[128]{0:T(128)} %param.10) | copy-start | bytes 1540
  33.9 15.9 %all-to-all-start.2 = ((f32[16,1,128]{2,1,0:T(1,128)}), f32[16,1,128]{2,1,0:T(1,128)S(1)}, u32[]{:S(2)}, u32[]{:S(2)}) async-start(f32[16,1,128]{2,1,0:T(1,128)} %z_scan.1), calls=%async_computation.2 | async-start | bytes 16384 | tf_op jit(solution)/shard_map/all_to_all | solution.py:435

commit v9 on v7

--- a/solution.py
+++ b/solution.py
@@ -24,7 +24,7 @@
 PEERS = 16
 PLANE_ORDER = (15, 14, 11, 13, 10, 7, 12, 9, 6, 3, 8, 5, 2, 4, 1, 0)
 Z_ORDER = ((7, 0, 6, 1, 5, 2, 4, 3), (3, 4, 2, 5, 1, 6, 0, 7))
-Z_PARTNER = (6, 7, 5, 0, 1, 2, 3, 4)
+Z_PARTNER = (6, 5, 4, 7, 0, 1, 2, 3)
 
 
 def dot(a, b, ca=1, cb=0):

time: 51.1 us -> 51.2 us (level)
  the two profiles are of different devices: /device:TPU:384 before, /device:TPU:64 now
where the time goes in v9:
time: 51.2 us; the launch traced here: 50.8 us
  starting transfers between devices  19.6 us (38%)
  blocking collectives  16.2 us (32%)
  Pallas kernels  8.07 us (16%)
  waiting for transfers between devices  5.49 us (11%)
  between operations  0.77 us (2%)
  local copies, waits for them, and re-layouts  0.63 us (1%)
    all_to_all x1, blocking collectives, per_device(): lax.all_to_all(totals, ('zh', 'z'), 0, 0, axis_index_groups=z_groups())  16.2 us
    all_to_all x1, starting transfers between devices, per_device(): lax.all_to_all(params, ('zh', 'z', 'y', 'x', 'core'), 0, 0, axis_index_gr...  10.8 us
    all_to_all x1, starting transfers between devices, per_device(): lax.all_to_all(message, ('y', 'x'), 0, 0, axis_index_groups=plane_groups())  8.79 us
    all_to_all x1, waiting for transfers between devices, per_device(): lax.all_to_all(message, ('y', 'x'), 0, 0, axis_index_groups=plane_groups())  4.42 us
    pallas_call x1, Pallas kernels, per_device(): call(local_kernel, shape(NP, ROWS, 128), 10 ** 8, 'local_states', vmem=60...  2.91 us
    pallas_call x1, Pallas kernels, per_device(): call(conv_kernel, (*(shape(128, 128),) * 4, shape(R, CH), shape(2, G, 128...  1.76 us
    pallas_call x1, Pallas kernels, per_device(): call(output_kernel, (*(shape(CH, L, dtype=jnp.bfloat16),) * 4, shape(1, C...  1.15 us
    all_to_all x1, waiting for transfers between devices, per_device(): lax.all_to_all(params, ('zh', 'z', 'y', 'x', 'core'), 0, 0, axis_index_gr...  1.08 us
  transfers between devices with their start and end apart: 2, of which 2 were waited for; matrix products, arithmetic and copies ran while one was open for 0% of the time, Pallas kernels for 6%

profile of v9, /device:TPU:64, one launch (start us, length us, event | category | flops | bytes accessed | tf_op | source)
XLA Modules:
  0.0 50.8 jit_solution(3764032641655952772)
XLA Ops:
  0.6 2.9 %local_states.1 = f32[16,48,128]{2,1,0:T(8,128)} custom-call(bf16[128,128]{1,0:T(8,128)(2,1)} %q_hbm.5, bf16[128,128]{1,0:T(8,128)(2,1)} %k_hbm.5, bf16[128,128]{1,0:T(8,128)(2,1)} %v_hbm.5, bf16[128,128]{1,0:T(8,128)(2,1)} %ct_hbm.5, f32[8,16]{1,0:T(8,128)} %tau_hbm.1), custom_call_target="tpu_custom_call" | custom-call | flops 100000000 | bytes 500000 | tf_op jit(solution)/shard_map/local_states/pallas_call | solution.py:398
  3.6 0.0 copy-start
  3.6 0.0 copy-start.1
  3.6 0.0 copy-start.2
  3.6 0.0 copy-start.3
  3.6 0.0 copy-start.4
  3.6 0.0 copy-start.5
  3.6 8.8 %all-to-all-start = ((f32[16,48,128]{2,1,0:T(8,128)}), f32[16,48,128]{2,1,0:T(8,128)S(1)}, u32[]{:S(2)}, u32[]{:S(2)}) async-start(f32[16,48,128]{2,1,0:T(8,128)} %local_states.1), calls=%async_computation | async-start | bytes 786432 | tf_op jit(solution)/shard_map/all_to_all | solution.py:416
  12.4 0.0 copy-done
  12.4 0.0 copy-done.1
  12.4 0.0 copy-done.2
  12.4 0.0 copy-done.3
  12.5 0.0 copy-done.4
  12.5 0.0 copy-done.5
  12.5 0.6 %copy-done.6 = f32[128]{0:T(128)S(1)} copy-done((f32[128]{0:T(128)S(1)}, f32[128]{0:T(128)}, u32[]{:S(2)}) %copy-start.6) | copy-done | bytes 536
  13.1 1.8 %local_conv.1 = (f32[128,128]{1,0:T(8,128)S(1)}, f32[128,128]{1,0:T(8,128)S(1)}, f32[128,128]{1,0:T(8,128)S(1)}, f32[128,128]{1,0:T(8,128)S(1)}, f32[16,128]{1,0:T(8,128)S(1)}, /*index=5*/f32[2,8,128]{2,1,0:T(8,128)S(1)}) custom-call(bf16[128,128]{1,0:T(8,128)(2,1)S(1)} %copy-done, bf16[128,128]{1,0:T(8,128)(2,1)S(1)} %copy-done.1, ...), custom_call_target="tpu_custom_call" | custom-call | flops 100000000 | bytes 500000 | tf_op jit(solution)/shard_map/local_conv/pallas_call | solution.py:417
  14.8 4.4 %all-to-all-done.msg_ref = f32[16,48,128]{2,1,0:T(8,128)S(1)} async-done(((f32[16,48,128]{2,1,0:T(8,128)}), f32[16,48,128]{2,1,0:T(8,128)S(1)}, u32[]{:S(2)}, u32[]{:S(2)}) %all-to-all-start) | async-done | bytes 393248 | tf_op jit(solution)/shard_map/all_to_all | solution.py:416
  19.2 0.4 plane_scan.1
  19.7 16.2 %all_to_all.15.msg_ref = f32[8,32,128]{2,1,0:T(8,128)S(1)} all-to-all(f32[8,32,128]{2,1,0:T(8,128)S(1)} %get-tuple-element.27), channel_id=1, replica_groups={{448,0,384,64,320,128,256,192},{194,258,130,322,66,386,2,450},{449,1,38..., dimensions={0} | all-to-all | bytes 262144 | tf_op jit(solution)/shard_map/all_to_all | solution.py:428
  35.9 1.0 %z_scan.1 = f32[16,1,128]{2,1,0:T(1,128)} custom-call(f32[8,32,128]{2,1,0:T(8,128)S(1)} %all_to_all.15.msg_ref, f32[16,128]{1,0:T(8,128)S(1)} %get-tuple-element.26.rate_ref, f32[2,8,128]{2,1,0:T(8,128)S(1)} %get-tuple-element.34.factor_ref), custom_call_target="tpu_custom_call" | custom-call | flops 10000000 | bytes 500000 | tf_op jit(solution)/shard_map/z_scan/pallas_call | solution.py:429
  36.9 10.8 %all-to-all-start.2 = ((f32[16,1,128]{2,1,0:T(1,128)}), f32[16,1,128]{2,1,0:T(1,128)S(1)}, u32[]{:S(2)}, u32[]{:S(2)}) async-start(f32[16,1,128]{2,1,0:T(1,128)} %z_scan.1), calls=%async_computation.2 | async-start | bytes 16384 | tf_op jit(solution)/shard_map/all_to_all | solution.py:430
  47.8 1.1 %outputs.1 = (bf16[128,128]{1,0:T(8,128)(2,1)}, bf16[128,128]{1,0:T(8,128)(2,1)}, bf16[128,128]{1,0:T(8,128)(2,1)}, bf16[128,128]{1,0:T(8,128)(2,1)}, f32[1,128]{1,0:T(1,128)}) custom-call(bf16[128,128]{1,0:T(8,128)(2,1)S(1)} %copy-done, bf16[128,128]{1,0:T(8,128)(2,1)S(1)} %copy-done.1, bf16[128,128]{1,0:T(8,128)(2,1)S(1)} %copy-done.2, ...), custom_call_target="tpu_custom_call" | custom-call | flops 100000000 | bytes 500000 | tf_op jit(solution)/shard_map/outputs/pallas_call | solution.py:431
  48.9 1.1 %all-to-all-done.2.part_ref = f32[16,1,128]{2,1,0:T(1,128)S(1)} async-done(((f32[16,1,128]{2,1,0:T(1,128)}), f32[16,1,128]{2,1,0:T(1,128)S(1)}, u32[]{:S(2)}, u32[]{:S(2)}) %all-to-all-start.2) | async-done | bytes 8224 | tf_op jit(solution)/shard_map/all_to_all | solution.py:430
  50.0 0.8 %gather.1 = (f32[16,32]{1,0:T(8,128)}, f32[16,32]{1,0:T(8,128)}) custom-call(f32[16,1,128]{2,1,0:T(1,128)S(1)} %all-to-all-done.2.part_ref), custom_call_target="tpu_custom_call" | custom-call | flops 1000000 | bytes 500000 | tf_op jit(solution)/shard_map/gather/pallas_call | solution.py:439
  (1 shorter events, 0.0 us)
Async XLA Ops:
  3.6 8.9 %copy-start = (bf16[128,128]{1,0:T(8,128)(2,1)S(1)}, bf16[128,128]{1,0:T(8,128)(2,1)}, u32[]{:S(2)}) copy-start(bf16[128,128]{1,0:T(8,128)(2,1)} %q_hbm.5) | copy-start | bytes 98308
  3.6 8.9 %copy-start.1 = (bf16[128,128]{1,0:T(8,128)(2,1)S(1)}, bf16[128,128]{1,0:T(8,128)(2,1)}, u32[]{:S(2)}) copy-start(bf16[128,128]{1,0:T(8,128)(2,1)} %k_hbm.5) | copy-start | bytes 98308
  3.6 8.9 %copy-start.2 = (bf16[128,128]{1,0:T(8,128)(2,1)S(1)}, bf16[128,128]{1,0:T(8,128)(2,1)}, u32[]{:S(2)}) copy-start(bf16[128,128]{1,0:T(8,128)(2,1)} %v_hbm.5) | copy-start | bytes 98308
  3.6 8.9 %copy-start.3 = (bf16[128,128]{1,0:T(8,128)(2,1)S(1)}, bf16[128,128]{1,0:T(8,128)(2,1)}, u32[]{:S(2)}) copy-start(bf16[128,128]{1,0:T(8,128)(2,1)} %ct_hbm.5) | copy-start | bytes 98308
  3.6 8.9 %copy-start.4 = (f32[8,16]{1,0:T(8,128)S(1)}, f32[8,16]{1,0:T(8,128)}, u32[]{:S(2)}) copy-start(f32[8,16]{1,0:T(8,128)} %tau_hbm.1) | copy-start | bytes 1540
  3.6 8.9 %copy-start.5 = (f32[8,16]{1,0:T(8,128)S(1)}, f32[8,16]{1,0:T(8,128)}, u32[]{:S(2)}) copy-start(f32[8,16]{1,0:T(8,128)} %res_ref.1) | copy-start | bytes 1540
  3.6 15.6 %all-to-all-start = ((f32[16,48,128]{2,1,0:T(8,128)}), f32[16,48,128]{2,1,0:T(8,128)S(1)}, u32[]{:S(2)}, u32[]{:S(2)}) async-start(f32[16,48,128]{2,1,0:T(8,128)} %local_states.1), calls=%async_computation | async-start | bytes 786432 | tf_op jit(solution)/shard_map/all_to_all | solution.py:416
  12.4 0.7 %copy-start.6 = (f32[128]{0:T(128)S(1)}, f32[128]{0:T(128)}, u32[]{:S(2)}) copy-start(f32[128]{0:T(128)} %param.10) | copy-start | bytes 1540
  36.9 13.1 %all-to-all-start.2 = ((f32[16,1,128]{2,1,0:T(1,128)}), f32[16,1,128]{2,1,0:T(1,128)S(1)}, u32[]{:S(2)}, u32[]{:S(2)}) async-start(f32[16,1,128]{2,1,0:T(1,128)} %z_scan.1), calls=%async_computation.2 | async-start | bytes 16384 | tf_op jit(solution)/shard_map/all_to_all | solution.py:430
